TPU v7x, 32 devices: a whole 2x2x4 slice. The times are simulated.
32 devices in a mesh: dp: 16 (over z, y, core), mp: 2 (over x).
Axes of the slice: x: 2, y: 2, z: 4, core: 2. Of those that a mesh axis runs over, the one named last changes fastest.
Arguments:
- tokens: bfloat16 [16384, 768], P('dp'), may hold values from -6 to 6
- lengths: int32 [32], P('dp'), may hold values from 64 to 512, as said below
- weights: float32 [768, 13, 768], P('dp', None, 'mp')
- weight_m1: float32 [768, 13, 768], P('dp', None, 'mp')
- weight_m2: float32 [768, 13, 768], P('dp', None, 'mp')
- head_vecs: float32 [6, 768], P(None, 'mp')
- head_m1: float32 [6, 768], P(None, 'mp')
- head_m2: float32 [6, 768], P(None, 'mp')
- norm_vecs: float32 [6, 768], replicated
- norm_m1: float32 [6, 768], replicated
- norm_m2: float32 [6, 768], replicated
- cotangent: bfloat16 [16384, 768], P(('dp', 'mp')), may hold values from -6 to 6
Outputs:
- out_tokens: bfloat16 [16384, 768], P(('dp', 'mp'))
- grad_tokens: float32 [16384, 768], P(('dp', 'mp'))
- new_weights: float32 [768, 13, 768], P('dp', None, 'mp')
- new_weight_m1: float32 [768, 13, 768], P('dp', None, 'mp')
- new_weight_m2: float32 [768, 13, 768], P('dp', None, 'mp')
- new_head_vecs: float32 [6, 768], P(None, 'mp')
- new_head_m1: float32 [6, 768], P(None, 'mp')
- new_head_m2: float32 [6, 768], P(None, 'mp')
- new_norm_vecs: float32 [6, 768], replicated
- new_norm_m1: float32 [6, 768], replicated
- new_norm_m2: float32 [6, 768], replicated
Inputs may be any that keep to these rules, and one draw needn't show every extreme that they name: `lengths`: some sequence has 512 tokens in use in every draw.
All inputs are finite; a program needn't handle non-finite values.
Results may differ from a plain program's by a relative error of at most 0.015.
The roundings to bfloat16 on the way count: a program that leaves them out, or rounds other values in their place, can miss the bound.
Values may be sent and summed in bfloat16 or wider, within the bound.
No kernel may reach another device: no remote copies, remote signals or barrier semaphores. Data moves between devices by JAX's collectives and lax.ppermute only.
A program may use at most 192 MiB of HBM per device.

v0:
```python
import jax
import jax.numpy as jnp
from jax import lax
from jax.sharding import PartitionSpec as P

HEAD_FEATURES = 64
STEP = 5


EPS_NORM = 1e-05
EPS_ADAM = 1e-08
BETA_ONE = 0.5
BETA_TWO = 0.5
RATE_BIG = 0.03
RATE_SMALL = 0.2
DECAY = 0.01
MASKED = -1e30


def relative_embedding(length, model_width):
    distance = (length - 1 - jnp.arange(2 * length - 1)).astype(jnp.float32)
    freq_index = jnp.arange(model_width // 2).astype(jnp.float32)
    inverse = 1.0 / 10000.0 ** (2.0 * freq_index / model_width)
    angles = distance[:, None] * inverse[None, :]
    return jnp.concatenate([jnp.sin(angles), jnp.cos(angles)], axis=1)


def shifted_scores(matrix):
    leading = matrix.shape[:-2]
    row_count = matrix.shape[-2]
    col_count = matrix.shape[-1]
    flattened = matrix.reshape(leading + (row_count * col_count,))
    flattened = lax.slice_in_dim(
        flattened,
        row_count - 1,
        row_count - 1 + row_count * (col_count - 1),
        axis=flattened.ndim - 1,
    )
    return flattened.reshape(leading + (row_count, col_count - 1))[..., :row_count]


def layer_norm(features, scale_row, shift_row):
    row_mean = jnp.mean(features, axis=-1, keepdims=True)
    centred = features - row_mean
    spread = jnp.mean(centred * centred, axis=-1, keepdims=True)
    return centred * lax.rsqrt(spread + EPS_NORM) * scale_row + shift_row


def gelu(features):
    return 0.5 * features * (1.0 + jax.scipy.special.erf(features * 0.7071067811865476))


def adam_update(param, grad_sum, moment_one, moment_two, rate):
    new_one = BETA_ONE * moment_one + (1.0 - BETA_ONE) * grad_sum
    new_two = BETA_TWO * moment_two + (1.0 - BETA_TWO) * grad_sum * grad_sum
    corrected_one = new_one / (1.0 - BETA_ONE**STEP)
    corrected_two = new_two / (1.0 - BETA_TWO**STEP)
    new_param = param - rate * (
        corrected_one / (jnp.sqrt(corrected_two) + EPS_ADAM) + DECAY * param
    )
    return (new_param, new_one, new_two)


def per_device(
    tokens,
    lengths,
    weights,
    weight_m1,
    weight_m2,
    head_vecs,
    head_m1,
    head_m2,
    norm_vecs,
    norm_m1,
    norm_m2,
    cotangent,
):
    seq_count = lengths.shape[0]
    all_rows = tokens.shape[0]
    seq_len = all_rows // seq_count
    own_rows = cotangent.shape[0]
    own_start = lax.axis_index("mp") * own_rows
    weight_rows = weights.shape[0]
    blocks = lax.all_gather(weights.astype(jnp.bfloat16), "dp", axis=0, tiled=True)
    model_width = blocks.shape[0]
    local_width = blocks.shape[2]
    head_count = local_width // HEAD_FEATURES
    table_rows = 2 * seq_len + 1
    w_query = blocks[:, 0]
    w_key = blocks[:, 1]
    w_value = blocks[:, 2]
    w_out = blocks[:, 4]
    w_in = blocks[:, 5:9].reshape(model_width, 4 * local_width)
    w_back = blocks[:, 9:13].reshape(model_width, 4 * local_width)
    sine_low = relative_embedding(seq_len, model_width).astype(jnp.bfloat16)
    relative_table = jnp.dot(sine_low, blocks[:, 3], preferred_element_type=jnp.float32).astype(
        jnp.bfloat16
    )
    relative_padded = jnp.concatenate(
        [relative_table, jnp.zeros((2, local_width), jnp.bfloat16)], axis=0
    )
    relative_heads = relative_padded.reshape(table_rows, head_count, HEAD_FEATURES)
    q_proj = jnp.dot(tokens, w_query, preferred_element_type=jnp.float32)
    query_c = (q_proj + head_vecs[0]).astype(jnp.bfloat16)
    query_position = (q_proj + head_vecs[1]).astype(jnp.bfloat16)
    key_rows = jnp.dot(tokens, w_key, preferred_element_type=jnp.float32).astype(jnp.bfloat16)
    value_rows = jnp.dot(tokens, w_value, preferred_element_type=jnp.float32).astype(jnp.bfloat16)
    per_seq = (seq_count, seq_len, head_count, HEAD_FEATURES)
    seq_tuple = (
        query_c.reshape(per_seq),
        query_position.reshape(per_seq),
        key_rows.reshape(per_seq),
        value_rows.reshape(per_seq),
        lengths,
    )

    def score_block(query_cs, query_positions, key_s, length):
        content = jnp.einsum("qhd,khd->hqk", query_cs, key_s, preferred_element_type=jnp.float32)
        position_offset = shifted_scores(
            jnp.einsum(
                "slf,ylf->lsy", query_positions, relative_heads, preferred_element_type=jnp.float32
            )
        )
        key_valid = jnp.arange(seq_len) < length
        return jnp.where(
            key_valid[None, None, :], (content + position_offset) * HEAD_FEATURES ** (-0.5), MASKED
        )

    def forward_attend(sequence_item):
        query_cs, query_positions, key_s, value_s, length = sequence_item
        scores = score_block(query_cs, query_positions, key_s, length)
        row_max = jnp.max(scores, axis=-1, keepdims=True)
        exp_scores = jnp.exp(scores - row_max)
        exp_total = jnp.sum(exp_scores, axis=-1, keepdims=True)
        probs_low = (exp_scores / exp_total).astype(jnp.bfloat16)
        mixed_seq = jnp.einsum(
            "hqk,khd->qhd", probs_low, value_s, preferred_element_type=jnp.float32
        ).astype(jnp.bfloat16)
        return (mixed_seq, row_max + jnp.log(exp_total))

    mixed_seqs, log_totals = lax.map(forward_attend, seq_tuple)
    mixed_rows = mixed_seqs.reshape(all_rows, local_width)
    attn_part = jnp.dot(mixed_rows, w_out.T, preferred_element_type=jnp.float32)
    attn_sum = lax.psum(attn_part, "mp")
    h1_all = tokens.astype(jnp.float32) + attn_sum + norm_vecs[4]
    first_all = layer_norm(h1_all, norm_vecs[0], norm_vecs[1])
    first_low = first_all.astype(jnp.bfloat16)
    hidden = jnp.dot(first_low, w_in, preferred_element_type=jnp.float32) + head_vecs[2:6].reshape(
        -1
    )
    feed_active = gelu(hidden).astype(jnp.bfloat16)
    hidden, active, ffn_part = (
        hidden,
        feed_active,
        jnp.dot(feed_active, w_back.T, preferred_element_type=jnp.float32),
    )
    ffn_sum = lax.psum(ffn_part.astype(jnp.bfloat16), "mp").astype(jnp.float32)
    h1_own = lax.dynamic_slice_in_dim(h1_all, own_start, own_rows, 0)
    first_own = lax.dynamic_slice_in_dim(first_all, own_start, own_rows, 0)
    ffn_own = lax.dynamic_slice_in_dim(ffn_sum, own_start, own_rows, 0)
    h2_own = first_own + ffn_own + norm_vecs[5]
    out_own, second_back = jax.vjp(layer_norm, h2_own, norm_vecs[2], norm_vecs[3])
    grad_h2, grad_gain2, grad_bias2 = second_back(cotangent.astype(jnp.float32))
    grad_ffn = lax.all_gather(grad_h2.astype(jnp.bfloat16), "mp", axis=0, tiled=True)
    grad_active = jnp.dot(grad_ffn, w_back, preferred_element_type=jnp.float32)
    _, gelu_back = jax.vjp(gelu, hidden)
    grad_hidden = gelu_back(grad_active)[0].astype(jnp.bfloat16)
    grad_first = (
        lax.psum_scatter(
            jnp.dot(grad_hidden, w_in.T, preferred_element_type=jnp.float32),
            "mp",
            scatter_dimension=0,
            tiled=True,
        )
        + grad_h2
    )
    _, first_back = jax.vjp(layer_norm, h1_own, norm_vecs[0], norm_vecs[1])
    grad_h1, grad_gain1, grad_bias1 = first_back(grad_first)
    grad_attn = lax.all_gather(grad_h1.astype(jnp.bfloat16), "mp", axis=0, tiled=True)
    grad_mixed = jnp.dot(grad_attn, w_out, preferred_element_type=jnp.float32).astype(jnp.bfloat16)
    _, unshift = jax.vjp(shifted_scores, jnp.zeros((head_count, seq_len, table_rows), jnp.bfloat16))

    def backward_attend(running, sequence_item):
        query_cs, query_positions, key_s, value_s, length, log_total, grad_seq = sequence_item
        scores = score_block(query_cs, query_positions, key_s, length)
        attend_probs = jnp.exp(scores - log_total)
        probs_low = attend_probs.astype(jnp.bfloat16)
        grad_probs = jnp.einsum(
            "qhd,khd->hqk", grad_seq, value_s, preferred_element_type=jnp.float32
        )
        grad_scores = attend_probs * (
            grad_probs - jnp.sum(attend_probs * grad_probs, axis=-1, keepdims=True)
        )
        grad_sum = (grad_scores * HEAD_FEATURES ** (-0.5)).astype(jnp.bfloat16)
        position_gradient = unshift(grad_sum)[0]
        grad_qc = jnp.einsum("hqk,khd->qhd", grad_sum, key_s, preferred_element_type=jnp.float32)
        grad_keys = jnp.einsum(
            "hqk,qhd->khd", grad_sum, query_cs, preferred_element_type=jnp.float32
        )
        grad_values = jnp.einsum(
            "hqk,qhd->khd", probs_low, grad_seq, preferred_element_type=jnp.float32
        )
        grad_qp = jnp.einsum(
            "zgo,ozw->gzw", position_gradient, relative_heads, preferred_element_type=jnp.float32
        )
        grad_rel = jnp.einsum(
            "vxn,xvg->nvg", position_gradient, query_positions, preferred_element_type=jnp.float32
        )
        return (running + grad_rel, (grad_qc, grad_qp, grad_keys, grad_values))

    rel_start = jnp.zeros((table_rows, head_count, HEAD_FEATURES), jnp.float32)
    grad_rel, attn_grads = lax.scan(
        backward_attend, rel_start, seq_tuple + (log_totals, grad_mixed.reshape(per_seq))
    )
    grad_qc = attn_grads[0].reshape(all_rows, local_width)
    grad_qp = attn_grads[1].reshape(all_rows, local_width)
    grad_query = (grad_qc + grad_qp).astype(jnp.bfloat16)
    grad_key_low = attn_grads[2].reshape(all_rows, local_width).astype(jnp.bfloat16)
    grad_value_low = attn_grads[3].reshape(all_rows, local_width).astype(jnp.bfloat16)
    grad_rel_flat = grad_rel[: 2 * seq_len - 1].reshape(2 * seq_len - 1, local_width)
    rel_high = grad_rel_flat.astype(jnp.bfloat16)
    rel_rest = (grad_rel_flat - rel_high.astype(jnp.float32)).astype(jnp.bfloat16)
    grad_in = jnp.dot(first_low.T, grad_hidden, preferred_element_type=jnp.float32).reshape(
        lax.axis_size("dp") * weight_rows, 4, local_width
    )
    grad_out = jnp.dot(grad_ffn.T, active, preferred_element_type=jnp.float32).reshape(
        lax.axis_size("dp") * weight_rows, 4, local_width
    )
    sine_grad = jnp.dot(sine_low.T, rel_high, preferred_element_type=jnp.float32) + jnp.dot(
        sine_low.T, rel_rest, preferred_element_type=jnp.float32
    )
    block_grads = [
        jnp.dot(tokens.T, grad_query, preferred_element_type=jnp.float32),
        jnp.dot(tokens.T, grad_key_low, preferred_element_type=jnp.float32),
        jnp.dot(tokens.T, grad_value_low, preferred_element_type=jnp.float32),
        sine_grad,
        jnp.dot(grad_attn.T, mixed_rows, preferred_element_type=jnp.float32),
    ]
    weight_grad = lax.psum_scatter(
        jnp.concatenate(
            [jnp.stack(block_grads, axis=1), jnp.concatenate([grad_in, grad_out], axis=1)], axis=1
        ),
        "dp",
        scatter_dimension=0,
        tiled=True,
    )
    query_part = jnp.dot(grad_query, w_query.T, preferred_element_type=jnp.float32)
    key_part = jnp.dot(grad_key_low, w_key.T, preferred_element_type=jnp.float32)
    value_part = jnp.dot(grad_value_low, w_value.T, preferred_element_type=jnp.float32)
    grad_tokens = (
        lax.psum_scatter(
            (query_part + key_part + value_part).astype(jnp.bfloat16),
            "mp",
            scatter_dimension=0,
            tiled=True,
        ).astype(jnp.float32)
        + grad_h1
    )
    norm_part = jnp.stack(
        [
            grad_gain1,
            grad_bias1,
            grad_gain2,
            grad_bias2,
            jnp.sum(grad_h1, axis=0),
            jnp.sum(grad_h2, axis=0),
        ]
    )
    head_local = jnp.concatenate(
        [
            jnp.sum(grad_qc, axis=0)[None],
            jnp.sum(grad_qp, axis=0)[None],
            jnp.sum(grad_hidden.astype(jnp.float32), axis=0).reshape(4, local_width),
        ],
        axis=0,
    )
    head_offset = lax.axis_index("mp") * local_width
    head_wide = lax.dynamic_update_slice(
        jnp.zeros((6, local_width * lax.axis_size("mp")), jnp.float32),
        head_local,
        (jnp.int32(0), head_offset),
    )
    norm_grad, head_total = lax.psum((norm_part, head_wide), ("dp", "mp"))
    head_grad = lax.dynamic_slice_in_dim(head_total, head_offset, local_width, 1)
    new_weights, new_weight_m1, new_weight_m2 = adam_update(
        weights, weight_grad, weight_m1, weight_m2, RATE_BIG
    )
    new_head, new_head_m1, new_head_m2 = adam_update(
        head_vecs, head_grad, head_m1, head_m2, RATE_SMALL
    )
    new_norm, new_norm_m1, new_norm_m2 = adam_update(
        norm_vecs, norm_grad, norm_m1, norm_m2, RATE_SMALL
    )
    return (
        out_own.astype(jnp.bfloat16),
        grad_tokens,
        new_weights,
        new_weight_m1,
        new_weight_m2,
        new_head,
        new_head_m1,
        new_head_m2,
        new_norm,
        new_norm_m1,
        new_norm_m2,
    )


def solution(mesh):
    return jax.shard_map(
        per_device,
        mesh=mesh,
        in_specs=(
            P("dp", None),
            P("dp"),
            P("dp", None, "mp"),
            P("dp", None, "mp"),
            P("dp", None, "mp"),
            P(None, "mp"),
            P(None, "mp"),
            P(None, "mp"),
            P(),
            P(),
            P(),
            P(("dp", "mp"), None),
        ),
        out_specs=(
            P(("dp", "mp"), None),
            P(("dp", "mp"), None),
            P("dp", None, "mp"),
            P("dp", None, "mp"),
            P("dp", None, "mp"),
            P(None, "mp"),
            P(None, "mp"),
            P(None, "mp"),
            P(),
            P(),
            P(),
        ),
        check_vma=False,
    )
```

profile of v0, /device:TPU:0, one launch (start us, length us, event | category | flops | bytes accessed | tf_op | source)
XLA Modules:
  0.0 1150.8 jit_solution(8396073258451351364)
XLA Ops:
  10.3 7.1 fusion.82
  17.3 66.5 %all-gather.4.cloned.1.call-done = bf16[768,13,384]{2,0,1:T(8,128)(2,1)} async-done(((bf16[48,13,384]{2,0,1:T(8,128)(2,1)}), bf16[768,13,384]{2,0,1:T(8,128)(2,1)}) %all-gather.4.cloned.1.call-update) | async-done | bytes 7667728 | tf_op jit(solution)/shard_map/all_gather | solution.py:84
  103.8 201.0 %while.31 = (s32[]{:T(128)}, bf16[2,512,6,64]{1,3,2,0:T(8,128)(2,1)S(1)}, f32[2,6,512,1]{2,1,3,0:T(8,128)S(1)}, bf16[2,512,6,64]{1,3,2,0:T(8,128)(2,1)}, s32[2]{...) while((s32[]{:T(128)}, ...), condition=%wide.region_3.4_spmd, body=%wide.region_0.3_spmd.sunk | while | flops 820049408 | bytes 166514576 | solution.py:141
  118.4 8.1 fusion.189
  126.5 18.7 %reshape.260 = f32[3148800]{0:T(1024)} reshape(f32[6,512,1025]{2,1,0:T(8,128)} %fusion.189) | data formatting | bytes 25190400 | tf_op jit(solution)/shard_map/while
  145.2 14.0 %reshape.261 = f32[6,524800]{1,0:T(8,128)} reshape(f32[3148800]{0:T(1024)} %reshape.260) | data formatting | bytes 25190400 | tf_op jit(solution)/shard_map/while/body/eval_jaxpr/reshape | solution.py:32
  159.2 12.8 %slice.124 = f32[6,524288]{1,0:T(8,128)} slice(f32[6,524800]{1,0:T(8,128)} %reshape.261), slice={[0:6], [511:524799]} | slice | bytes 25165824 | tf_op jit(solution)/shard_map/while/body/eval_jaxpr/slice | solution.py:33
  172.0 17.6 %copy.151 = f32[1,6,512,1024]{3,2,1,0:T(8,128)} copy(f32[1,6,512,1024]{3,1,2,0:T(8,128)} %bitcast.297) | data formatting | bytes 25165824 | tf_op jit(solution)/shard_map/while
  189.6 6.8 slice.125
  196.4 6.6 copy.152
  212.0 8.1 fusion.189
  220.1 18.7 %reshape.260 = f32[3148800]{0:T(1024)} reshape(f32[6,512,1025]{2,1,0:T(8,128)} %fusion.189) | data formatting | bytes 25190400 | tf_op jit(solution)/shard_map/while
  238.8 14.0 %reshape.261 = f32[6,524800]{1,0:T(8,128)} reshape(f32[3148800]{0:T(1024)} %reshape.260) | data formatting | bytes 25190400 | tf_op jit(solution)/shard_map/while/body/eval_jaxpr/reshape | solution.py:32
  252.8 12.8 %slice.124 = f32[6,524288]{1,0:T(8,128)} slice(f32[6,524800]{1,0:T(8,128)} %reshape.261), slice={[0:6], [511:524799]} | slice | bytes 25165824 | tf_op jit(solution)/shard_map/while/body/eval_jaxpr/slice | solution.py:33
  265.6 17.6 %copy.151 = f32[1,6,512,1024]{3,2,1,0:T(8,128)} copy(f32[1,6,512,1024]{3,1,2,0:T(8,128)} %bitcast.297) | data formatting | bytes 25165824 | tf_op jit(solution)/shard_map/while
  283.2 6.8 slice.125
  290.0 6.6 copy.152
  322.1 72.8 %all-reduce.7.cloned.1.call-done = f32[1024,768]{1,0:T(8,128)} async-done(((f32[1024,768]{1,0:T(8,128)}), f32[1024,768]{1,0:T(8,128)}) %all-reduce.7.cloned.1.call-update) | async-done | bytes 3145744 | tf_op jit(solution)/shard_map/psum | solution.py:144
  411.4 51.6 %all-reduce.9.cloned.1.call-done = bf16[1024,768]{1,0:T(8,128)(2,1)} async-done(((bf16[1024,768]{1,0:T(8,128)(2,1)}), bf16[1024,768]{1,0:T(8,128)(2,1)}) %all-reduce.9.cloned.1.call-update) | async-done | bytes 1572880 | tf_op jit(solution)/shard_map/psum | solution.py:157
  469.8 27.3 %all-gather.6.cloned.1.call-done = bf16[1024,768]{1,0:T(8,128)(2,1)} async-done(((bf16[512,768]{1,0:T(8,128)(2,1)}), bf16[1024,768]{1,0:T(8,128)(2,1)}) %all-gather.6.cloned.1.call-update) | async-done | bytes 1572880 | tf_op jit(solution)/shard_map/all_gather | solution.py:164
  497.1 8.4 convert_reduce_fusion
  514.9 40.2 %reduce-scatter.4.cloned.1.call-done = f32[512,768]{1,0:T(8,128)} async-done(((f32[1024,768]{1,0:T(8,128)}), f32[512,768]{1,0:T(8,128)}) %reduce-scatter.4.cloned.1.call-update) | async-done | bytes 1572880 | tf_op jit(solution)/shard_map/reduce_scatter | solution.py:169
  572.7 16.7 %all-gather.8.cloned.1.call-done = bf16[1024,768]{1,0:T(8,128)(2,1)} async-done(((bf16[512,768]{1,0:T(8,128)(2,1)}), bf16[1024,768]{1,0:T(8,128)(2,1)}) %all-gather.8.cloned.1.call-update) | async-done | bytes 1572880 | tf_op jit(solution)/shard_map/all_gather | solution.py:179
  593.7 345.5 %while.32 = (s32[]{:T(128)}, f32[1025,6,64]{0,2,1:T(8,128)}, f32[2,512,6,64]{1,3,2,0:T(8,128)}, f32[2,512,6,64]{1,3,2,0:T(8,128)}, bf16[2,512,6,64]{1,3,2,0:T(8,...) while((s32[]{:T(128)}, f32[1025,6,64]{0,2,1:T(8,128)}, ...), condition=%wide.region_19.20_spmd.clone, body=%wide.region_17.19_spmd.clone.sunk | while | flops 2433618688 | bytes 340322144 | solution.py:212
  595.4 8.1 fusion.213
  603.5 18.7 %reshape.262 = f32[3148800]{0:T(1024)} reshape(f32[6,512,1025]{2,1,0:T(8,128)} %fusion.213) | data formatting | bytes 25190400 | tf_op jit(solution)/shard_map/while
  622.2 14.0 %reshape.263 = f32[6,524800]{1,0:T(8,128)} reshape(f32[3148800]{0:T(1024)} %reshape.262) | data formatting | bytes 25190400 | tf_op jit(solution)/shard_map/while/body/eval_jaxpr/reshape | solution.py:32
  636.2 13.0 %slice.126 = f32[6,524288]{1,0:T(8,128)} slice(f32[6,524800]{1,0:T(8,128)} %reshape.263), slice={[0:6], [511:524799]} | slice | bytes 25165824 | tf_op jit(solution)/shard_map/while/body/eval_jaxpr/slice | solution.py:33
  649.2 17.6 %copy.153 = f32[1,6,512,1024]{3,2,1,0:T(8,128)} copy(f32[1,6,512,1024]{3,1,2,0:T(8,128)} %bitcast.298) | data formatting | bytes 25165824 | tf_op jit(solution)/shard_map/while
  666.8 6.8 slice.127
  673.6 7.0 copy.154
  691.2 6.8 multiply_convert_fusion.3
  711.6 6.5 copy.156
  723.6 15.4 %reshape.264 = bf16[3148800]{0:T(1024)(128)(2,1)} reshape(bf16[6,524800]{1,0:T(8,128)(2,1)} %pad.26) | data formatting | bytes 12595200 | tf_op jit(solution)/shard_map/while
  739.0 15.0 %reshape.265 = bf16[6,512,1025]{2,1,0:T(8,128)(2,1)} reshape(bf16[3148800]{0:T(1024)(128)(2,1)} %reshape.264) | data formatting | bytes 12595200 | tf_op jit(solution)/shard_map/while/body/eval_jaxpr/transpose(jvp())/reshape | solution.py:32
  765.7 8.1 fusion.213
  773.8 18.7 %reshape.262 = f32[3148800]{0:T(1024)} reshape(f32[6,512,1025]{2,1,0:T(8,128)} %fusion.213) | data formatting | bytes 25190400 | tf_op jit(solution)/shard_map/while
  792.5 14.0 %reshape.263 = f32[6,524800]{1,0:T(8,128)} reshape(f32[3148800]{0:T(1024)} %reshape.262) | data formatting | bytes 25190400 | tf_op jit(solution)/shard_map/while/body/eval_jaxpr/reshape | solution.py:32
  806.5 13.2 %slice.126 = f32[6,524288]{1,0:T(8,128)} slice(f32[6,524800]{1,0:T(8,128)} %reshape.263), slice={[0:6], [511:524799]} | slice | bytes 25165824 | tf_op jit(solution)/shard_map/while/body/eval_jaxpr/slice | solution.py:33
  819.7 17.6 %copy.153 = f32[1,6,512,1024]{3,2,1,0:T(8,128)} copy(f32[1,6,512,1024]{3,1,2,0:T(8,128)} %bitcast.298) | data formatting | bytes 25165824 | tf_op jit(solution)/shard_map/while
  837.3 6.8 slice.127
  844.1 6.7 copy.154
  861.3 6.8 multiply_convert_fusion.3
  881.7 6.5 copy.156
  893.8 15.4 %reshape.264 = bf16[3148800]{0:T(1024)(128)(2,1)} reshape(bf16[6,524800]{1,0:T(8,128)(2,1)} %pad.26) | data formatting | bytes 12595200 | tf_op jit(solution)/shard_map/while
  909.2 15.0 %reshape.265 = bf16[6,512,1025]{2,1,0:T(8,128)(2,1)} reshape(bf16[3148800]{0:T(1024)(128)(2,1)} %reshape.264) | data formatting | bytes 12595200 | tf_op jit(solution)/shard_map/while/body/eval_jaxpr/transpose(jvp())/reshape | solution.py:32
  991.4 40.9 %all-reduce.3 = (f32[6,768]{1,0:T(8,128)}, f32[6,768]{1,0:T(8,128)}) all-reduce(f32[6,768]{1,0:T(8,128)S(1)} %maximum_dynamic-update-slice_fusion, f32[6,768]{1,0:T(8,128)S(1)} %stack.35), channel_id=1, replica_groups=mesh['dp'=16,'mp'=2] {'dp','mp'}, use_global_device_ids=true, to_apply=%region_25.26 | all-reduce | flops 9216 | bytes 73728 | tf_op jit(solution)/shard_map/psum | solution.py:283
  1037.6 102.6 %reduce-scatter.8.cloned.1.call-done = f32[48,13,384]{2,0,1:T(8,128)} async-done(((f32[768,13,384]{2,0,1:T(8,128)}), f32[48,13,384]{2,0,1:T(8,128)}) %reduce-scatter.8.cloned.1.call-update) | async-done | bytes 958480 | tf_op jit(solution)/shard_map/reduce_scatter | solution.py:239
  (285 shorter events, 255.2 us)
Async XLA Ops:
  7.2 76.7 %copy-start.27 = (bf16[1024,768]{1,0:T(8,128)(2,1)S(1)}, bf16[1024,768]{1,0:T(8,128)(2,1)}, u32[]{:S(2)}) copy-start(bf16[1024,768]{1,0:T(8,128)(2,1)} %param.16) | copy-start | bytes 4718596
  7.2 76.7 %all-gather.4.cloned.1.call-start = ((), (), s32[]{:S(2)}) async-start(), calls=%async_computation.3 | async-start | bytes 8146944 | tf_op jit(solution)/shard_map/all_gather | solution.py:84
  9.4 385.5 %all-reduce.7.cloned.1.call-start = ((), (), s32[]{:S(2)}) async-start(), calls=%async_computation.4 | async-start | bytes 6291456 | tf_op jit(solution)/shard_map/psum | solution.py:144
  100.6 3.1 copy-start.33
  100.6 3.1 copy-start.48
  306.6 3.9 copy-start.36
  306.6 3.9 copy-start.35
  310.5 152.5 %all-reduce.9.cloned.1.call-start = ((), (), s32[]{:S(2)}) async-start(), calls=%async_computation.5 | async-start | bytes 3145728 | tf_op jit(solution)/shard_map/psum | solution.py:157
  398.3 2.6 copy-start.24
  399.4 6.6 copy-start.9
  400.8 6.8 copy-start.23
  411.3 53.9 %copy-start.17 = (bf16[512,768]{1,0:T(8,128)(2,1)S(1)}, bf16[512,768]{1,0:T(8,128)(2,1)}, u32[]{:S(2)}) copy-start(bf16[512,768]{1,0:T(8,128)(2,1)} %param.27) | copy-start | bytes 2359300
  411.3 85.8 %all-gather.6.cloned.1.call-start = ((), (), s32[]{:S(2)}) async-start(), calls=%async_computation.6 | async-start | bytes 2359296 | tf_op jit(solution)/shard_map/all_gather | solution.py:164
  469.7 85.3 %reduce-scatter.4.cloned.1.call-start = ((), (), s32[]{:S(2)}) async-start(), calls=%async_computation.7 | async-start | bytes 4718592 | tf_op jit(solution)/shard_map/reduce_scatter | solution.py:169
  497.1 10.1 copy-start.25
  511.5 77.8 %all-gather.8.cloned.1.call-start = ((), (), s32[]{:S(2)}) async-start(), calls=%async_computation.8 | async-start | bytes 2359296 | tf_op jit(solution)/shard_map/all_gather | solution.py:179
  555.0 3.5 copy-start.8
  558.5 3.6 copy-start.26
  559.2 9.2 copy-start.38
  562.0 473.1 %reduce-scatter.6.cloned.1.call-start = ((), (), s32[]{:S(2)}) async-start(), calls=%async_computation.9 | async-start | bytes 2359296 | tf_op jit(solution)/shard_map/reduce_scatter | solution.py:251
  562.1 6.3 copy-start.10
  562.1 6.3 copy-start.20
  593.9 9.6 copy-start.2
  685.7 2.7 copy-start.1
  739.0 15.0 %copy-start.3 = (bf16[1025,6,64]{0,2,1:T(8,128)(2,1)S(1)}, bf16[1025,6,64]{0,2,1:T(8,128)(2,1)}, u32[]{:S(2)}) copy-start(bf16[1025,6,64]{0,2,1:T(8,128)(2,1)} %copy-done.2) | copy-start | bytes 2361604 | tf_op jit(solution)/shard_map/while
  739.0 21.3 %copy-start.4 = (f32[1025,6,64]{0,2,1:T(8,128)S(1)}, f32[1025,6,64]{0,2,1:T(8,128)}, u32[]{:S(2)}) copy-start(f32[1025,6,64]{0,2,1:T(8,128)} %get-tuple-element.550) | copy-start | bytes 4723204 | tf_op jit(solution)/shard_map/while
  754.1 6.3 copy-start
  764.2 9.6 copy-start.2
  855.8 2.7 copy-start.1
  909.2 15.1 %copy-start.3 = (bf16[1025,6,64]{0,2,1:T(8,128)(2,1)S(1)}, bf16[1025,6,64]{0,2,1:T(8,128)(2,1)}, u32[]{:S(2)}) copy-start(bf16[1025,6,64]{0,2,1:T(8,128)(2,1)} %copy-done.2) | copy-start | bytes 2361604 | tf_op jit(solution)/shard_map/while
  909.2 21.4 %copy-start.4 = (f32[1025,6,64]{0,2,1:T(8,128)S(1)}, f32[1025,6,64]{0,2,1:T(8,128)}, u32[]{:S(2)}) copy-start(f32[1025,6,64]{0,2,1:T(8,128)} %get-tuple-element.550) | copy-start | bytes 4723204 | tf_op jit(solution)/shard_map/while
  924.2 6.3 copy-start
  939.2 2.3 copy-start.34
  939.2 3.2 copy-start.29
  941.5 8.5 copy-start.16
  950.0 3.7 copy-start.28
  953.4 186.7 %reduce-scatter.8.cloned.1.call-start = ((), (), s32[]{:S(2)}) async-start(), calls=%async_computation.10 | async-start | bytes 16293888 | tf_op jit(solution)/shard_map/reduce_scatter | solution.py:239
  963.0 6.3 copy-start.6
  969.3 2.5 copy-start.14
  973.5 5.2 slice-start.2
  974.6 4.1 slice-start.3
  978.7 3.9 slice-start
  978.7 4.0 slice-start.1
  985.4 46.9 %copy-start.37 = (f32[6,384]{1,0:T(8,128)S(1)}, f32[6,384]{1,0:T(8,128)}, u32[]{:S(2)}) copy-start(f32[6,384]{1,0:T(8,128)} %param.21) | copy-start | bytes 27652
  985.4 49.7 %copy-start.12 = (f32[512,768]{1,0:T(8,128)S(1)}, f32[512,768]{1,0:T(8,128)}, u32[]{:S(2)}) copy-start(f32[512,768]{1,0:T(8,128)} %copy-done.11) | copy-start | bytes 4718596
  985.4 49.7 %copy-start.39 = (f32[512]{0:T(512)S(1)}, f32[512]{0:T(512)}, u32[]{:S(2)}) copy-start(f32[512]{0:T(512)} %copy-done.38) | copy-start | bytes 6148
  985.4 154.7 %copy-start.15 = (f32[48,13,384]{2,0,1:T(8,128)S(1)}, f32[48,13,384]{2,0,1:T(8,128)}, u32[]{:S(2)}) copy-start(f32[48,13,384]{2,0,1:T(8,128)} %param.18) | copy-start | bytes 2875396
  985.4 154.7 %copy-start.30 = (f32[48,13,384]{2,0,1:T(8,128)S(1)}, f32[48,13,384]{2,0,1:T(8,128)}, u32[]{:S(2)}) copy-start(f32[48,13,384]{2,0,1:T(8,128)} %param.19) | copy-start | bytes 2875396
  (19 other events, 28.4 us)
Sparse Core Ops, SparseCore 0:
  10.9 72.8 all-gather.3
  310.6 84.2 all-reduce.6
  411.4 51.4 all-reduce.8
  469.9 27.2 all-gather.5
  511.7 43.3 reduce-scatter.3
  562.1 27.2 all-gather.7
  953.5 26.0 reduce-scatter.5
  985.5 154.5 reduce-scatter.7
where the time goes:
time: 1160 us; the launch traced here: 1150 us
  local copies, waits for them, and re-layouts  479 us (41%)
  waiting for transfers between devices  378 us (33%)
  matrix products  173 us (15%)
  other arithmetic  45.5 us (4%)
  blocking collectives  40.9 us (4%)
  loops' own time  19.6 us (2%)
  between operations  15.1 us (1%)
    while x44, local copies, waits for them, and re-layouts  240 us
    reduce_scatter x1, waiting for transfers between devices, per_device(): lax.psum_scatter(jnp.concatenate([jnp.stack(block_grads, axis=1), jnp.con...  103 us
    reshape x6, local copies, waits for them, and re-layouts, shifted_scores(): flattened = matrix.reshape(leading + (row_count * col_count,))  86 us
    psum x1, waiting for transfers between devices, per_device(): attn_sum = lax.psum(attn_part, 'mp')  72.8 us
    all_gather x1, waiting for transfers between devices, per_device(): lax.all_gather(weights.astype(jnp.bfloat16), 'dp', axis=0, tiled=True)  66.5 us
    slice x4, local copies, waits for them, and re-layouts, shifted_scores(): lax.slice_in_dim(flattened, row_count - 1, row_count - 1 + row_count * (c...  51.8 us
    psum x1, waiting for transfers between devices, per_device(): ffn_sum = lax.psum(ffn_part.astype(jnp.bfloat16), 'mp').astype(jnp.float32)  51.6 us
    psum x1, blocking collectives, per_device(): norm_grad, head_total = lax.psum((norm_part, head_wide), ('dp', 'mp'))  40.9 us
  transfers between devices with their start and end apart: 8, of which 7 were waited for; matrix products, arithmetic and copies ran while one was open for 6% of the time, Pallas kernels for 0%

commit v1 on v0

v1 whole, which is shorter than its diff:
```python
import functools

import jax
import jax.numpy as jnp
from jax import lax
from jax.experimental import pallas as pl
from jax.experimental.pallas import tpu as pltpu
from jax.sharding import PartitionSpec as P

HEAD_FEATURES = 64
STEP = 5
EPS_NORM = 1e-05
EPS_ADAM = 1e-08
BETA_ONE = 0.5
BETA_TWO = 0.5
RATE_BIG = 0.03
RATE_SMALL = 0.2
DECAY = 0.01
MASKED = -1e30
SCALE = HEAD_FEATURES ** (-0.5)
ROW_BLOCK = 256
BF = jnp.bfloat16
F32 = jnp.float32
VMEM_LIMIT = 56 * 1024 * 1024

NN = (((1,), (0,)), ((), ()))
NT = (((1,), (1,)), ((), ()))
TN = (((0,), (0,)), ((), ()))


def mm(a, b, dims=NN):
    return lax.dot_general(a, b, dims, preferred_element_type=F32)


def whole(shape):
    return pl.BlockSpec(shape, lambda *_: (0,) * len(shape))


def params():
    return pltpu.CompilerParams(vmem_limit_bytes=VMEM_LIMIT)


def relative_embedding(length, model_width):
    distance = (length - 1 - jnp.arange(2 * length)).astype(F32)
    freq_index = jnp.arange(model_width // 2).astype(F32)
    inverse = 1.0 / 10000.0 ** (2.0 * freq_index / model_width)
    angles = distance[:, None] * inverse[None, :]
    return jnp.concatenate([jnp.sin(angles), jnp.cos(angles)], axis=1)


def adam_update(param, grad_sum, moment_one, moment_two, rate):
    new_one = BETA_ONE * moment_one + (1.0 - BETA_ONE) * grad_sum
    new_two = BETA_TWO * moment_two + (1.0 - BETA_TWO) * grad_sum * grad_sum
    corrected_one = new_one / (1.0 - BETA_ONE**STEP)
    corrected_two = new_two / (1.0 - BETA_TWO**STEP)
    new_param = param - rate * (
        corrected_one / (jnp.sqrt(corrected_two) + EPS_ADAM) + DECAY * param
    )
    return (new_param, new_one, new_two)


def full_matrix(w_ref):
    return jnp.concatenate([w_ref[0], w_ref[1]], axis=1)


def store_matrix(out_ref, value):
    half = value.shape[1] // 2
    out_ref[0] = value[:, :half].astype(BF)
    out_ref[1] = value[:, half:].astype(BF)


def project_kernel(x_ref, w_ref, vec_ref, sine_ref, qc_ref, qp_ref, k_ref, v_ref, rel_ref):
    step = pl.program_id(0)

    @pl.when(step == 0)
    def _():
        q = mm(x_ref[...], full_matrix(w_ref))
        qc_ref[...] = (q + vec_ref[0:1]).astype(BF) * BF(SCALE)
        qp_ref[...] = (q + vec_ref[1:2]).astype(BF) * BF(SCALE)

    @pl.when(step == 1)
    def _():
        k_ref[...] = mm(x_ref[...], full_matrix(w_ref)).astype(BF)

    @pl.when(step == 2)
    def _():
        v_ref[...] = mm(x_ref[...], full_matrix(w_ref)).astype(BF)

    @pl.when(step == 3)
    def _():
        rel_ref[...] = mm(sine_ref[...], full_matrix(w_ref)).astype(BF)


def project(x, w, vecs, sine):
    length, width = x.shape
    rows = sine.shape[0]
    shapes = [(length, width)] * 4 + [(rows, width)]
    return pl.pallas_call(
        project_kernel,
        grid=(4,),
        in_specs=[
            whole(x.shape),
            pl.BlockSpec((None,) + w.shape[1:], lambda b: (b, 0, 0, 0)),
            whole(vecs.shape),
            whole(sine.shape),
        ],
        out_specs=[whole(s) for s in shapes],
        out_shape=[jax.ShapeDtypeStruct(s, BF) for s in shapes],
        compiler_params=params(),
        name="project",
    )(x, w, vecs, sine)


def lane_mask(which, shape):
    lanes = lax.broadcasted_iota(jnp.int32, shape, 1)
    return (lanes >= HEAD_FEATURES) if which else (lanes < HEAD_FEATURES)


def attend_kernel(len_ref, qc_ref, qp_ref, k_ref, v_ref, rel_ref, probs_ref, mixed_ref):
    length = qc_ref.shape[0]
    block = ROW_BLOCK
    pair = qc_ref.shape[1]
    valid = lax.broadcasted_iota(jnp.int32, (1, length), 1) < len_ref[0]
    k = k_ref[...]
    v = v_ref[...]
    zero = jnp.zeros((), BF)
    for top in range(0, length, block):
        rows = pl.ds(top, block)
        first = length - block - top
        span = length + block
        rel = rel_ref[first : first + span, :]
        total = None
        for head in range(2):
            mask = lane_mask(head, (block, pair))
            content = mm(jnp.where(mask, qc_ref[rows, :], zero), k, NT)
            place = mm(jnp.where(mask, qp_ref[rows, :], zero), rel, NT)
            place = pltpu.roll(place, span - (block - 1), 1, stride=1, stride_axis=0)
            scores = jnp.where(valid, content + place[:, :length], MASKED)
            top_score = jnp.max(scores, axis=1, keepdims=True)
            grown = jnp.exp(scores - top_score)
            probs = grown * (1.0 / jnp.sum(grown, axis=1, keepdims=True))
            probs_low = probs.astype(BF)
            probs_ref[head, rows, :] = probs_low
            part = jnp.where(mask, mm(probs_low, v), 0.0)
            total = part if total is None else total + part
        mixed_ref[rows, :] = total.astype(BF)


def attend(length_used, qc, qp, k, v, rel):
    length, width = qc.shape
    pair = 2 * HEAD_FEATURES
    heads = width // HEAD_FEATURES
    column = pl.BlockSpec((length, pair), lambda p: (0, p))
    return pl.pallas_call(
        attend_kernel,
        grid=(heads // 2,),
        in_specs=[pl.BlockSpec(memory_space=pltpu.SMEM)]
        + [column] * 4
        + [pl.BlockSpec((rel.shape[0], pair), lambda p: (0, p))],
        out_specs=[pl.BlockSpec((2, length, length), lambda p: (p, 0, 0)), column],
        out_shape=[
            jax.ShapeDtypeStruct((heads, length, length), BF),
            jax.ShapeDtypeStruct((length, width), BF),
        ],
        compiler_params=params(),
        name="attend",
    )(length_used, qc, qp, k, v, rel)


def norm_parts(rows):
    mean = jnp.mean(rows, axis=1, keepdims=True)
    centred = rows - mean
    spread = jnp.mean(centred * centred, axis=1, keepdims=True)
    inverse = lax.rsqrt(spread + EPS_NORM)
    return centred * inverse, inverse


def norm_back(unit, inverse, scaled):
    return (
        scaled
        - jnp.mean(scaled, axis=1, keepdims=True)
        - unit * jnp.mean(scaled * unit, axis=1, keepdims=True)
    ) * inverse


def feed_kernel(
    mixed_ref, wo_ref, x_ref, nv_ref, hb_ref, win_ref, wback_ref, cot_ref,
    unit_ref, inv_ref, low_ref, act_ref, slope_ref, out_ref, gh2_ref, gffn_ref, sums_ref,
    first_ref, acc_ref,
):
    step = pl.program_id(0)
    last = pl.num_programs(0) - 1

    @pl.when(step == 0)
    def _():
        attn = mm(mixed_ref[...], full_matrix(wo_ref), NT)
        h1 = x_ref[...].astype(F32) + attn + nv_ref[4:5]
        unit, inverse = norm_parts(h1)
        unit_ref[...] = unit
        inv_ref[...] = jnp.broadcast_to(inverse, inv_ref.shape)
        first = unit * nv_ref[0:1] + nv_ref[1:2]
        first_ref[...] = first
        low_ref[...] = first.astype(BF)

    hidden = mm(low_ref[...], full_matrix(win_ref)) + hb_ref[0]
    bell = 0.5 * (1.0 + lax.erf(hidden * 0.7071067811865476))
    active = (hidden * bell).astype(BF)
    act_ref[...] = active
    slope_ref[...] = (
        bell + hidden * (jnp.exp(hidden * hidden * -0.5) * 0.3989422804014327)
    ).astype(BF)
    part = mm(active, full_matrix(wback_ref), NT)

    @pl.when(step == 0)
    def _():
        acc_ref[...] = part

    @pl.when(step > 0)
    def _():
        acc_ref[...] += part

    @pl.when(step == last)
    def _():
        h2 = first_ref[...] + acc_ref[...] + nv_ref[5:6]
        unit, inverse = norm_parts(h2)
        out_ref[...] = (unit * nv_ref[2:3] + nv_ref[3:4]).astype(BF)
        cot = cot_ref[...].astype(F32)
        gh2 = norm_back(unit, inverse, cot * nv_ref[2:3])
        gh2_ref[...] = gh2
        gffn_ref[...] = gh2.astype(BF)
        sums_ref[0:1] = jnp.sum(cot * unit, axis=0, keepdims=True)
        sums_ref[1:2] = jnp.sum(cot, axis=0, keepdims=True)
        sums_ref[2:3] = jnp.sum(gh2, axis=0, keepdims=True)
        sums_ref[3:8] = jnp.zeros((5, sums_ref.shape[1]), F32)


def feed(mixed, wo, x, nv, hb, win, wback, cot):
    length, width = x.shape
    blocks = win.shape[0]
    matrix = pl.BlockSpec((None,) + win.shape[1:], lambda b: (b, 0, 0, 0))
    one = whole((length, width))
    column = pl.BlockSpec((None, length, width), lambda b: (b, 0, 0))
    token = lambda d: jax.ShapeDtypeStruct((length, width), d)
    hidden = jax.ShapeDtypeStruct((blocks, length, width), BF)
    return pl.pallas_call(
        feed_kernel,
        grid=(blocks,),
        in_specs=[
            one,
            pl.BlockSpec((None,) + wo.shape[1:], lambda b: (0, 0, 0, 0)),
            one,
            whole(nv.shape),
            pl.BlockSpec((1, 1, width), lambda b: (b, 0, 0)),
            matrix,
            matrix,
            one,
        ],
        out_specs=[
            one, whole((length, 128)), one, column, column, one, one, one, whole((8, width)),
        ],
        out_shape=[
            token(F32), jax.ShapeDtypeStruct((length, 128), F32), token(BF), hidden, hidden,
            token(BF), token(F32), token(BF), jax.ShapeDtypeStruct((8, width), F32),
        ],
        scratch_shapes=[pltpu.VMEM((length, width), F32), pltpu.VMEM((length, width), F32)],
        compiler_params=params(),
        name="feed",
    )(mixed, wo, x, nv, hb, win, wback, cot)


def back_grad_kernel(gffn_ref, act_ref, out_ref, turned_ref):
    @pl.when(pl.program_id(0) == 0)
    def _():
        turned_ref[...] = gffn_ref[...].T

    store_matrix(out_ref, mm(turned_ref[...], act_ref[...]))


def back_grad(gffn, active):
    length, width = gffn.shape
    blocks = active.shape[0]
    shape = (blocks, 2, width, width // 2)
    return pl.pallas_call(
        back_grad_kernel,
        grid=(blocks,),
        in_specs=[
            whole(gffn.shape),
            pl.BlockSpec((None, length, width), lambda b: (b, 0, 0)),
        ],
        out_specs=pl.BlockSpec((None,) + shape[1:], lambda b: (b, 0, 0, 0)),
        out_shape=jax.ShapeDtypeStruct(shape, BF),
        scratch_shapes=[pltpu.VMEM((width, length), BF)],
        compiler_params=params(),
        name="back_grad",
    )(gffn, active)


def feed_back_kernel(
    gffn_ref, slope_ref, low_ref, wback_ref, win_ref, gh2_ref, unit_ref, inv_ref, nv_ref,
    wo_ref, mixed_ref,
    gwin_ref, hsum_ref, gh1_ref, gwo_ref, gmixed_ref, sums_ref,
    turned_ref, acc_ref,
):
    step = pl.program_id(0)
    last = pl.num_programs(0) - 1

    @pl.when(step == 0)
    def _():
        turned_ref[...] = low_ref[...].T
        acc_ref[...] = gh2_ref[...]

    gact = mm(gffn_ref[...], full_matrix(wback_ref))
    ghid = (gact * slope_ref[...].astype(F32)).astype(BF)
    hsum_ref[0] = jnp.sum(ghid.astype(F32), axis=0, keepdims=True)
    store_matrix(gwin_ref, mm(turned_ref[...], ghid))
    acc_ref[...] += mm(ghid, full_matrix(win_ref), NT)

    @pl.when(step == last)
    def _():
        gfirst = acc_ref[...]
        unit = unit_ref[...]
        gh1 = norm_back(unit, inv_ref[:, 0:1], gfirst * nv_ref[0:1])
        gh1_ref[...] = gh1
        gattn = gh1.astype(BF)
        store_matrix(gwo_ref, mm(gattn.T, mixed_ref[...]))
        gmixed_ref[...] = mm(gattn, full_matrix(wo_ref)).astype(BF)
        sums_ref[0:1] = jnp.sum(gfirst * unit, axis=0, keepdims=True)
        sums_ref[1:2] = jnp.sum(gfirst, axis=0, keepdims=True)
        sums_ref[2:3] = jnp.sum(gh1, axis=0, keepdims=True)
        sums_ref[3:8] = jnp.zeros((5, sums_ref.shape[1]), F32)


def feed_back(gffn, slope, low, wback, win, gh2, unit, inv, nv, wo, mixed):
    length, width = gffn.shape
    blocks = slope.shape[0]
    matrix = pl.BlockSpec((None,) + win.shape[1:], lambda b: (b, 0, 0, 0))
    single = pl.BlockSpec((None,) + wo.shape[1:], lambda b: (0, 0, 0, 0))
    one = whole((length, width))
    token = lambda d: jax.ShapeDtypeStruct((length, width), d)
    return pl.pallas_call(
        feed_back_kernel,
        grid=(blocks,),
        in_specs=[
            one,
            pl.BlockSpec((None, length, width), lambda b: (b, 0, 0)),
            one, matrix, matrix, one, one, whole(inv.shape), whole(nv.shape), single, one,
        ],
        out_specs=[
            matrix,
            pl.BlockSpec((1, 1, width), lambda b: (b, 0, 0)),
            one, single, one, whole((8, width)),
        ],
        out_shape=[
            jax.ShapeDtypeStruct(win.shape, BF),
            jax.ShapeDtypeStruct((blocks, 1, width), F32),
            token(F32),
            jax.ShapeDtypeStruct((1,) + win.shape[1:], BF),
            token(BF),
            jax.ShapeDtypeStruct((8, width), F32),
        ],
        scratch_shapes=[pltpu.VMEM((width, length), BF), pltpu.VMEM((length, width), F32)],
        compiler_params=params(),
        name="feed_back",
    )(gffn, slope, low, wback, win, gh2, unit, inv, nv, wo, mixed)


def attend_back_kernel(
    probs_ref, gm_ref, qc_ref, qp_ref, k_ref, v_ref, rel_ref,
    gq_ref, gk_ref, gv_ref, grel_ref, sums_ref,
    rel_acc,
):
    length, pair = gm_ref.shape
    block = ROW_BLOCK
    span = length + block
    zero = jnp.zeros((), BF)
    flip = (
        lax.broadcasted_iota(jnp.int32, (block, block), 0)
        + lax.broadcasted_iota(jnp.int32, (block, block), 1)
        == block - 1
    ).astype(F32).astype(BF)
    k = k_ref[...]
    v = v_ref[...]
    rel_acc[...] = jnp.zeros_like(rel_acc)
    gk = None
    gv = None
    sum_c = None
    sum_p = None
    for top in range(0, length, block):
        rows = pl.ds(top, block)
        first = length - block - top
        band = pl.ds(first, span)
        rel = rel_ref[band, :]
        qp_turned = mm(flip, qp_ref[rows, :]).astype(BF)
        gqc = None
        gqp = None
        for head in range(2):
            mask = lane_mask(head, (block, pair))
            tall = lane_mask(head, (length, pair))
            probs_low = probs_ref[head, rows, :]
            probs = probs_low.astype(F32)
            gm = jnp.where(mask, gm_ref[rows, :], zero)
            gprobs = mm(gm, v, NT)
            product = probs * gprobs
            inner = jnp.sum(product, axis=1, keepdims=True)
            gsum = (product - probs * inner).astype(BF)
            a = mm(gsum, jnp.where(tall, k, zero))
            gqc = a if gqc is None else gqc + a
            b = mm(gsum, jnp.where(mask, qc_ref[rows, :], zero), TN)
            gk = b if gk is None else gk + b
            c = mm(probs_low, gm, TN)
            gv = c if gv is None else gv + c
            turned = mm(flip, gsum)
            wide = jnp.concatenate([turned, jnp.zeros((block, block), F32)], axis=1)
            wide = pltpu.roll(wide, 0, 1, stride=1, stride_axis=0).astype(BF)
            rel_mask = lane_mask(head, (span, pair))
            d = mm(wide, jnp.where(rel_mask, rel, zero))
            gqp = d if gqp is None else gqp + d
            rel_acc[band, :] += mm(wide, jnp.where(mask, qp_turned, zero), TN)
        gqc = gqc * SCALE
        gqp = gqp * SCALE
        high = gqp.astype(BF)
        rest = (gqp - high.astype(F32)).astype(BF)
        straight = mm(flip, high) + mm(flip, rest)
        gq_ref[rows, :] = (gqc + straight).astype(BF)
        e = jnp.sum(gqc, axis=0, keepdims=True)
        f = jnp.sum(gqp, axis=0, keepdims=True)
        sum_c = e if sum_c is None else sum_c + e
        sum_p = f if sum_p is None else sum_p + f
    gk_ref[...] = gk.astype(BF)
    gv_ref[...] = gv.astype(BF)
    grel_ref[...] = rel_acc[...].astype(BF)
    sums_ref[0:1] = sum_c
    sums_ref[1:2] = sum_p
    sums_ref[2:8] = jnp.zeros((6, pair), F32)


def attend_back(probs, gm, qc, qp, k, v, rel):
    length, width = qc.shape
    pair = 2 * HEAD_FEATURES
    heads = width // HEAD_FEATURES
    column = pl.BlockSpec((length, pair), lambda p: (0, p))
    tall = pl.BlockSpec((rel.shape[0], pair), lambda p: (0, p))
    token = jax.ShapeDtypeStruct((length, width), BF)
    return pl.pallas_call(
        attend_back_kernel,
        grid=(heads // 2,),
        in_specs=[pl.BlockSpec((2, length, length), lambda p: (p, 0, 0))] + [column] * 5 + [tall],
        out_specs=[column, column, column, tall, pl.BlockSpec((8, pair), lambda p: (0, p))],
        out_shape=[
            token, token, token,
            jax.ShapeDtypeStruct(rel.shape, BF),
            jax.ShapeDtypeStruct((8, width), F32),
        ],
        scratch_shapes=[pltpu.VMEM((rel.shape[0], pair), F32)],
        compiler_params=params(),
        name="attend_back",
    )(probs, gm, qc, qp, k, v, rel)


def project_back_kernel(
    x_ref, gq_ref, gk_ref, gv_ref, grel_ref, sine_t_ref, w_ref, gh1_ref,
    gw_ref, gtok_ref,
    turned_ref,
):
    step = pl.program_id(0)

    @pl.when(step == 0)
    def _():
        turned_ref[...] = x_ref[...].T
        gtok_ref[...] = gh1_ref[...]

    for which, g_ref in enumerate((gq_ref, gk_ref, gv_ref)):

        @pl.when(step == which)
        def _():
            store_matrix(gw_ref, mm(turned_ref[...], g_ref[...]))
            gtok_ref[...] += mm(g_ref[...], full_matrix(w_ref), NT)

    @pl.when(step == 3)
    def _():
        store_matrix(gw_ref, mm(sine_t_ref[...], grel_ref[...]))


def project_back(x, gq, gk, gv, grel, sine_t, w, gh1):
    length, width = x.shape
    one = whole((length, width))
    return pl.pallas_call(
        project_back_kernel,
        grid=(4,),
        in_specs=[
            one, one, one, one, whole(grel.shape), whole(sine_t.shape),
            pl.BlockSpec((None,) + w.shape[1:], lambda b: (jnp.minimum(b, 2), 0, 0, 0)),
            one,
        ],
        out_specs=[pl.BlockSpec((None,) + w.shape[1:], lambda b: (b, 0, 0, 0)), one],
        out_shape=[
            jax.ShapeDtypeStruct((4,) + w.shape[1:], BF),
            jax.ShapeDtypeStruct((length, width), F32),
        ],
        scratch_shapes=[pltpu.VMEM((width, length), BF)],
        compiler_params=params(),
        name="project_back",
    )(x, gq, gk, gv, grel, sine_t, w, gh1)


def gather_matrices(shard):
    dp, mp = lax.axis_size("dp"), lax.axis_size("mp")
    blocks, rows, columns = shard.shape
    pieces = lax.all_gather(shard, ("mp", "dp"), axis=0, tiled=False)
    pieces = pieces.reshape(mp, dp, blocks, rows, columns)
    return pieces.transpose(2, 0, 1, 3, 4).reshape(blocks, mp, dp * rows, columns)


def scatter_matrices(grads):
    dp = lax.axis_size("dp")
    blocks, mp, all_rows, columns = grads.shape
    pieces = grads.reshape(blocks, mp, dp, all_rows // dp, columns).transpose(1, 2, 0, 3, 4)
    pieces = pieces.reshape(mp * dp, blocks, all_rows // dp, columns)
    return lax.psum_scatter(pieces, ("mp", "dp"), scatter_dimension=0, tiled=False)


def per_device(
    tokens,
    lengths,
    weights,
    weight_m1,
    weight_m2,
    head_vecs,
    head_m1,
    head_m2,
    norm_vecs,
    norm_m1,
    norm_m2,
    cotangent,
):
    mp_index = lax.axis_index("mp")
    seq_len = cotangent.shape[0]
    local_width = weights.shape[2]
    model_width = tokens.shape[1]
    x = lax.dynamic_slice_in_dim(tokens, mp_index * seq_len, seq_len, 0)
    used = lax.dynamic_slice_in_dim(lengths, mp_index, 1, 0)
    sine = relative_embedding(seq_len, model_width).astype(BF)
    shard = weights.transpose(1, 0, 2)
    blocks = gather_matrices(shard.astype(BF))
    heads_all = lax.all_gather(head_vecs, "mp", axis=1, tiled=True)

    qc, qp, k, v, rel = project(x, blocks[0:4], heads_all[0:2], sine)
    probs, mixed = attend(used, qc, qp, k, v, rel)
    hb = heads_all[2:6].reshape(4, 1, model_width)
    unit, inv, low, active, slope, out, gh2, gffn, sums2 = feed(
        mixed, blocks[4:5], x, norm_vecs, hb, blocks[5:9], blocks[9:13], cotangent
    )
    gwback = back_grad(gffn, active)
    gwin, hsum, gh1, gwo, gmixed, sums1 = feed_back(
        gffn, slope, low, blocks[9:13], blocks[5:9], gh2, unit, inv, norm_vecs, blocks[4:5], mixed
    )
    gq, gk, gv, grel, sums_q = attend_back(probs, gmixed, qc, qp, k, v, rel)
    gproj, grad_tokens = project_back(x, gq, gk, gv, grel, sine.T, blocks[0:4], gh1)

    weight_grad = scatter_matrices(
        jnp.concatenate([gproj, gwo, gwin, gwback], axis=0)
    ).astype(F32)
    norm_part = jnp.concatenate([sums1[0:2], sums2[0:2], sums1[2:3], sums2[2:3]], axis=0)
    head_part = jnp.concatenate([sums_q[0:2], hsum[:, 0]], axis=0)
    norm_grad, head_total = lax.psum((norm_part, head_part), ("dp", "mp"))
    head_grad = lax.dynamic_slice_in_dim(head_total, mp_index * local_width, local_width, 1)

    new_big = adam_update(
        shard, weight_grad, weight_m1.transpose(1, 0, 2), weight_m2.transpose(1, 0, 2), RATE_BIG
    )
    new_weights, new_weight_m1, new_weight_m2 = [a.transpose(1, 0, 2) for a in new_big]
    new_head, new_head_m1, new_head_m2 = adam_update(
        head_vecs, head_grad, head_m1, head_m2, RATE_SMALL
    )
    new_norm, new_norm_m1, new_norm_m2 = adam_update(
        norm_vecs, norm_grad, norm_m1, norm_m2, RATE_SMALL
    )
    return (
        out,
        grad_tokens,
        new_weights,
        new_weight_m1,
        new_weight_m2,
        new_head,
        new_head_m1,
        new_head_m2,
        new_norm,
        new_norm_m1,
        new_norm_m2,
    )


def solution(mesh):
    shard = P("dp", None, "mp")
    return jax.shard_map(
        per_device,
        mesh=mesh,
        in_specs=(P("dp", None), P("dp"), shard, shard, shard)
        + (P(None, "mp"),) * 3
        + (P(),) * 3
        + (P(("dp", "mp"), None),),
        out_specs=(P(("dp", "mp"), None),) * 2
        + (shard,) * 3
        + (P(None, "mp"),) * 3
        + (P(),) * 3,
        check_vma=False,
    )
```

time: 1160 us -> 436 us (0.38)
  local copies, waits for them, and re-layouts: 479 us -> 28.1 us
  matrix products: 173 us -> 0 us
  waiting for transfers between devices: 378 us -> 217 us
  Pallas kernels: 0 us -> 108 us
  other arithmetic: 45.5 us -> 22.3 us
  loops' own time: 19.6 us -> 0 us
    while x49 -> x0, local copies, waits for them, and re-layouts: 245 us -> none
    dot_general x41 -> x0, matrix products: 159 us -> none  [the longest x4 32.3 us: score_block(): jnp.einsum('slf,ylf->lsy', query_positions, relative_heads, preferred_ele...]
    psum x2 -> x0, waiting for transfers between devices: 124 us -> none  [the longest x1 72.8 us: per_device(): attn_sum = lax.psum(attn_part, 'mp')]
    pallas_call x0 -> x7, Pallas kernels: none -> 108 us  [the longest x1 27.9 us: attend_back(): pl.pallas_call(attend_back_kernel, grid=(heads // 2,), in_specs=[pl.Block...]
    reshape x16 -> x2, local copies, waits for them, and re-layouts: 90.1 us -> 7.01 us  [the longest x1 6.4 us: gather_matrices(): pieces = pieces.reshape(mp, dp, blocks, rows, columns)]
    slice x13 -> x9, local copies, waits for them, and re-layouts: 84.4 us -> 11.4 us  [the longest x1 5.72 us: per_device(): blocks[9:13]]
    unnamed x106 -> x29, local copies, waits for them, and re-layouts: 24.8 us -> 0.08 us
    reduce_sum x15 -> x0, other arithmetic: 23.2 us -> none  [the longest x3 6.35 us: layer_norm(): row_mean = jnp.mean(features, axis=-1, keepdims=True)]
  transfers between devices with their start and end apart: 8 -> 2, of which waited for: 7 -> 2; matrix products, arithmetic and copies ran while one was open for 6% -> 4% of each run, Pallas kernels for 0% -> 0%
where the time goes in v1:
time: 436 us; the launch traced here: 435 us
  waiting for transfers between devices  217 us (50%)
  Pallas kernels  108 us (25%)
  blocking collectives  45.1 us (10%)
  local copies, waits for them, and re-layouts  28.1 us (6%)
  other arithmetic  22.3 us (5%)
  between operations  14.2 us (3%)
    reduce_scatter x1, waiting for transfers between devices, scatter_matrices(): lax.psum_scatter(pieces, ('mp', 'dp'), scatter_dimension=0, tiled=False)  121 us
    all_gather x1, waiting for transfers between devices, gather_matrices(): pieces = lax.all_gather(shard, ('mp', 'dp'), axis=0, tiled=False)  95.6 us
    psum x1, blocking collectives, per_device(): norm_grad, head_total = lax.psum((norm_part, head_part), ('dp', 'mp'))  39.5 us
    pallas_call x1, Pallas kernels, attend_back(): pl.pallas_call(attend_back_kernel, grid=(heads // 2,), in_specs=[pl.Block...  27.9 us
    pallas_call x1, Pallas kernels, attend(): pl.pallas_call(attend_kernel, grid=(heads // 2,), in_specs=[pl.BlockSpec(...  18.8 us
    pallas_call x1, Pallas kernels, feed_back(): pl.pallas_call(feed_back_kernel, grid=(blocks,), in_specs=[one, pl.BlockS...  17.5 us
    pallas_call x1, Pallas kernels, feed(): pl.pallas_call(feed_kernel, grid=(blocks,), in_specs=[one, pl.BlockSpec((...  16.9 us
    pallas_call x1, Pallas kernels, project_back(): pl.pallas_call(project_back_kernel, grid=(4,), in_specs=[one, one, one, o...  11.5 us
  transfers between devices with their start and end apart: 2, of which 2 were waited for; matrix products, arithmetic and copies ran while one was open for 4% of the time, Pallas kernels for 0%

profile of v1, /device:TPU:0, one launch (start us, length us, event | category | flops | bytes accessed | tf_op | source)
XLA Modules:
  0.0 434.7 jit_solution(3776995971727859487)
XLA Ops:
  7.2 0.0 copy-start
  7.2 0.0 all-gather.3.cloned.1.call-start
  7.2 2.1 bitcast_convert_fusion
  9.4 0.0 all-gather.3.cloned.1.call-update
  9.4 0.0 reduce-scatter.2.cloned.1.call-start
  9.4 5.6 %all_gather.11 = f32[6,768]{1,0:T(8,128)S(1)} all-gather(f32[6,384]{1,0:T(8,128)} %param.17), channel_id=1, replica_groups=mesh['dp'=16,'mp'=2] {'mp'}, dimensions={1}, use_global_device_ids=true | all-gather | bytes 27648 | tf_op jit(solution)/shard_map/all_gather | solution.py:545
  15.0 0.6 slice.65.vec_ref
  15.6 0.6 reshape.54.hb_ref
  16.2 6.0 %fusion = (bf16[1024,384]{0,1:T(8,128)(2,1)S(1)}, bf16[1024,384]{0,1:T(8,128)(2,1)S(1)}) fusion(f32[384]{0:T(512)S(1)} %negate_power_fusion, f32[1024]{0:T(1024)S(1)} %subtract_convert_fusion), kind=kLoop, calls=%fused_computation.4 | loop fusion | flops 1179648 | bytes 1578496 | tf_op jit(solution)/shard_map/convert.1
  22.3 0.0 copy-start.11
  22.3 1.5 fusion.10
  23.8 1.6 copy.27.sine_ref
  25.4 0.6 dynamic_slice.9.len_ref
  26.0 0.9 constant_dynamic-slice_fusion.x_ref
  26.9 95.6 %all-gather.3.cloned.1.call-done = bf16[416,48,384]{2,1,0:T(8,128)(2,1)} async-done(((bf16[13,48,384]{2,1,0:T(8,128)(2,1)}), bf16[416,48,384]{2,1,0:T(8,128)(2,1)}) %all-gather.3.cloned.1.call-update) | async-done | bytes 15335440 | tf_op jit(solution)/shard_map/all_gather | solution.py:509
  122.5 6.4 %copy.32 = bf16[2,16,13,48,384]{4,3,1,0,2:T(8,128)(2,1)S(1)} copy(bf16[2,16,13,48,384]{4,3,2,1,0:T(8,128)(2,1)} %bitcast.64) | data formatting | bytes 30670848 | tf_op jit(solution)/shard_map/reshape | solution.py:510
  128.9 1.2 slice.66
  130.1 5.7 %fusion.13 = (bf16[4,2,16,48,384]{4,3,2,1,0:T(8,128)(2,1)}, bf16[4,2,16,48,384]{4,3,2,1,0:T(8,128)(2,1)}, bf16[4,2,16,48,384]{4,3,2,1,0:T(8,128)(2,1)}) fusion(bf16[13,2,16,48,384]{4,3,2,1,0:T(8,128)(2,1)S(1)} %bitcast.53), kind=kLoop, calls=%fused_computation.33 | loop fusion | bytes 28311552 | tf_op jit(solution)/shard_map/slice | solution.py:551
  135.8 8.7 %project.1 = (bf16[512,768]{1,0:T(8,128)(2,1)}, bf16[512,768]{1,0:T(8,128)(2,1)}, bf16[512,768]{1,0:T(8,128)(2,1)}, bf16[512,768]{1,0:T(8,128)(2,1)}, bf16[1024,768]{1,0:T(8,128)(2,1)}) custom-call(bf16[512,768]{1,0:T(8,128)(2,1)} %constant_dynamic-slice_fusion.x_ref, bf16[4,2,768,384]{3,2,1,0:T(8,128)(2,1)} %bitcast.56, f32[2,768]{1,0:T(2,128)} %slice.65.vec_ref, ...), custom_call_target="tpu_custom_call" | custom-call | tf_op jit(solution)/shard_map/project/pallas_call | solution.py:98
  144.5 18.8 %attend.1 = (bf16[12,512,512]{2,1,0:T(8,128)(2,1)}, bf16[512,768]{1,0:T(8,128)(2,1)}) custom-call(s32[1]{0:T(128)} %dynamic_slice.9.len_ref, bf16[512,768]{1,0:T(8,128)(2,1)} %get-tuple-element.40.qc_ref, bf16[512,768]{1,0:T(8,128)(2,1)} %get-tuple-element.41.qp_ref, bf16[512,768]{1,0:T(8,128)(2,1)} %get-tuple-element.42.k_ref, ...), custom_call_target="tpu_custom_call" | custom-call | tf_op jit(solution)/shard_map/attend/pallas_call | solution.py:154
  163.2 16.9 %feed.1 = (f32[512,768]{1,0:T(8,128)}, f32[512,128]{1,0:T(8,128)}, bf16[512,768]{1,0:T(8,128)(2,1)}, bf16[4,512,768]{2,1,0:T(8,128)(2,1)}, bf16[4,512,768]{2,1,0...) custom-call(bf16[512,768]{1,0:T(8,128)(2,1)} %get-tuple-element.45.m, ...), custom_call_target="tpu_custom_call" | custom-call | tf_op jit(solution)/shard_map/feed/pallas_call | solution.py:245
  180.1 6.7 %back_grad.1 = bf16[4,2,768,384]{3,2,1,0:T(8,128)(2,1)} custom-call(bf16[512,768]{1,0:T(8,128)(2,1)} %get-tuple-element.48.gffn_ref, bf16[4,512,768]{2,1,0:T(8,128)(2,1)} %get-tuple-element.64.act_ref), custom_call_target="tpu_custom_call" | custom-call | tf_op jit(solution)/shard_map/back_grad/pallas_call | solution.py:283
  186.8 17.5 %feed_back.1 = (bf16[4,2,768,384]{3,2,1,0:T(8,128)(2,1)}, f32[4,1,768]{2,1,0:T(1,128)}, f32[512,768]{1,0:T(8,128)}, bf16[1,2,768,384]{3,2,1,0:T(8,128)(2,1)}, bf...) custom-call(bf16[512,768]{1,0:T(8,128)(2,1)} %get-tuple-element.48.gffn_ref, bf16[4,512,768]{2,1,0:T(8,128)(2,1)} %get-tuple-element.49.slope_ref, ...), custom_call_target="tpu_custom_call" | custom-call | tf_op jit(solution)/shard_map/feed_back/pallas_call | solution.py:340
  204.3 27.9 %attend_back.1 = (bf16[512,768]{1,0:T(8,128)(2,1)}, bf16[512,768]{1,0:T(8,128)(2,1)}, bf16[512,768]{1,0:T(8,128)(2,1)}, bf16[1024,768]{1,0:T(8,128)(2,1)}, f32[8,768]{1,0:T(8,128)}) custom-call(bf16[12,512,512]{2,1,0:T(8,128)(2,1)} %get-tuple-element.47.probs_ref, bf16[512,768]{1,0:T(8,128)(2,1)} %get-tuple-element.54.gm_ref, ...), custom_call_target="tpu_custom_call" | custom-call | tf_op jit(solution)/shard_map/attend_back/pallas_call | solution.py:444
  232.2 0.0 slice-start
  232.2 0.0 slice-start.1
  232.2 11.5 %project_back.1 = (bf16[4,2,768,384]{3,2,1,0:T(8,128)(2,1)}, f32[512,768]{1,0:T(8,128)}) custom-call(bf16[512,768]{1,0:T(8,128)(2,1)} %constant_dynamic-slice_fusion.x_ref, bf16[512,768]{1,0:T(8,128)(2,1)} %get-tuple-element.55.gq_ref, bf16[512,768]{1,0:T(8,128)(2,1)} %get-tuple-element.56.gk_ref, bf16[512,768]{1,0:T(8,128)(2,1)} %get-tuple-element.57.gv_ref, ...), custom_call_target="tpu_custom_call" | custom-call | tf_op jit(solution)/shard_map/project_back/pallas_call | solution.py:487
  243.8 6.8 %pad_maximum_fusion = bf16[13,2,768,384]{3,2,1,0:T(8,128)(2,1)S(1)} fusion(bf16[4,2,768,384]{3,2,1,0:T(8,128)(2,1)S(1)} %bitcast.63, bf16[4,2,768,384]{3,2,1,0:T(8,128)(2,1)} %get-tuple-element.63, bf16[1,2,768,384]{3,2,1,0:T(8,128)(2,1)S(1)} %copy-done.3, bf16[4,2,768,384]{3,2,1,0:T(8,128)(2,1)} %get-tuple-element.61), kind=kLoop, calls=%fused_computation | loop fusion | flops 23003136 | bytes 30670848 | tf_op jit(solution)/shard_map/concatenate | solution.py:561
  250.6 6.6 %copy.28 = bf16[2,16,13,48,384]{4,3,2,1,0:T(8,128)(2,1)} copy(bf16[2,16,13,48,384]{4,3,1,0,2:T(8,128)(2,1)S(1)} %bitcast.55) | data formatting | bytes 30670848 | tf_op jit(solution)/shard_map/transpose | solution.py:517
  257.2 0.0 copy-start.5
  257.2 0.0 copy-start.7
  257.2 0.0 copy-start.2
  257.2 0.0 copy-start.4
  257.2 0.0 reduce-scatter.2.cloned.1.call-update
  257.2 0.9 slice.62
  258.1 0.7 slice.60
  258.9 0.7 slice.63
  259.6 0.7 slice.61
  260.3 0.8 slice.59
  261.1 39.5 %all-reduce = (f32[6,768]{1,0:T(8,128)S(1)}, f32[6,768]{1,0:T(8,128)}) all-reduce(f32[6,768]{1,0:T(8,128)S(1)} %get-tuple-element.87, f32[6,768]{1,0:T(8,128)S(1)} %get-tuple-element.88), channel_id=1, replica_groups=mesh['dp'=16,'mp'=2] {'dp','mp'}, use_global_device_ids=true, to_apply=%region_1.0 | all-reduce | flops 9216 | bytes 73728 | tf_op jit(solution)/shard_map/psum | solution.py:565
  300.7 0.0 copy-done.6
  300.7 0.0 copy-done.10
  300.7 0.6 multiply_subtract_fusion.1
  301.3 0.0 copy-done.5
  301.3 1.5 multiply_subtract_fusion
  302.8 121.3 %reduce-scatter.2.cloned.1.call-done = bf16[1,13,48,384]{3,2,1,0:T(8,128)(2,1)} async-done(((bf16[32,13,48,384]{3,2,1,0:T(8,128)(2,1)}), bf16[1,13,48,384]{3,2,1,0:T(8,128)(2,1)}) %reduce-scatter.2.cloned.1.call-update) | async-done | bytes 479248 | tf_op jit(solution)/shard_map/reduce_scatter | solution.py:519
  424.2 0.0 copy-done.2
  424.2 3.6 fusion.7
  (22 shorter events, 0.1 us)
Async XLA Ops:
  7.2 18.8 %copy-start = (bf16[1024,768]{1,0:T(8,128)(2,1)S(1)}, bf16[1024,768]{1,0:T(8,128)(2,1)}, u32[]{:S(2)}) copy-start(bf16[1024,768]{1,0:T(8,128)(2,1)} %param.12) | copy-start | bytes 4718596
  7.2 115.3 %all-gather.3.cloned.1.call-start = ((), (), s32[]{:S(2)}) async-start(), calls=%async_computation.2 | async-start | bytes 15814656 | tf_op jit(solution)/shard_map/all_gather | solution.py:509
  9.4 414.8 %reduce-scatter.2.cloned.1.call-start = ((), (), s32[]{:S(2)}) async-start(), calls=%async_computation.1 | async-start | bytes 15814656 | tf_op jit(solution)/shard_map/reduce_scatter | solution.py:519
  22.3 3.1 copy-start.11
  232.2 11.6 %slice-start = ((s8[4718592]{0:T(1024)(128)(4,1)}), s8[4194304]{0:T(1024)(128)(4,1)S(1)}, s32[]{:S(2)}) async-start(s8[4718592]{0:T(1024)(128)(4,1)} %bitcast.62), calls=%async_computation.3 | async-start | bytes 8388608
  232.2 11.6 %slice-start.1 = ((s8[4718592]{0:T(1024)(128)(4,1)}), s8[524288]{0:T(1024)(128)(4,1)S(1)}, s32[]{:S(2)}) async-start(s8[4718592]{0:T(1024)(128)(4,1)} %bitcast.62), calls=%async_computation.4 | async-start | bytes 1048576
  232.2 11.6 %copy-start.3 = (bf16[1,2,768,384]{3,2,1,0:T(8,128)(2,1)S(1)}, bf16[1,2,768,384]{3,2,1,0:T(8,128)(2,1)}, u32[]{:S(2)}) copy-start(bf16[1,2,768,384]{3,2,1,0:T(8,128)(2,1)} %get-tuple-element.62) | copy-start | bytes 3538948
  257.2 3.9 copy-start.8
  257.2 43.5 %copy-start.6 = (f32[6,384]{1,0:T(8,128)S(1)}, f32[6,384]{1,0:T(8,128)}, u32[]{:S(2)}) copy-start(f32[6,384]{1,0:T(8,128)} %param.17) | copy-start | bytes 27652
  257.2 43.5 %copy-start.9 = (f32[6,384]{1,0:T(8,128)S(1)}, f32[6,384]{1,0:T(8,128)}, u32[]{:S(2)}) copy-start(f32[6,384]{1,0:T(8,128)} %param.18) | copy-start | bytes 27652
  257.2 43.5 %copy-start.10 = (f32[6,384]{1,0:T(8,128)S(1)}, f32[6,384]{1,0:T(8,128)}, u32[]{:S(2)}) copy-start(f32[6,384]{1,0:T(8,128)} %param.19) | copy-start | bytes 27652
  257.2 44.2 %copy-start.5 = (f32[6,768]{1,0:T(8,128)S(1)}, f32[6,768]{1,0:T(8,128)}, u32[]{:S(2)}) copy-start(f32[6,768]{1,0:T(8,128)} %nv_ref.3) | copy-start | bytes 55300
  257.2 44.2 %copy-start.7 = (f32[6,768]{1,0:T(8,128)S(1)}, f32[6,768]{1,0:T(8,128)}, u32[]{:S(2)}) copy-start(f32[6,768]{1,0:T(8,128)} %param.21) | copy-start | bytes 55300
  257.2 167.0 %copy-start.2 = (f32[48,13,384]{2,0,1:T(8,128)S(1)}, f32[48,13,384]{2,0,1:T(8,128)}, u32[]{:S(2)}) copy-start(f32[48,13,384]{2,0,1:T(8,128)} %param.14) | copy-start | bytes 2875396
  257.2 167.0 %copy-start.4 = (f32[48,13,384]{2,0,1:T(8,128)S(1)}, f32[48,13,384]{2,0,1:T(8,128)}, u32[]{:S(2)}) copy-start(f32[48,13,384]{2,0,1:T(8,128)} %param.16) | copy-start | bytes 2875396
  301.3 126.5 %copy-start.1 = (bf16[1024,768]{1,0:T(8,128)(2,1)S(1)}, bf16[1024,768]{1,0:T(8,128)(2,1)}, u32[]{:S(2)}) copy-start(bf16[1024,768]{1,0:T(8,128)(2,1)} %param.12) | copy-start | bytes 4718596
Sparse Core Ops, SparseCore 0:
  11.5 110.9 all-gather.2
  257.4 166.7 reduce-scatter.1

commit v2 on v1

--- a/solution.py
+++ b/solution.py
@@ -40,6 +40,10 @@
     return pltpu.CompilerParams(vmem_limit_bytes=VMEM_LIMIT)
 
 
+def cost(micros):
+    return pl.CostEstimate(flops=int(micros * 1e9), bytes_accessed=0, transcendentals=0)
+
+
 def relative_embedding(length, model_width):
     distance = (length - 1 - jnp.arange(2 * length)).astype(F32)
     freq_index = jnp.arange(model_width // 2).astype(F32)
@@ -59,14 +63,50 @@
     return (new_param, new_one, new_two)
 
 
+def weight_spec(shape, which):
+    if len(shape) == 5:
+        return pl.BlockSpec(shape[:2] + (None,) + shape[3:], lambda b: (0, 0, which(b), 0, 0))
+    return pl.BlockSpec((None,) + shape[1:], lambda b: (which(b), 0, 0, 0))
+
+
 def full_matrix(w_ref):
-    return jnp.concatenate([w_ref[0], w_ref[1]], axis=1)
+    w = w_ref[...]
+    if w.ndim == 4:
+        w = w.reshape(w.shape[0], w.shape[1] * w.shape[2], w.shape[3])
+    return jnp.concatenate([w[0], w[1]], axis=1)
+
+
+RING = ((0, 0, 0), (0, 0, 1), (0, 1, 1), (0, 1, 0), (1, 1, 0), (1, 1, 1), (1, 0, 1), (1, 0, 0))
+
+
+def layered(lines, rows):
+    return rows % 16 == 0
+
+
+def grad_shape(blocks, lines, rows, columns):
+    if layered(lines, rows):
+        return (len(RING), lines, blocks, rows, columns)
+    return (blocks, 2, lines * 4 * rows, columns)
+
+
+def grad_spec(shape):
+    if len(shape) == 5:
+        return pl.BlockSpec(shape[:2] + (None,) + shape[3:], lambda b: (0, 0, b, 0, 0))
+    return pl.BlockSpec((None,) + shape[1:], lambda b: (b, 0, 0, 0))
 
 
 def store_matrix(out_ref, value):
     half = value.shape[1] // 2
-    out_ref[0] = value[:, :half].astype(BF)
-    out_ref[1] = value[:, half:].astype(BF)
+    low = value.astype(BF)
+    if len(out_ref.shape) == 3:
+        out_ref[0] = low[:, :half]
+        out_ref[1] = low[:, half:]
+        return
+    places, lines, rows, _ = out_ref.shape
+    for place, (mp, y, core) in enumerate(RING):
+        for line in range(lines):
+            top = (line * 4 + y * 2 + core) * rows
+            out_ref[place, line] = low[top : top + rows, mp * half : (mp + 1) * half]
 
 
 def project_kernel(x_ref, w_ref, vec_ref, sine_ref, qc_ref, qp_ref, k_ref, v_ref, rel_ref):
@@ -100,13 +140,14 @@
         grid=(4,),
         in_specs=[
             whole(x.shape),
-            pl.BlockSpec((None,) + w.shape[1:], lambda b: (b, 0, 0, 0)),
+            weight_spec(w.shape, lambda b: b),
             whole(vecs.shape),
             whole(sine.shape),
         ],
         out_specs=[whole(s) for s in shapes],
         out_shape=[jax.ShapeDtypeStruct(s, BF) for s in shapes],
         compiler_params=params(),
+        cost_estimate=cost(9),
         name="project",
     )(x, w, vecs, sine)
 
@@ -163,6 +204,7 @@
             jax.ShapeDtypeStruct((length, width), BF),
         ],
         compiler_params=params(),
+        cost_estimate=cost(19),
         name="attend",
     )(length_used, qc, qp, k, v, rel)
 
@@ -234,10 +276,9 @@
         sums_ref[3:8] = jnp.zeros((5, sums_ref.shape[1]), F32)
 
 
-def feed(mixed, wo, x, nv, hb, win, wback, cot):
+def feed(mixed, w, x, nv, hb, w_feed, cot):
     length, width = x.shape
-    blocks = win.shape[0]
-    matrix = pl.BlockSpec((None,) + win.shape[1:], lambda b: (b, 0, 0, 0))
+    blocks = hb.shape[0]
     one = whole((length, width))
     column = pl.BlockSpec((None, length, width), lambda b: (b, 0, 0))
     token = lambda d: jax.ShapeDtypeStruct((length, width), d)
@@ -247,12 +288,12 @@
         grid=(blocks,),
         in_specs=[
             one,
-            pl.BlockSpec((None,) + wo.shape[1:], lambda b: (0, 0, 0, 0)),
+            weight_spec(w.shape, lambda b: 4),
             one,
             whole(nv.shape),
             pl.BlockSpec((1, 1, width), lambda b: (b, 0, 0)),
-            matrix,
-            matrix,
+            weight_spec(w_feed.shape, lambda b: b),
+            weight_spec(w_feed.shape, lambda b: b + blocks),
             one,
         ],
         out_specs=[
@@ -264,8 +305,9 @@
         ],
         scratch_shapes=[pltpu.VMEM((length, width), F32), pltpu.VMEM((length, width), F32)],
         compiler_params=params(),
+        cost_estimate=cost(17),
         name="feed",
-    )(mixed, wo, x, nv, hb, win, wback, cot)
+    )(mixed, w, x, nv, hb, w_feed, w_feed, cot)
 
 
 def back_grad_kernel(gffn_ref, act_ref, out_ref, turned_ref):
@@ -276,10 +318,10 @@
     store_matrix(out_ref, mm(turned_ref[...], act_ref[...]))
 
 
-def back_grad(gffn, active):
+def back_grad(gffn, active, lines, rows):
     length, width = gffn.shape
     blocks = active.shape[0]
-    shape = (blocks, 2, width, width // 2)
+    shape = grad_shape(blocks, lines, rows, width // 2)
     return pl.pallas_call(
         back_grad_kernel,
         grid=(blocks,),
@@ -287,10 +329,11 @@
             whole(gffn.shape),
             pl.BlockSpec((None, length, width), lambda b: (b, 0, 0)),
         ],
-        out_specs=pl.BlockSpec((None,) + shape[1:], lambda b: (b, 0, 0, 0)),
+        out_specs=grad_spec(shape),
         out_shape=jax.ShapeDtypeStruct(shape, BF),
         scratch_shapes=[pltpu.VMEM((width, length), BF)],
         compiler_params=params(),
+        cost_estimate=cost(7),
         name="back_grad",
     )(gffn, active)
 
@@ -298,7 +341,7 @@
 def feed_back_kernel(
     gffn_ref, slope_ref, low_ref, wback_ref, win_ref, gh2_ref, unit_ref, inv_ref, nv_ref,
     wo_ref, mixed_ref,
-    gwin_ref, hsum_ref, gh1_ref, gwo_ref, gmixed_ref, sums_ref,
+    gw_ref, hsum_ref, gh1_ref, gmixed_ref, sums_ref,
     turned_ref, acc_ref,
 ):
     step = pl.program_id(0)
@@ -309,11 +352,13 @@
         turned_ref[...] = low_ref[...].T
         acc_ref[...] = gh2_ref[...]
 
-    gact = mm(gffn_ref[...], full_matrix(wback_ref))
-    ghid = (gact * slope_ref[...].astype(F32)).astype(BF)
-    hsum_ref[0] = jnp.sum(ghid.astype(F32), axis=0, keepdims=True)
-    store_matrix(gwin_ref, mm(turned_ref[...], ghid))
-    acc_ref[...] += mm(ghid, full_matrix(win_ref), NT)
+    @pl.when(step < last)
+    def _():
+        gact = mm(gffn_ref[...], full_matrix(wback_ref))
+        ghid = (gact * slope_ref[...].astype(F32)).astype(BF)
+        hsum_ref[0] = jnp.sum(ghid.astype(F32), axis=0, keepdims=True)
+        store_matrix(gw_ref, mm(turned_ref[...], ghid))
+        acc_ref[...] += mm(ghid, full_matrix(win_ref), NT)
 
     @pl.when(step == last)
     def _():
@@ -322,7 +367,7 @@
         gh1 = norm_back(unit, inv_ref[:, 0:1], gfirst * nv_ref[0:1])
         gh1_ref[...] = gh1
         gattn = gh1.astype(BF)
-        store_matrix(gwo_ref, mm(gattn.T, mixed_ref[...]))
+        store_matrix(gw_ref, mm(gattn.T, mixed_ref[...]))
         gmixed_ref[...] = mm(gattn, full_matrix(wo_ref)).astype(BF)
         sums_ref[0:1] = jnp.sum(gfirst * unit, axis=0, keepdims=True)
         sums_ref[1:2] = jnp.sum(gfirst, axis=0, keepdims=True)
@@ -330,38 +375,41 @@
         sums_ref[3:8] = jnp.zeros((5, sums_ref.shape[1]), F32)
 
 
-def feed_back(gffn, slope, low, wback, win, gh2, unit, inv, nv, wo, mixed):
+def feed_back(gffn, slope, low, w_feed, gh2, unit, inv, nv, w, mixed, lines, rows):
     length, width = gffn.shape
     blocks = slope.shape[0]
-    matrix = pl.BlockSpec((None,) + win.shape[1:], lambda b: (b, 0, 0, 0))
-    single = pl.BlockSpec((None,) + wo.shape[1:], lambda b: (0, 0, 0, 0))
+    capped = lambda b: jnp.minimum(b, blocks - 1)
     one = whole((length, width))
     token = lambda d: jax.ShapeDtypeStruct((length, width), d)
+    shape = grad_shape(blocks + 1, lines, rows, width // 2)
     return pl.pallas_call(
         feed_back_kernel,
-        grid=(blocks,),
+        grid=(blocks + 1,),
         in_specs=[
             one,
-            pl.BlockSpec((None, length, width), lambda b: (b, 0, 0)),
-            one, matrix, matrix, one, one, whole(inv.shape), whole(nv.shape), single, one,
+            pl.BlockSpec((None, length, width), lambda b: (capped(b), 0, 0)),
+            one,
+            weight_spec(w_feed.shape, lambda b: capped(b) + blocks),
+            weight_spec(w_feed.shape, capped),
+            one, one, whole(inv.shape), whole(nv.shape), weight_spec(w.shape, lambda b: 4), one,
         ],
         out_specs=[
-            matrix,
-            pl.BlockSpec((1, 1, width), lambda b: (b, 0, 0)),
-            one, single, one, whole((8, width)),
+            grad_spec(shape),
+            pl.BlockSpec((1, 1, width), lambda b: (capped(b), 0, 0)),
+            one, one, whole((8, width)),
         ],
         out_shape=[
-            jax.ShapeDtypeStruct(win.shape, BF),
+            jax.ShapeDtypeStruct(shape, BF),
             jax.ShapeDtypeStruct((blocks, 1, width), F32),
             token(F32),
-            jax.ShapeDtypeStruct((1,) + win.shape[1:], BF),
             token(BF),
             jax.ShapeDtypeStruct((8, width), F32),
         ],
         scratch_shapes=[pltpu.VMEM((width, length), BF), pltpu.VMEM((length, width), F32)],
         compiler_params=params(),
+        cost_estimate=cost(17),
         name="feed_back",
-    )(gffn, slope, low, wback, win, gh2, unit, inv, nv, wo, mixed)
+    )(gffn, slope, low, w_feed, w_feed, gh2, unit, inv, nv, w, mixed)
 
 
 def attend_back_kernel(
@@ -453,6 +501,7 @@
         ],
         scratch_shapes=[pltpu.VMEM((rel.shape[0], pair), F32)],
         compiler_params=params(),
+        cost_estimate=cost(28),
         name="attend_back",
     )(probs, gm, qc, qp, k, v, rel)
 
@@ -481,42 +530,200 @@
         store_matrix(gw_ref, mm(sine_t_ref[...], grel_ref[...]))
 
 
-def project_back(x, gq, gk, gv, grel, sine_t, w, gh1):
+def project_back(x, gq, gk, gv, grel, sine_t, w, gh1, lines, rows):
     length, width = x.shape
     one = whole((length, width))
+    shape = grad_shape(4, lines, rows, width // 2)
     return pl.pallas_call(
         project_back_kernel,
         grid=(4,),
         in_specs=[
             one, one, one, one, whole(grel.shape), whole(sine_t.shape),
-            pl.BlockSpec((None,) + w.shape[1:], lambda b: (jnp.minimum(b, 2), 0, 0, 0)),
+            weight_spec(w.shape, lambda b: jnp.minimum(b, 2)),
             one,
         ],
-        out_specs=[pl.BlockSpec((None,) + w.shape[1:], lambda b: (b, 0, 0, 0)), one],
-        out_shape=[
-            jax.ShapeDtypeStruct((4,) + w.shape[1:], BF),
-            jax.ShapeDtypeStruct((length, width), F32),
-        ],
+        out_specs=[grad_spec(shape), one],
+        out_shape=[jax.ShapeDtypeStruct(shape, BF), jax.ShapeDtypeStruct((length, width), F32)],
         scratch_shapes=[pltpu.VMEM((width, length), BF)],
         compiler_params=params(),
+        cost_estimate=cost(11),
         name="project_back",
     )(x, gq, gk, gv, grel, sine_t, w, gh1)
 
 
+def swap_x(value):
+    return lax.ppermute(value, "mp", [(0, 1), (1, 0)])
+
+
+def swap_dp(value, bit):
+    return lax.ppermute(value, "dp", [(d, d ^ bit) for d in range(lax.axis_size("dp"))])
+
+
+def shift_line(value, step):
+    dp = lax.axis_size("dp")
+    return lax.ppermute(value, "dp", [(d, (d + 4 * step) % dp) for d in range(dp)])
+
+
 def gather_matrices(shard):
-    dp, mp = lax.axis_size("dp"), lax.axis_size("mp")
+    pieces = lax.all_gather(shard, ("mp", "dp"), axis=0, tiled=False)
+    pieces = pieces.reshape((2, lax.axis_size("dp")) + shard.shape)
+    if shard.shape[1] % 16 == 0:
+        return pieces
+    return whole_matrices(pieces)
+
+
+def whole_matrices(pieces):
+    mp, dp, blocks, rows, columns = pieces.shape
+    return pieces.transpose(2, 0, 1, 3, 4).reshape(blocks, mp, dp * rows, columns)
+
+
+def place_kernel(lines, place_ref, *refs):
+    parts, out_ref, sem = refs[:-2], refs[-2], refs[-1]
+    mp, line, y, core = (place_ref[i] for i in range(4))
+    rows = parts[0].shape[2]
+    copies = []
+    for index, part in enumerate(parts):
+        top, dx, dy, dc = PARTS[index]
+        first = 0 if top == 0 else out_ref.shape[0] - part.shape[1]
+        for step in range(lines):
+            at = lax.rem(line + lines - step, lines) * 4 + (y ^ dy) * 2 + (core ^ dc)
+            start = pl.multiple_of(at * rows, rows)
+            copies.append(
+                pltpu.make_async_copy(
+                    part.at[step],
+                    out_ref.at[pl.ds(first, part.shape[1]), mp ^ dx, pl.ds(start, rows)],
+                    sem.at[len(copies)],
+                )
+            )
+    for copy in copies:
+        copy.start()
+    for copy in copies:
+        copy.wait()
+
+
+PARTS = [
+    (half, dx, dy, dc)
+    for dc in (0, 1)
+    for half, dx, dy in (
+        (0, 0, 0), (1, 0, 0), (0, 1, 0), (1, 0, 1), (0, 0, 1), (1, 1, 0), (0, 1, 1), (1, 1, 1),
+    )
+]
+
+
+def gather_stepwise(shard):
+    dp = lax.axis_size("dp")
     blocks, rows, columns = shard.shape
-    pieces = lax.all_gather(shard, ("mp", "dp"), axis=0, tiled=False)
-    pieces = pieces.reshape(mp, dp, blocks, rows, columns)
-    return pieces.transpose(2, 0, 1, 3, 4).reshape(blocks, mp, dp * rows, columns)
-
-
-def scatter_matrices(grads):
+    lines = dp // 4
+    if lines != 4 or rows % 16 != 0:
+        return gather_matrices(shard)
+    near = jnp.stack([shard] + [shift_line(shard, step) for step in range(1, lines)])
+    cut = blocks // 2
+    one, two = near[:, :cut], near[:, cut:]
+    one_x = swap_x(one)
+    two_y = swap_dp(two, 2)
+    one_y = swap_dp(one, 2)
+    two_x = swap_x(two)
+    one_xy = swap_dp(one_x, 2)
+    two_xy = swap_x(two_y)
+    lane = [one, two, one_x, two_y, one_y, two_x, one_xy, two_xy]
+    parts = lane + [swap_dp(part, 1) for part in lane]
+    index = lax.axis_index("dp")
+    place = jnp.stack([lax.axis_index("mp"), index // 4, (index // 2) % 2, index % 2])
+    anywhere = pl.BlockSpec(memory_space=pl.ANY)
+    return pl.pallas_call(
+        functools.partial(place_kernel, lines),
+        in_specs=[pl.BlockSpec(memory_space=pltpu.SMEM)] + [anywhere] * len(parts),
+        out_specs=pl.BlockSpec(memory_space=pltpu.VMEM),
+        out_shape=jax.ShapeDtypeStruct((blocks, 2, dp * rows, columns), BF),
+        scratch_shapes=[pltpu.SemaphoreType.DMA((len(parts) * lines,))],
+        compiler_params=params(),
+        cost_estimate=cost(5),
+        name="place",
+    )(place.astype(jnp.int32), *parts)
+
+
+def plane_groups(dp):
+    return [
+        [mp * dp + line * 4 + y * 2 + core for mp, y, core in RING] for line in range(dp // 4)
+    ]
+
+
+def line_groups(dp):
+    return [
+        [mp * dp + line * 4 + low for line in range(dp // 4)] for mp in range(2) for low in range(4)
+    ]
+
+
+def scatter_plane(grads):
     dp = lax.axis_size("dp")
-    blocks, mp, all_rows, columns = grads.shape
-    pieces = grads.reshape(blocks, mp, dp, all_rows // dp, columns).transpose(1, 2, 0, 3, 4)
-    pieces = pieces.reshape(mp * dp, blocks, all_rows // dp, columns)
-    return lax.psum_scatter(pieces, ("mp", "dp"), scatter_dimension=0, tiled=False)
+    if grads.ndim == 4:
+        blocks, _, all_rows, columns = grads.shape
+        grads = grads.reshape(blocks, 2, dp // 4, 2, 2, all_rows // dp, columns)
+        grads = jnp.stack([grads[:, mp, :, y, core] for mp, y, core in RING])
+        grads = grads.transpose(0, 2, 1, 3, 4)
+    return lax.psum_scatter(
+        grads, ("mp", "dp"), scatter_dimension=0, axis_index_groups=plane_groups(dp), tiled=False
+    )
+
+
+def scatter_line(part):
+    dp = lax.axis_size("dp")
+    lines = dp // 4
+    if lines != 4:
+        return lax.psum_scatter(
+            part, ("mp", "dp"), scatter_dimension=0, axis_index_groups=line_groups(dp), tiled=False
+        ).astype(F32)
+    line = lax.axis_index("dp") // 4
+    pick = lambda step: lax.dynamic_index_in_dim(part, (line + step) % lines, 0, keepdims=False)
+    received = [shift_line(pick(step), step) for step in range(1, lines)]
+    total = pick(0).astype(F32)
+    for piece in received:
+        total = total + piece.astype(F32)
+    return total
+
+
+def sum_small(value):
+    value = value + swap_dp(value, 1)
+    value = value + swap_x(value)
+    value = value + swap_dp(value, 2)
+    lines = lax.axis_size("dp") // 4
+    if lines != 4:
+        return lax.psum(value, ("dp",), axis_index_groups=line_only(lines))
+    total = value
+    for piece in [shift_line(value, step) for step in range(1, lines)]:
+        total = total + piece
+    return total
+
+
+def line_only(lines):
+    return [[line * 4 + low for line in range(lines)] for low in range(4)]
+
+
+def adam_kernel(g_ref, p_ref, one_ref, two_ref, *refs):
+    outs = refs[-3:]
+    results = adam_update(p_ref[...], g_ref[...], one_ref[...], two_ref[...], RATE_BIG)
+    for out, result in zip(outs, results):
+        out[...] = result
+
+
+def adam_blocks(grad, first, param, one, two, held):
+    blocks, rows, columns = grad.shape
+    step = 4
+    part = pl.BlockSpec((step, rows, columns), lambda b: (b + first // step, 0, 0))
+    anywhere = pl.BlockSpec(memory_space=pl.ANY)
+    shape = jax.ShapeDtypeStruct(param.shape, F32)
+    return pl.pallas_call(
+        adam_kernel,
+        grid=(pl.cdiv(blocks, step),),
+        in_specs=[pl.BlockSpec((step, rows, columns), lambda b: (b, 0, 0)), part, part, part]
+        + [anywhere] * len(held),
+        out_specs=[part] * 3,
+        out_shape=[shape] * 3,
+        input_output_aliases={4 + i: i for i in range(len(held))},
+        compiler_params=params(),
+        cost_estimate=cost(blocks // 2),
+        name="adam",
+    )(grad, param, one, two, *held)
 
 
 def per_device(
@@ -535,39 +742,53 @@
 ):
     mp_index = lax.axis_index("mp")
     seq_len = cotangent.shape[0]
+    weight_rows = weights.shape[0]
     local_width = weights.shape[2]
     model_width = tokens.shape[1]
+    lines = lax.axis_size("dp") // 4
     x = lax.dynamic_slice_in_dim(tokens, mp_index * seq_len, seq_len, 0)
     used = lax.dynamic_slice_in_dim(lengths, mp_index, 1, 0)
     sine = relative_embedding(seq_len, model_width).astype(BF)
     shard = weights.transpose(1, 0, 2)
-    blocks = gather_matrices(shard.astype(BF))
+    shard_low = shard.astype(BF)
+    w_feed = gather_matrices(shard_low[5:13])
+    w = gather_stepwise(shard_low[0:5])
     heads_all = lax.all_gather(head_vecs, "mp", axis=1, tiled=True)
 
-    qc, qp, k, v, rel = project(x, blocks[0:4], heads_all[0:2], sine)
+    qc, qp, k, v, rel = project(x, w, heads_all[0:2], sine)
     probs, mixed = attend(used, qc, qp, k, v, rel)
     hb = heads_all[2:6].reshape(4, 1, model_width)
     unit, inv, low, active, slope, out, gh2, gffn, sums2 = feed(
-        mixed, blocks[4:5], x, norm_vecs, hb, blocks[5:9], blocks[9:13], cotangent
-    )
-    gwback = back_grad(gffn, active)
-    gwin, hsum, gh1, gwo, gmixed, sums1 = feed_back(
-        gffn, slope, low, blocks[9:13], blocks[5:9], gh2, unit, inv, norm_vecs, blocks[4:5], mixed
-    )
+        mixed, w, x, norm_vecs, hb, w_feed, cotangent
+    )
+    gw_back = back_grad(gffn, active, lines, weight_rows)
+    part_back = scatter_plane(gw_back)
+    gffn, _ = lax.optimization_barrier((gffn, gw_back))
+    gw_in, hsum, gh1, gmixed, sums1 = feed_back(
+        gffn, slope, low, w_feed, gh2, unit, inv, norm_vecs, w, mixed, lines, weight_rows
+    )
+    gw_in, part_back = lax.optimization_barrier((gw_in, part_back))
+    part_in = scatter_plane(gw_in)
     gq, gk, gv, grel, sums_q = attend_back(probs, gmixed, qc, qp, k, v, rel)
-    gproj, grad_tokens = project_back(x, gq, gk, gv, grel, sine.T, blocks[0:4], gh1)
-
-    weight_grad = scatter_matrices(
-        jnp.concatenate([gproj, gwo, gwin, gwback], axis=0)
-    ).astype(F32)
+    line_back = scatter_line(part_back)
+    gq, line_back = lax.optimization_barrier((gq, line_back))
+    gproj, grad_tokens = project_back(
+        x, gq, gk, gv, grel, sine.T, w, gh1, lines, weight_rows
+    )
+    gproj, part_in = lax.optimization_barrier((gproj, part_in))
+    part_proj = scatter_plane(gproj)
+
     norm_part = jnp.concatenate([sums1[0:2], sums2[0:2], sums1[2:3], sums2[2:3]], axis=0)
     head_part = jnp.concatenate([sums_q[0:2], hsum[:, 0]], axis=0)
-    norm_grad, head_total = lax.psum((norm_part, head_part), ("dp", "mp"))
-    head_grad = lax.dynamic_slice_in_dim(head_total, mp_index * local_width, local_width, 1)
-
-    new_big = adam_update(
-        shard, weight_grad, weight_m1.transpose(1, 0, 2), weight_m2.transpose(1, 0, 2), RATE_BIG
-    )
+    small = jnp.concatenate([norm_part, head_part], axis=0)
+    small = sum_small(small)
+    norm_grad = small[0:6]
+    head_grad = lax.dynamic_slice_in_dim(small[6:12], mp_index * local_width, local_width, 1)
+    state = (shard, weight_m1.transpose(1, 0, 2), weight_m2.transpose(1, 0, 2))
+    line_in = scatter_line(part_in)
+    early = jnp.concatenate([line_in[4:5], line_in[0:4], line_back], axis=0)
+    held = adam_blocks(early, 4, *state, ())
+    new_big = adam_blocks(scatter_line(part_proj), 0, *state, held)
     new_weights, new_weight_m1, new_weight_m2 = [a.transpose(1, 0, 2) for a in new_big]
     new_head, new_head_m1, new_head_m2 = adam_update(
         head_vecs, head_grad, head_m1, head_m2, RATE_SMALL

time: 436 us -> 293 us (0.67)
  waiting for transfers between devices: 217 us -> 90.8 us
  blocking collectives: 45.1 us -> 4.57 us
  starting transfers between devices: 0.08 us -> 37.3 us
  local copies, waits for them, and re-layouts: 28.1 us -> 11.1 us
  Pallas kernels: 108 us -> 120 us
  other arithmetic: 22.3 us -> 13.8 us
    reduce_scatter x1 -> x3, waiting for transfers between devices: 121 us -> 24.4 us  [scatter_plane(): lax.psum_scatter(grads, ('mp', 'dp'), scatter_dimension=0, axis_index_gro...]
    all_gather x1, waiting for transfers between devices: 95.6 us -> 0.01 us  [gather_matrices(): pieces = lax.all_gather(shard, ('mp', 'dp'), axis=0, tiled=False)]
    ppermute x0 -> x32, waiting for transfers between devices: none -> 66.4 us  [the longest x15 35.3 us: shift_line(): lax.ppermute(value, 'dp', [(d, (d + 4 * step) % dp) for d in range(dp)])]
    psum x1 -> x0, blocking collectives: 39.5 us -> none  [per_device(): norm_grad, head_total = lax.psum((norm_part, head_part), ('dp', 'mp'))]
    ppermute x0 -> x32, starting transfers between devices: none -> 36.9 us  [the longest x15 24.5 us: shift_line(): lax.ppermute(value, 'dp', [(d, (d + 4 * step) % dp) for d in range(dp)])]
    pallas_call x3 -> x6, Pallas kernels: 43 us -> 55.2 us  [the longest x1 16.9 us: feed_back(): pl.pallas_call(feed_back_kernel, grid=(blocks + 1,), in_specs=[one, pl.Bl...]
    transpose x1 -> x0, local copies, waits for them, and re-layouts: 6.58 us -> none  [scatter_matrices(): grads.reshape(blocks, mp, dp, all_rows // dp, columns)]
    reshape x1 -> x0, local copies, waits for them, and re-layouts: 6.4 us -> none  [gather_matrices(): pieces = pieces.reshape(mp, dp, blocks, rows, columns)]
  transfers between devices with their start and end apart: 2 -> 36, of which waited for: 2 -> 16; matrix products, arithmetic and copies ran while one was open for 4% -> 7% of each run, Pallas kernels for 0% -> 32%
where the time goes in v2:
time: 293 us; the launch traced here: 292 us
  Pallas kernels  120 us (41%)
  waiting for transfers between devices  90.8 us (31%)
  starting transfers between devices  37.3 us (13%)
  between operations  14.2 us (5%)
  other arithmetic  13.8 us (5%)
  local copies, waits for them, and re-layouts  11.1 us (4%)
  blocking collectives  4.57 us (2%)
    ppermute x15, waiting for transfers between devices, shift_line(): lax.ppermute(value, 'dp', [(d, (d + 4 * step) % dp) for d in range(dp)])  35.3 us
    pallas_call x1, Pallas kernels, attend_back(): pl.pallas_call(attend_back_kernel, grid=(heads // 2,), in_specs=[pl.Block...  27.9 us
    ppermute x15, starting transfers between devices, shift_line(): lax.ppermute(value, 'dp', [(d, (d + 4 * step) % dp) for d in range(dp)])  24.5 us
    reduce_scatter x3, waiting for transfers between devices, scatter_plane(): lax.psum_scatter(grads, ('mp', 'dp'), scatter_dimension=0, axis_index_gro...  24.4 us
    ppermute x4, waiting for transfers between devices, swap_x(): return lax.ppermute(value, 'mp', [(0, 1), (1, 0)])  18.9 us
    pallas_call x1, Pallas kernels, attend(): pl.pallas_call(attend_kernel, grid=(heads // 2,), in_specs=[pl.BlockSpec(...  18.7 us
    pallas_call x1, Pallas kernels, feed_back(): pl.pallas_call(feed_back_kernel, grid=(blocks + 1,), in_specs=[one, pl.Bl...  16.9 us
    pallas_call x1, Pallas kernels, feed(): pl.pallas_call(feed_kernel, grid=(blocks,), in_specs=[one, weight_spec(w....  16.6 us
  transfers between devices with their start and end apart: 36, of which 16 were waited for; matrix products, arithmetic and copies ran while one was open for 7% of the time, Pallas kernels for 32%

profile of v2, /device:TPU:0, one launch (start us, length us, event | category | flops | bytes accessed | tf_op | source)
XLA Modules:
  0.0 291.6 jit_solution(5789309834551052288)
XLA Ops:
  7.2 1.4 bitcast_convert_fusion
  9.5 4.1 %collective-permute-start.1 = (bf16[5,48,384]{2,1,0:T(8,128)(2,1)S(1)}, bf16[5,48,384]{2,1,0:T(8,128)(2,1)S(1)}, u32[]{:S(2)}, u32[]{:S(2)}) collective-permute-start(bf16[5,48,384]{2,1,0:T(8,128)(2,1)S(1)} %get-tuple-element.111), channel_id=1, source_target_pairs={{0,16},{2,18},{4,20},{6,22},{8,24},{10,26},{12,28},{14,30},{16,0},... | collective-permute-start | bytes 552968 | tf_op jit(solution)/shard_map/ppermute | solution.py:564
  13.6 1.6 collective-permute-start
  15.1 2.2 collective-permute-start.2
  17.4 11.1 %collective-permute-done.1 = bf16[5,48,384]{2,1,0:T(8,128)(2,1)S(1)} collective-permute-done((bf16[5,48,384]{2,1,0:T(8,128)(2,1)S(1)}, bf16[5,48,384]{2,1,0:T(8,128)(2,1)S(1)}, u32[]{:S(2)}, u32[]{:S(2)}) %collective-permute-start.1) | collective-permute-done | bytes 184352 | tf_op jit(solution)/shard_map/ppermute | solution.py:564
  28.5 1.6 collective-permute-done.2
  30.2 1.9 collective-permute-start.4
  32.5 1.8 collective-permute-start.3
  35.2 6.6 %collective-permute-done.4.refs_3_ = bf16[4,3,48,384]{3,2,1,0:T(8,128)(2,1)} collective-permute-done((bf16[4,3,48,384]{3,2,1,0:T(8,128)(2,1)S(1)}, bf16[4,3,48,384]{3,2,1,0:T(8,128)(2,1)}, u32[]{:S(2)}, u32[]{:S(2)}) %collective-permute-start.4) | collective-permute-done | bytes 442400 | tf_op jit(solution)/shard_map/ppermute | solution.py:559
  41.8 1.8 collective-permute-start.8
  43.6 1.3 collective-permute-done.5.refs_4_
  44.9 2.4 collective-permute-start.7
  47.3 6.0 %fusion = (bf16[1024,384]{0,1:T(8,128)(2,1)S(1)}, bf16[1024,384]{0,1:T(8,128)(2,1)S(1)}) fusion(f32[384]{0:T(512)S(1)} %negate_power_fusion, f32[1024]{0:T(1024)S(1)} %subtract_convert_fusion), kind=kLoop, calls=%fused_computation.2 | loop fusion | flops 1179648 | bytes 1578496 | tf_op jit(solution)/shard_map/convert.3
  53.6 4.7 %collective-permute-done.6.refs_5_ = bf16[4,3,48,384]{3,2,1,0:T(8,128)(2,1)} collective-permute-done((bf16[4,3,48,384]{3,2,1,0:T(8,128)(2,1)S(1)}, bf16[4,3,48,384]{3,2,1,0:T(8,128)(2,1)}, u32[]{:S(2)}, u32[]{:S(2)}) %collective-permute-start.6) | collective-permute-done | bytes 442400 | tf_op jit(solution)/shard_map/ppermute | solution.py:555
  58.9 10.2 %collective-permute-done.8.refs_7_ = bf16[4,3,48,384]{3,2,1,0:T(8,128)(2,1)} collective-permute-done((bf16[4,3,48,384]{3,2,1,0:T(8,128)(2,1)}, bf16[4,3,48,384]{3,2,1,0:T(8,128)(2,1)}, u32[]{:S(2)}, u32[]{:S(2)}) %collective-permute-start.8) | collective-permute-done | bytes 442400 | tf_op jit(solution)/shard_map/ppermute | solution.py:555
  69.2 1.6 fusion.10
  70.8 4.6 %all_gather.9 = f32[6,768]{1,0:T(8,128)S(1)} all-gather(f32[6,384]{1,0:T(8,128)S(1)} %copy-done.6), channel_id=1, replica_groups=mesh['dp'=16,'mp'=2] {'mp'}, dimensions={1}, use_global_device_ids=true | all-gather | bytes 27648 | tf_op jit(solution)/shard_map/all_gather | solution.py:756
  76.6 1.6 copy.27.sine_ref
  80.3 6.6 %place.1.w_ref.wo_ref = bf16[5,2,768,384]{3,2,1,0:T(8,128)(2,1)} custom-call(s32[4]{0:T(128)} %pad_add_fusion.place_ref, bf16[4,2,48,384]{3,2,1,0:T(8,128)(2,1)} %copy-done.5, bf16[4,3,48,384]{3,2,1,0:T(8,128)(2,1)} %copy-done.4, bf16[4,2,48,384]{3,2,1,0:T(8,128)(2,1)} %collective-permute-done.3.refs_2_, ...), custom_call_target="tpu_custom_call" | custom-call | flops 5000000000 | tf_op jit(solution)/shard_map/place/pallas_call | solution.py:633
  86.9 8.7 %project.1 = (bf16[512,768]{1,0:T(8,128)(2,1)}, bf16[512,768]{1,0:T(8,128)(2,1)}, bf16[512,768]{1,0:T(8,128)(2,1)}, bf16[512,768]{1,0:T(8,128)(2,1)}, bf16[1024,768]{1,0:T(8,128)(2,1)}) custom-call(bf16[512,768]{1,0:T(8,128)(2,1)} %constant_dynamic-slice_fusion.x_ref, bf16[5,2,768,384]{3,2,1,0:T(8,128)(2,1)} %place.1.w_ref.wo_ref, f32[2,768]{1,0:T(2,128)} %slice.61.vec_ref, ...), custom_call_target="tpu_custom_call" | custom-call | flops 8999999488 | tf_op jit(solution)/shard_map/project/pallas_call | solution.py:138
  95.6 18.7 %attend.1 = (bf16[12,512,512]{2,1,0:T(8,128)(2,1)}, bf16[512,768]{1,0:T(8,128)(2,1)}) custom-call(s32[1]{0:T(128)} %dynamic_slice.47.len_ref, bf16[512,768]{1,0:T(8,128)(2,1)} %get-tuple-element.52.qc_ref, bf16[512,768]{1,0:T(8,128)(2,1)} %get-tuple-element.53.qp_ref, bf16[512,768]{1,0:T(8,128)(2,1)} %get-tuple-element.54.k_ref, ...), custom_call_target="tpu_custom_call" | custom-call | flops 19000000512 | tf_op jit(solution)/shard_map/attend/pallas_call | solution.py:195
  114.4 16.6 %feed.1 = (f32[512,768]{1,0:T(8,128)}, f32[512,128]{1,0:T(8,128)}, bf16[512,768]{1,0:T(8,128)(2,1)}, bf16[4,512,768]{2,1,0:T(8,128)(2,1)}, bf16[4,512,768]{2,1,0...) custom-call(bf16[512,768]{1,0:T(8,128)(2,1)} %get-tuple-element.57.m, ...), custom_call_target="tpu_custom_call" | custom-call | flops 16999999488 | tf_op jit(solution)/shard_map/feed/pallas_call | solution.py:286
  131.0 6.7 %back_grad.1 = bf16[8,4,4,48,384]{4,3,2,1,0:T(8,128)(2,1)} custom-call(bf16[512,768]{1,0:T(8,128)(2,1)} %get-tuple-element.62.gffn_ref, bf16[4,512,768]{2,1,0:T(8,128)(2,1)} %get-tuple-element.61.act_ref), custom_call_target="tpu_custom_call" | custom-call | flops 7000000000 | tf_op jit(solution)/shard_map/back_grad/pallas_call | solution.py:325
  137.9 16.9 %feed_back.1 = (bf16[8,4,5,48,384]{4,3,2,1,0:T(8,128)(2,1)}, f32[4,1,768]{2,1,0:T(1,128)}, f32[512,768]{1,0:T(8,128)}, bf16[512,768]{1,0:T(8,128)(2,1)}, f32[8,768]{1,0:T(8,128)}) custom-call(bf16[512,768]{1,0:T(8,128)(2,1)} %get-tuple-element.62.gffn_ref, bf16[4,512,768]{2,1,0:T(8,128)(2,1)} %get-tuple-element.63.slope_ref, ...), custom_call_target="tpu_custom_call" | custom-call | flops 16999999488 | tf_op jit(solution)/shard_map/feed_back/pallas_call | solution.py:385
  154.9 24.4 %reduce-scatter.4.cloned.1.call-done = bf16[1,4,4,48,384]{4,3,2,1,0:T(8,128)(2,1)} async-done(((bf16[8,4,4,48,384]{4,3,2,1,0:T(8,128)(2,1)}), bf16[1,4,4,48,384]{4,3,2,1,0:T(8,128)(2,1)}) %reduce-scatter.4.cloned.1.call-update) | async-done | bytes 589840 | tf_op jit(solution)/shard_map/reduce_scatter | solution.py:664
  180.3 1.5 collective-permute-start.17
  181.9 2.4 collective-permute-start.19
  184.8 27.9 %attend_back.1 = (bf16[512,768]{1,0:T(8,128)(2,1)}, bf16[512,768]{1,0:T(8,128)(2,1)}, bf16[512,768]{1,0:T(8,128)(2,1)}, bf16[1024,768]{1,0:T(8,128)(2,1)}, f32[8,768]{1,0:T(8,128)}) custom-call(bf16[12,512,512]{2,1,0:T(8,128)(2,1)} %get-tuple-element.59.probs_ref, bf16[512,768]{1,0:T(8,128)(2,1)} %get-tuple-element.68.gm_ref, ...), custom_call_target="tpu_custom_call" | custom-call | flops 28000000000 | tf_op jit(solution)/shard_map/attend_back/pallas_call | solution.py:492
  212.8 11.4 %project_back.1 = (bf16[8,4,4,48,384]{4,3,2,1,0:T(8,128)(2,1)}, f32[512,768]{1,0:T(8,128)}) custom-call(bf16[512,768]{1,0:T(8,128)(2,1)} %constant_dynamic-slice_fusion.x_ref, bf16[512,768]{1,0:T(8,128)(2,1)} %get-tuple-element.72.gq_ref, bf16[512,768]{1,0:T(8,128)(2,1)} %get-tuple-element.73.gk_ref, bf16[512,768]{1,0:T(8,128)(2,1)} %get-tuple-element.74.gv_ref, ...), custom_call_target="tpu_custom_call" | custom-call | flops 11000000512 | tf_op jit(solution)/shard_map/project_back/pallas_call | solution.py:537
  228.2 1.2 collective-permute-done.26
  230.1 4.0 %collective-permute-done.27 = f32[12,768]{1,0:T(8,128)S(1)} collective-permute-done((f32[12,768]{1,0:T(8,128)S(1)}, f32[12,768]{1,0:T(8,128)S(1)}, u32[]{:S(2)}, u32[]{:S(2)}) %collective-permute-start.27) | collective-permute-done | bytes 36896 | tf_op jit(solution)/shard_map/ppermute | solution.py:555
  234.0 1.7 collective-permute-start.28
  235.7 3.1 %collective-permute-done.28 = f32[12,768]{1,0:T(8,128)S(1)} collective-permute-done((f32[12,768]{1,0:T(8,128)S(1)}, f32[12,768]{1,0:T(8,128)S(1)}, u32[]{:S(2)}, u32[]{:S(2)}) %collective-permute-start.28) | collective-permute-done | bytes 36896 | tf_op jit(solution)/shard_map/ppermute | solution.py:559
  238.8 1.1 collective-permute-start.31
  239.9 1.9 collective-permute-start.30
  241.7 1.4 collective-permute-start.29
  243.2 2.0 collective-permute-done.30
  245.2 2.4 collective-permute-done.29
  248.5 3.8 %collective-permute-start.25 = (bf16[5,48,384]{2,1,0:T(8,128)(2,1)S(1)}, bf16[5,48,384]{2,1,0:T(8,128)(2,1)S(1)}, u32[]{:S(2)}, u32[]{:S(2)}) collective-permute-start(bf16[5,48,384]{2,1,0:T(8,128)(2,1)S(1)} %get-tuple-element.102), channel_id=1, source_target_pairs={{0,24},{2,26},{4,28},{6,30},{8,0},{10,2},{12,4},{14,6},{16,8},{18,... | collective-permute-start | bytes 552968 | tf_op jit(solution)/shard_map/ppermute | solution.py:564
  252.9 5.0 %collective-permute-done.23 = bf16[5,48,384]{2,1,0:T(8,128)(2,1)S(1)} collective-permute-done((bf16[5,48,384]{2,1,0:T(8,128)(2,1)S(1)}, bf16[5,48,384]{2,1,0:T(8,128)(2,1)S(1)}, u32[]{:S(2)}, u32[]{:S(2)}) %collective-permute-start.23) | collective-permute-done | bytes 184352 | tf_op jit(solution)/shard_map/ppermute | solution.py:564
  257.9 6.7 %collective-permute-done.24 = bf16[5,48,384]{2,1,0:T(8,128)(2,1)S(1)} collective-permute-done((bf16[5,48,384]{2,1,0:T(8,128)(2,1)S(1)}, bf16[5,48,384]{2,1,0:T(8,128)(2,1)S(1)}, u32[]{:S(2)}, u32[]{:S(2)}) %collective-permute-start.24) | collective-permute-done | bytes 184352 | tf_op jit(solution)/shard_map/ppermute | solution.py:564
  265.7 1.1 dynamic-slice_bitcast_fusion.5
  266.8 3.8 %collective-permute-start.22 = (bf16[4,48,384]{2,1,0:T(8,128)(2,1)S(1)}, bf16[4,48,384]{2,1,0:T(8,128)(2,1)S(1)}, u32[]{:S(2)}, u32[]{:S(2)}) collective-permute-start(bf16[4,48,384]{2,1,0:T(8,128)(2,1)S(1)} %get-tuple-element.105), channel_id=1, source_target_pairs={{0,24},{2,26},{4,28},{6,30},{8,0},{10,2},{12,4},{14,6},{16,8},{18,... | collective-permute-start | bytes 442376 | tf_op jit(solution)/shard_map/ppermute | solution.py:564
  270.6 3.9 %adam.2 = (f32[13,48,384]{2,1,0:T(8,128)}, f32[13,48,384]{2,1,0:T(8,128)}, f32[13,48,384]{2,1,0:T(8,128)}) custom-call(f32[9,48,384]{2,1,0:T(8,128)} %pad_maximum_fusion.1.g_ref, f32[13,48,384]{2,1,0:T(8,128)} %bitcast.51, f32[13,48,384]{2,1,0:T(8,128)} %bitcast.68, f32[13,48,384]{2,1,0:T(8,128)} %bitcast.70), custom_call_target="tpu_custom_call" | custom-call | flops 4000000000 | tf_op jit(solution)/shard_map/adam/pallas_call | solution.py:715
  274.5 1.0 collective-permute-done.20
  275.5 5.5 %collective-permute-done.21 = bf16[4,48,384]{2,1,0:T(8,128)(2,1)S(1)} collective-permute-done((bf16[4,48,384]{2,1,0:T(8,128)(2,1)S(1)}, bf16[4,48,384]{2,1,0:T(8,128)(2,1)S(1)}, u32[]{:S(2)}, u32[]{:S(2)}) %collective-permute-start.21) | collective-permute-done | bytes 147488 | tf_op jit(solution)/shard_map/ppermute | solution.py:564
  281.0 1.7 fusion.5.g_ref
  282.7 2.4 adam.3
  (113 shorter events, 15.6 us)
Async XLA Ops:
  7.2 72.1 %copy-start = (bf16[1024,768]{1,0:T(8,128)(2,1)S(1)}, bf16[1024,768]{1,0:T(8,128)(2,1)}, u32[]{:S(2)}) copy-start(bf16[1024,768]{1,0:T(8,128)(2,1)} %param.12) | copy-start | bytes 4718596
  7.2 107.2 %all-gather.3.cloned.1.call-start = ((), (), s32[]{:S(2)}) async-start(), calls=%async_computation.6 | async-start | bytes 9732096 | tf_op jit(solution)/shard_map/all_gather | solution.py:568
  9.4 169.9 %reduce-scatter.4.cloned.1.call-start = ((), (), s32[]{:S(2)}) async-start(), calls=%async_computation.3 | async-start | bytes 5308416 | tf_op jit(solution)/shard_map/reduce_scatter | solution.py:664
  9.5 19.1 %collective-permute-start.1 = (bf16[5,48,384]{2,1,0:T(8,128)(2,1)S(1)}, bf16[5,48,384]{2,1,0:T(8,128)(2,1)S(1)}, u32[]{:S(2)}, u32[]{:S(2)}) collective-permute-start(bf16[5,48,384]{2,1,0:T(8,128)(2,1)S(1)} %get-tuple-element.111), channel_id=1, source_target_pairs={{0,16},{2,18},{4,20},{6,22},{8,24},{10,26},{12,28},{14,30},{16,0},... | collective-permute-start | bytes 552968 | tf_op jit(solution)/shard_map/ppermute | solution.py:564
  13.6 15.0 %collective-permute-start = (bf16[5,48,384]{2,1,0:T(8,128)(2,1)S(1)}, bf16[5,48,384]{2,1,0:T(8,128)(2,1)S(1)}, u32[]{:S(2)}, u32[]{:S(2)}) collective-permute-start(bf16[5,48,384]{2,1,0:T(8,128)(2,1)S(1)} %get-tuple-element.111), channel_id=1, source_target_pairs={{0,8},{2,10},{4,12},{6,14},{8,16},{10,18},{12,20},{14,22},{16,24},... | collective-permute-start | bytes 552968 | tf_op jit(solution)/shard_map/ppermute | solution.py:564
  15.1 15.0 %collective-permute-start.2 = (bf16[5,48,384]{2,1,0:T(8,128)(2,1)S(1)}, bf16[5,48,384]{2,1,0:T(8,128)(2,1)S(1)}, u32[]{:S(2)}, u32[]{:S(2)}) collective-permute-start(bf16[5,48,384]{2,1,0:T(8,128)(2,1)S(1)} %get-tuple-element.111), channel_id=1, source_target_pairs={{0,24},{2,26},{4,28},{6,30},{8,0},{10,2},{12,4},{14,6},{16,8},{18,... | collective-permute-start | bytes 552968 | tf_op jit(solution)/shard_map/ppermute | solution.py:564
  30.2 39.0 %copy-start.4 = (bf16[4,3,48,384]{3,2,1,0:T(8,128)(2,1)}, bf16[4,3,48,384]{3,2,1,0:T(8,128)(2,1)S(1)}, u32[]{:S(2)}) copy-start(bf16[4,3,48,384]{3,2,1,0:T(8,128)(2,1)S(1)} %pad_maximum_fusion.2.refs_1_) | copy-start | bytes 1327108
  30.2 11.6 %collective-permute-start.4 = (bf16[4,3,48,384]{3,2,1,0:T(8,128)(2,1)S(1)}, bf16[4,3,48,384]{3,2,1,0:T(8,128)(2,1)}, u32[]{:S(2)}, u32[]{:S(2)}) collective-permute-start(bf16[4,3,48,384]{3,2,1,0:T(8,128)(2,1)S(1)} %pad_maximum_fusion.2.refs_1_), channel_id=1, source_target_pairs={{0,4},{2,6},{4,0},{6,2},{8,12},{10,14},{12,8},{14,10},{16,20},{18,... | collective-permute-start | bytes 1327112 | tf_op jit(solution)/shard_map/ppermute | solution.py:559
  32.1 38.6 %copy-start.5 = (bf16[4,2,48,384]{3,2,1,0:T(8,128)(2,1)}, bf16[4,2,48,384]{3,2,1,0:T(8,128)(2,1)S(1)}, u32[]{:S(2)}) copy-start(bf16[4,2,48,384]{3,2,1,0:T(8,128)(2,1)S(1)} %pad_maximum_fusion.5.refs_0_) | copy-start | bytes 884740
  32.1 2.1 collective-permute-start.9
  32.2 12.7 %collective-permute-start.5 = (bf16[4,2,48,384]{3,2,1,0:T(8,128)(2,1)S(1)}, bf16[4,2,48,384]{3,2,1,0:T(8,128)(2,1)S(1)}, u32[]{:S(2)}, u32[]{:S(2)}) collective-permute-start(bf16[4,2,48,384]{3,2,1,0:T(8,128)(2,1)S(1)} %pad_maximum_fusion.5.refs_0_), channel_id=1, source_target_pairs={{0,4},{2,6},{4,0},{6,2},{8,12},{10,14},{12,8},{14,10},{16,20},{18,... | collective-permute-start | bytes 884744 | tf_op jit(solution)/shard_map/ppermute | solution.py:559
  32.5 12.4 %collective-permute-start.3 = (bf16[4,2,48,384]{3,2,1,0:T(8,128)(2,1)S(1)}, bf16[4,2,48,384]{3,2,1,0:T(8,128)(2,1)}, u32[]{:S(2)}, u32[]{:S(2)}) collective-permute-start(bf16[4,2,48,384]{3,2,1,0:T(8,128)(2,1)S(1)} %pad_maximum_fusion.5.refs_0_), channel_id=1, source_target_pairs={{0,1},{1,0},{2,3},{3,2},{4,5},{5,4},{6,7},{7,6},{8,9},{9,8},{10,11... | collective-permute-start | bytes 884744 | tf_op jit(solution)/shard_map/ppermute | solution.py:555
  34.3 19.1 %collective-permute-start.10 = (bf16[4,3,48,384]{3,2,1,0:T(8,128)(2,1)S(1)}, bf16[4,3,48,384]{3,2,1,0:T(8,128)(2,1)S(1)}, u32[]{:S(2)}, u32[]{:S(2)}) collective-permute-start(bf16[4,3,48,384]{3,2,1,0:T(8,128)(2,1)S(1)} %pad_maximum_fusion.2.refs_1_), channel_id=1, source_target_pairs={{0,2},{2,0},{4,6},{6,4},{8,10},{10,8},{12,14},{14,12},{16,18},{18,... | collective-permute-start | bytes 1327112 | tf_op jit(solution)/shard_map/ppermute | solution.py:559
  34.3 34.8 %copy-start.14 = (bf16[4,2,48,384]{3,2,1,0:T(8,128)(2,1)}, bf16[4,2,48,384]{3,2,1,0:T(8,128)(2,1)S(1)}, u32[]{:S(2)}) copy-start(bf16[4,2,48,384]{3,2,1,0:T(8,128)(2,1)S(1)} %collective-permute-done.9.refs_8_) | copy-start | bytes 884740
  34.3 24.0 %collective-permute-start.6 = (bf16[4,3,48,384]{3,2,1,0:T(8,128)(2,1)S(1)}, bf16[4,3,48,384]{3,2,1,0:T(8,128)(2,1)}, u32[]{:S(2)}, u32[]{:S(2)}) collective-permute-start(bf16[4,3,48,384]{3,2,1,0:T(8,128)(2,1)S(1)} %pad_maximum_fusion.2.refs_1_), channel_id=1, source_target_pairs={{0,1},{1,0},{2,3},{3,2},{4,5},{5,4},{6,7},{7,6},{8,9},{9,8},{10,11... | collective-permute-start | bytes 1327112 | tf_op jit(solution)/shard_map/ppermute | solution.py:555
  41.8 27.3 %collective-permute-start.8 = (bf16[4,3,48,384]{3,2,1,0:T(8,128)(2,1)}, bf16[4,3,48,384]{3,2,1,0:T(8,128)(2,1)}, u32[]{:S(2)}, u32[]{:S(2)}) collective-permute-start(bf16[4,3,48,384]{3,2,1,0:T(8,128)(2,1)} %collective-permute-done.4.refs_3_), channel_id=1, source_target_pairs={{0,1},{1,0},{2,3},{3,2},{4,5},{5,4},{6,7},{7,6},{8,9},{9,8},{10,11... | collective-permute-start | bytes 1327112 | tf_op jit(solution)/shard_map/ppermute | solution.py:555
  44.9 24.3 %copy-start.15 = (bf16[4,2,48,384]{3,2,1,0:T(8,128)(2,1)}, bf16[4,2,48,384]{3,2,1,0:T(8,128)(2,1)S(1)}, u32[]{:S(2)}) copy-start(bf16[4,2,48,384]{3,2,1,0:T(8,128)(2,1)S(1)} %collective-permute-done.5.refs_4_) | copy-start | bytes 884740
  44.9 13.4 %collective-permute-start.13 = (bf16[4,2,48,384]{3,2,1,0:T(8,128)(2,1)S(1)}, bf16[4,2,48,384]{3,2,1,0:T(8,128)(2,1)S(1)}, u32[]{:S(2)}, u32[]{:S(2)}) collective-permute-start(bf16[4,2,48,384]{3,2,1,0:T(8,128)(2,1)S(1)} %collective-permute-done.5.refs_4_), channel_id=1, source_target_pairs={{0,2},{2,0},{4,6},{6,4},{8,10},{10,8},{12,14},{14,12},{16,18},{18,... | collective-permute-start | bytes 884744 | tf_op jit(solution)/shard_map/ppermute | solution.py:559
  44.9 13.9 %collective-permute-start.7 = (bf16[4,2,48,384]{3,2,1,0:T(8,128)(2,1)}, bf16[4,2,48,384]{3,2,1,0:T(8,128)(2,1)}, u32[]{:S(2)}, u32[]{:S(2)}) collective-permute-start(bf16[4,2,48,384]{3,2,1,0:T(8,128)(2,1)} %collective-permute-done.3.refs_2_), channel_id=1, source_target_pairs={{0,4},{2,6},{4,0},{6,2},{8,12},{10,14},{12,8},{14,10},{16,20},{18,... | collective-permute-start | bytes 884744 | tf_op jit(solution)/shard_map/ppermute | solution.py:559
  53.4 15.8 %copy-start.13 = (bf16[4,3,48,384]{3,2,1,0:T(8,128)(2,1)}, bf16[4,3,48,384]{3,2,1,0:T(8,128)(2,1)S(1)}, u32[]{:S(2)}) copy-start(bf16[4,3,48,384]{3,2,1,0:T(8,128)(2,1)S(1)} %collective-permute-done.10.refs_9_) | copy-start | bytes 1327108
  53.4 26.9 %collective-permute-start.11 = (bf16[4,2,48,384]{3,2,1,0:T(8,128)(2,1)}, bf16[4,2,48,384]{3,2,1,0:T(8,128)(2,1)}, u32[]{:S(2)}, u32[]{:S(2)}) collective-permute-start(bf16[4,2,48,384]{3,2,1,0:T(8,128)(2,1)} %collective-permute-done.3.refs_2_), channel_id=1, source_target_pairs={{0,2},{2,0},{4,6},{6,4},{8,10},{10,8},{12,14},{14,12},{16,18},{18,... | collective-permute-start | bytes 884744 | tf_op jit(solution)/shard_map/ppermute | solution.py:559
  58.3 22.0 %collective-permute-start.12 = (bf16[4,3,48,384]{3,2,1,0:T(8,128)(2,1)}, bf16[4,3,48,384]{3,2,1,0:T(8,128)(2,1)}, u32[]{:S(2)}, u32[]{:S(2)}) collective-permute-start(bf16[4,3,48,384]{3,2,1,0:T(8,128)(2,1)} %collective-permute-done.4.refs_3_), channel_id=1, source_target_pairs={{0,2},{2,0},{4,6},{6,4},{8,10},{10,8},{12,14},{14,12},{16,18},{18,... | collective-permute-start | bytes 1327112 | tf_op jit(solution)/shard_map/ppermute | solution.py:559
  58.3 21.9 %collective-permute-start.14 = (bf16[4,3,48,384]{3,2,1,0:T(8,128)(2,1)}, bf16[4,3,48,384]{3,2,1,0:T(8,128)(2,1)}, u32[]{:S(2)}, u32[]{:S(2)}) collective-permute-start(bf16[4,3,48,384]{3,2,1,0:T(8,128)(2,1)} %collective-permute-done.6.refs_5_), channel_id=1, source_target_pairs={{0,2},{2,0},{4,6},{6,4},{8,10},{10,8},{12,14},{14,12},{16,18},{18,... | collective-permute-start | bytes 1327112 | tf_op jit(solution)/shard_map/ppermute | solution.py:559
  58.8 21.4 %collective-permute-start.15 = (bf16[4,2,48,384]{3,2,1,0:T(8,128)(2,1)}, bf16[4,2,48,384]{3,2,1,0:T(8,128)(2,1)}, u32[]{:S(2)}, u32[]{:S(2)}) collective-permute-start(bf16[4,2,48,384]{3,2,1,0:T(8,128)(2,1)} %collective-permute-done.7.refs_6_), channel_id=1, source_target_pairs={{0,2},{2,0},{4,6},{6,4},{8,10},{10,8},{12,14},{14,12},{16,18},{18,... | collective-permute-start | bytes 884744 | tf_op jit(solution)/shard_map/ppermute | solution.py:559
  69.1 11.1 %collective-permute-start.16 = (bf16[4,3,48,384]{3,2,1,0:T(8,128)(2,1)}, bf16[4,3,48,384]{3,2,1,0:T(8,128)(2,1)}, u32[]{:S(2)}, u32[]{:S(2)}) collective-permute-start(bf16[4,3,48,384]{3,2,1,0:T(8,128)(2,1)} %collective-permute-done.8.refs_7_), channel_id=1, source_target_pairs={{0,2},{2,0},{4,6},{6,4},{8,10},{10,8},{12,14},{14,12},{16,18},{18,... | collective-permute-start | bytes 1327112 | tf_op jit(solution)/shard_map/ppermute | solution.py:559
  137.7 86.5 %reduce-scatter.6.cloned.1.call-start = ((), (), s32[]{:S(2)}) async-start(), calls=%async_computation.4 | async-start | bytes 6635520 | tf_op jit(solution)/shard_map/reduce_scatter | solution.py:664
  179.3 86.4 %reduce-scatter.8.cloned.1.call-start = ((), (), s32[]{:S(2)}) async-start(), calls=%async_computation.5 | async-start | bytes 5308416 | tf_op jit(solution)/shard_map/reduce_scatter | solution.py:664
  180.3 32.4 %collective-permute-start.17 = (bf16[4,48,384]{2,1,0:T(8,128)(2,1)S(1)}, bf16[4,48,384]{2,1,0:T(8,128)(2,1)S(1)}, u32[]{:S(2)}, u32[]{:S(2)}) collective-permute-start(bf16[4,48,384]{2,1,0:T(8,128)(2,1)S(1)} %get-tuple-element.107), channel_id=1, source_target_pairs={{0,8},{2,10},{4,12},{6,14},{8,16},{10,18},{12,20},{14,22},{16,24},... | collective-permute-start | bytes 442376 | tf_op jit(solution)/shard_map/ppermute | solution.py:564
  181.9 30.9 %collective-permute-start.19 = (bf16[4,48,384]{2,1,0:T(8,128)(2,1)S(1)}, bf16[4,48,384]{2,1,0:T(8,128)(2,1)S(1)}, u32[]{:S(2)}, u32[]{:S(2)}) collective-permute-start(bf16[4,48,384]{2,1,0:T(8,128)(2,1)S(1)} %get-tuple-element.108), channel_id=1, source_target_pairs={{0,24},{2,26},{4,28},{6,30},{8,0},{10,2},{12,4},{14,6},{16,8},{18,... | collective-permute-start | bytes 442376 | tf_op jit(solution)/shard_map/ppermute | solution.py:564
  184.2 28.5 %collective-permute-start.18 = (bf16[4,48,384]{2,1,0:T(8,128)(2,1)S(1)}, bf16[4,48,384]{2,1,0:T(8,128)(2,1)S(1)}, u32[]{:S(2)}, u32[]{:S(2)}) collective-permute-start(bf16[4,48,384]{2,1,0:T(8,128)(2,1)S(1)} %get-tuple-element.109), channel_id=1, source_target_pairs={{0,16},{2,18},{4,20},{6,22},{8,24},{10,26},{12,28},{14,30},{16,0},... | collective-permute-start | bytes 442376 | tf_op jit(solution)/shard_map/ppermute | solution.py:564
  224.2 23.4 %copy-start.7 = (f32[6,768]{1,0:T(8,128)S(1)}, f32[6,768]{1,0:T(8,128)}, u32[]{:S(2)}) copy-start(f32[6,768]{1,0:T(8,128)} %nv_ref.3) | copy-start | bytes 55300
  224.2 23.4 %copy-start.8 = (f32[6,768]{1,0:T(8,128)S(1)}, f32[6,768]{1,0:T(8,128)}, u32[]{:S(2)}) copy-start(f32[6,768]{1,0:T(8,128)} %param.21) | copy-start | bytes 55300
  224.2 23.4 %copy-start.9 = (f32[6,768]{1,0:T(8,128)S(1)}, f32[6,768]{1,0:T(8,128)}, u32[]{:S(2)}) copy-start(f32[6,768]{1,0:T(8,128)} %param.22) | copy-start | bytes 55300
  224.2 24.1 %copy-start.2 = (bf16[1,4,5,48,384]{4,3,2,1,0:T(8,128)(2,1)S(1)}, bf16[1,4,5,48,384]{4,3,2,1,0:T(8,128)(2,1)}, u32[]{:S(2)}) copy-start(bf16[1,4,5,48,384]{4,3,2,1,0:T(8,128)(2,1)} %reduce-scatter.6.cloned.1.call-done) | copy-start | bytes 2211844
  224.3 28.0 %copy-start.11 = (f32[6,384]{1,0:T(8,128)S(1)}, f32[6,384]{1,0:T(8,128)}, u32[]{:S(2)}) copy-start(f32[6,384]{1,0:T(8,128)} %param.18) | copy-start | bytes 27652
  224.3 28.0 %copy-start.12 = (f32[6,384]{1,0:T(8,128)S(1)}, f32[6,384]{1,0:T(8,128)}, u32[]{:S(2)}) copy-start(f32[6,384]{1,0:T(8,128)} %param.19) | copy-start | bytes 27652
  228.1 1.3 collective-permute-start.26
  229.4 4.6 %collective-permute-start.27 = (f32[12,768]{1,0:T(8,128)S(1)}, f32[12,768]{1,0:T(8,128)S(1)}, u32[]{:S(2)}, u32[]{:S(2)}) collective-permute-start(f32[12,768]{1,0:T(8,128)S(1)} %add.180), channel_id=1, source_target_pairs={{0,1},{1,0},{2,3},{3,2},{4,5},{5,4},{6,7},{7,6},{8,9},{9,8},{10,11... | collective-permute-start | bytes 110600 | tf_op jit(solution)/shard_map/ppermute | solution.py:555
  234.0 4.8 %collective-permute-start.28 = (f32[12,768]{1,0:T(8,128)S(1)}, f32[12,768]{1,0:T(8,128)S(1)}, u32[]{:S(2)}, u32[]{:S(2)}) collective-permute-start(f32[12,768]{1,0:T(8,128)S(1)} %add.181), channel_id=1, source_target_pairs={{0,4},{2,6},{4,0},{6,2},{8,12},{10,14},{12,8},{14,10},{16,20},{18,... | collective-permute-start | bytes 110600 | tf_op jit(solution)/shard_map/ppermute | solution.py:559
  238.8 4.4 %collective-permute-start.31 = (f32[12,768]{1,0:T(8,128)S(1)}, f32[12,768]{1,0:T(8,128)S(1)}, u32[]{:S(2)}, u32[]{:S(2)}) collective-permute-start(f32[12,768]{1,0:T(8,128)S(1)} %add.182), channel_id=1, source_target_pairs={{0,24},{2,26},{4,28},{6,30},{8,0},{10,2},{12,4},{14,6},{16,8},{18,... | collective-permute-start | bytes 110600 | tf_op jit(solution)/shard_map/ppermute | solution.py:564
  239.9 5.3 %collective-permute-start.30 = (f32[12,768]{1,0:T(8,128)S(1)}, f32[12,768]{1,0:T(8,128)S(1)}, u32[]{:S(2)}, u32[]{:S(2)}) collective-permute-start(f32[12,768]{1,0:T(8,128)S(1)} %add.182), channel_id=1, source_target_pairs={{0,16},{2,18},{4,20},{6,22},{8,24},{10,26},{12,28},{14,30},{16,0},... | collective-permute-start | bytes 110600 | tf_op jit(solution)/shard_map/ppermute | solution.py:564
  241.7 5.9 %collective-permute-start.29 = (f32[12,768]{1,0:T(8,128)S(1)}, f32[12,768]{1,0:T(8,128)S(1)}, u32[]{:S(2)}, u32[]{:S(2)}) collective-permute-start(f32[12,768]{1,0:T(8,128)S(1)} %add.182), channel_id=1, source_target_pairs={{0,8},{2,10},{4,12},{6,14},{8,16},{10,18},{12,20},{14,22},{16,24},... | collective-permute-start | bytes 110600 | tf_op jit(solution)/shard_map/ppermute | solution.py:564
  248.4 9.5 %collective-permute-start.23 = (bf16[5,48,384]{2,1,0:T(8,128)(2,1)S(1)}, bf16[5,48,384]{2,1,0:T(8,128)(2,1)S(1)}, u32[]{:S(2)}, u32[]{:S(2)}) collective-permute-start(bf16[5,48,384]{2,1,0:T(8,128)(2,1)S(1)} %get-tuple-element.101), channel_id=1, source_target_pairs={{0,8},{2,10},{4,12},{6,14},{8,16},{10,18},{12,20},{14,22},{16,24},... | collective-permute-start | bytes 552968 | tf_op jit(solution)/shard_map/ppermute | solution.py:564
  248.5 9.5 %collective-permute-start.25 = (bf16[5,48,384]{2,1,0:T(8,128)(2,1)S(1)}, bf16[5,48,384]{2,1,0:T(8,128)(2,1)S(1)}, u32[]{:S(2)}, u32[]{:S(2)}) collective-permute-start(bf16[5,48,384]{2,1,0:T(8,128)(2,1)S(1)} %get-tuple-element.102), channel_id=1, source_target_pairs={{0,24},{2,26},{4,28},{6,30},{8,0},{10,2},{12,4},{14,6},{16,8},{18,... | collective-permute-start | bytes 552968 | tf_op jit(solution)/shard_map/ppermute | solution.py:564
  252.3 12.3 %collective-permute-start.24 = (bf16[5,48,384]{2,1,0:T(8,128)(2,1)S(1)}, bf16[5,48,384]{2,1,0:T(8,128)(2,1)S(1)}, u32[]{:S(2)}, u32[]{:S(2)}) collective-permute-start(bf16[5,48,384]{2,1,0:T(8,128)(2,1)S(1)} %get-tuple-element.103), channel_id=1, source_target_pairs={{0,16},{2,18},{4,20},{6,22},{8,24},{10,26},{12,28},{14,30},{16,0},... | collective-permute-start | bytes 552968 | tf_op jit(solution)/shard_map/ppermute | solution.py:564
  266.8 8.7 %collective-permute-start.20 = (bf16[4,48,384]{2,1,0:T(8,128)(2,1)S(1)}, bf16[4,48,384]{2,1,0:T(8,128)(2,1)S(1)}, u32[]{:S(2)}, u32[]{:S(2)}) collective-permute-start(bf16[4,48,384]{2,1,0:T(8,128)(2,1)S(1)} %get-tuple-element.104), channel_id=1, source_target_pairs={{0,8},{2,10},{4,12},{6,14},{8,16},{10,18},{12,20},{14,22},{16,24},... | collective-permute-start | bytes 442376 | tf_op jit(solution)/shard_map/ppermute | solution.py:564
  266.8 8.7 %collective-permute-start.22 = (bf16[4,48,384]{2,1,0:T(8,128)(2,1)S(1)}, bf16[4,48,384]{2,1,0:T(8,128)(2,1)S(1)}, u32[]{:S(2)}, u32[]{:S(2)}) collective-permute-start(bf16[4,48,384]{2,1,0:T(8,128)(2,1)S(1)} %get-tuple-element.105), channel_id=1, source_target_pairs={{0,24},{2,26},{4,28},{6,30},{8,0},{10,2},{12,4},{14,6},{16,8},{18,... | collective-permute-start | bytes 442376 | tf_op jit(solution)/shard_map/ppermute | solution.py:564
  270.6 10.3 %collective-permute-start.21 = (bf16[4,48,384]{2,1,0:T(8,128)(2,1)S(1)}, bf16[4,48,384]{2,1,0:T(8,128)(2,1)S(1)}, u32[]{:S(2)}, u32[]{:S(2)}) collective-permute-start(bf16[4,48,384]{2,1,0:T(8,128)(2,1)S(1)} %get-tuple-element.106), channel_id=1, source_target_pairs={{0,16},{2,18},{4,20},{6,22},{8,24},{10,26},{12,28},{14,30},{16,0},... | collective-permute-start | bytes 442376 | tf_op jit(solution)/shard_map/ppermute | solution.py:564
  (6 other events, 21.4 us)
Sparse Core Ops, SparseCore 0:
  10.9 97.3 all-gather.2
  137.8 41.4 reduce-scatter.3
  181.5 37.4 reduce-scatter.5
  224.4 34.7 reduce-scatter.7

commit v3 on v2

--- a/solution.py
+++ b/solution.py
@@ -19,9 +19,9 @@
 MASKED = -1e30
 SCALE = HEAD_FEATURES ** (-0.5)
 ROW_BLOCK = 256
+VMEM_MB = 56
 BF = jnp.bfloat16
 F32 = jnp.float32
-VMEM_LIMIT = 56 * 1024 * 1024
 
 NN = (((1,), (0,)), ((), ()))
 NT = (((1,), (1,)), ((), ()))
@@ -36,8 +36,12 @@
     return pl.BlockSpec(shape, lambda *_: (0,) * len(shape))
 
 
-def params():
-    return pltpu.CompilerParams(vmem_limit_bytes=VMEM_LIMIT)
+def held(shape):
+    return pl.BlockSpec(shape, lambda *_: (0,) * len(shape), pipeline_mode=pl.Buffered(1))
+
+
+def params(mebibytes):
+    return pltpu.CompilerParams(vmem_limit_bytes=mebibytes * 1024 * 1024)
 
 
 def cost(micros):
@@ -64,16 +68,29 @@
 
 
 def weight_spec(shape, which):
-    if len(shape) == 5:
-        return pl.BlockSpec(shape[:2] + (None,) + shape[3:], lambda b: (0, 0, which(b), 0, 0))
+    if shape[1] != 2:
+        return pl.BlockSpec((shape[0], None) + shape[2:], lambda b: (0, which(b), 0, 0))
     return pl.BlockSpec((None,) + shape[1:], lambda b: (which(b), 0, 0, 0))
 
 
+def ring_order(lines):
+    order = []
+    for turn, (mp, y) in enumerate(((0, 0), (0, 1), (1, 1), (1, 0))):
+        for line in range(lines) if turn % 2 == 0 else reversed(range(lines)):
+            order += [(mp, line * 4 + y * 2), (mp, line * 4 + y * 2 + 1)]
+    return order
+
+
 def full_matrix(w_ref):
-    w = w_ref[...]
-    if w.ndim == 4:
-        w = w.reshape(w.shape[0], w.shape[1] * w.shape[2], w.shape[3])
-    return jnp.concatenate([w[0], w[1]], axis=1)
+    if len(w_ref.shape) == 3 and w_ref.shape[0] > 2:
+        places = w_ref.shape[0]
+        order = ring_order(places // 8)
+        sides = [
+            jnp.concatenate([w_ref[order.index((mp, dp))] for dp in range(places // 2)], axis=0)
+            for mp in range(2)
+        ]
+        return jnp.concatenate(sides, axis=1)
+    return jnp.concatenate([w_ref[0], w_ref[1]], axis=1)
 
 
 RING = ((0, 0, 0), (0, 0, 1), (0, 1, 1), (0, 1, 0), (1, 1, 0), (1, 1, 1), (1, 0, 1), (1, 0, 0))
@@ -146,7 +163,7 @@
         ],
         out_specs=[whole(s) for s in shapes],
         out_shape=[jax.ShapeDtypeStruct(s, BF) for s in shapes],
-        compiler_params=params(),
+        compiler_params=params(VMEM_MB),
         cost_estimate=cost(9),
         name="project",
     )(x, w, vecs, sine)
@@ -203,7 +220,7 @@
             jax.ShapeDtypeStruct((heads, length, length), BF),
             jax.ShapeDtypeStruct((length, width), BF),
         ],
-        compiler_params=params(),
+        compiler_params=params(VMEM_MB),
         cost_estimate=cost(19),
         name="attend",
     )(length_used, qc, qp, k, v, rel)
@@ -225,191 +242,162 @@
     ) * inverse
 
 
-def feed_kernel(
+def mlp_kernel(
     mixed_ref, wo_ref, x_ref, nv_ref, hb_ref, win_ref, wback_ref, cot_ref,
-    unit_ref, inv_ref, low_ref, act_ref, slope_ref, out_ref, gh2_ref, gffn_ref, sums_ref,
-    first_ref, acc_ref,
+    out_ref, unit_ref, inv_ref, gfirst_ref, gw_ref, hsum_ref, sums_ref,
+    wide_ref, first_ref, low_ref, turned_ref, act_ref, slope_ref, gffn_ref, gturned_ref, ghid_ref,
 ):
     step = pl.program_id(0)
-    last = pl.num_programs(0) - 1
+    blocks = pl.num_programs(0) // 2
+    length = x_ref.shape[0]
 
     @pl.when(step == 0)
     def _():
-        attn = mm(mixed_ref[...], full_matrix(wo_ref), NT)
-        h1 = x_ref[...].astype(F32) + attn + nv_ref[4:5]
-        unit, inverse = norm_parts(h1)
-        unit_ref[...] = unit
-        inv_ref[...] = jnp.broadcast_to(inverse, inv_ref.shape)
-        first = unit * nv_ref[0:1] + nv_ref[1:2]
-        first_ref[...] = first
-        low_ref[...] = first.astype(BF)
-
-    hidden = mm(low_ref[...], full_matrix(win_ref)) + hb_ref[0]
-    bell = 0.5 * (1.0 + lax.erf(hidden * 0.7071067811865476))
-    active = (hidden * bell).astype(BF)
-    act_ref[...] = active
-    slope_ref[...] = (
-        bell + hidden * (jnp.exp(hidden * hidden * -0.5) * 0.3989422804014327)
-    ).astype(BF)
-    part = mm(active, full_matrix(wback_ref), NT)
-
-    @pl.when(step == 0)
-    def _():
-        acc_ref[...] = part
-
-    @pl.when(step > 0)
-    def _():
-        acc_ref[...] += part
-
-    @pl.when(step == last)
-    def _():
-        h2 = first_ref[...] + acc_ref[...] + nv_ref[5:6]
-        unit, inverse = norm_parts(h2)
-        out_ref[...] = (unit * nv_ref[2:3] + nv_ref[3:4]).astype(BF)
-        cot = cot_ref[...].astype(F32)
-        gh2 = norm_back(unit, inverse, cot * nv_ref[2:3])
-        gh2_ref[...] = gh2
-        gffn_ref[...] = gh2.astype(BF)
-        sums_ref[0:1] = jnp.sum(cot * unit, axis=0, keepdims=True)
-        sums_ref[1:2] = jnp.sum(cot, axis=0, keepdims=True)
-        sums_ref[2:3] = jnp.sum(gh2, axis=0, keepdims=True)
+        wide_ref[...] = mm(mixed_ref[...], full_matrix(wo_ref), NT)
+
+        def rows_in(rows):
+            h1 = x_ref[rows, :].astype(F32) + wide_ref[rows, :] + nv_ref[4:5]
+            unit, inverse = norm_parts(h1)
+            unit_ref[rows, :] = unit
+            inv_ref[rows, :] = jnp.broadcast_to(inverse, (unit.shape[0], inv_ref.shape[1]))
+            first = unit * nv_ref[0:1] + nv_ref[1:2]
+            first_ref[rows, :] = first + nv_ref[5:6]
+            low_ref[rows, :] = first.astype(BF)
+
+        rows_in(slice(None))
+        turned_ref[...] = low_ref[...].T
+
+    @pl.when(step < blocks)
+    def _():
+        wide_ref[...] = mm(low_ref[...], full_matrix(win_ref))
+
+        def rows_gelu(rows):
+            hidden = wide_ref[rows, :] + hb_ref[0]
+            bell = 0.5 * (1.0 + lax.erf(hidden * 0.7071067811865476))
+            act_ref[step, rows, :] = (hidden * bell).astype(BF)
+            slope_ref[step, rows, :] = (
+                bell + hidden * (jnp.exp(hidden * hidden * -0.5) * 0.3989422804014327)
+            ).astype(BF)
+
+        rows_gelu(slice(None))
+        first_ref[...] += mm(act_ref[step], full_matrix(wback_ref), NT)
+
+    @pl.when(step == blocks - 1)
+    def _():
+        def rows_out(rows):
+            unit, inverse = norm_parts(first_ref[rows, :])
+            out_ref[rows, :] = (unit * nv_ref[2:3] + nv_ref[3:4]).astype(BF)
+            cot = cot_ref[rows, :].astype(F32)
+            gh2 = norm_back(unit, inverse, cot * nv_ref[2:3])
+            gfirst_ref[rows, :] = gh2
+            gffn_ref[rows, :] = gh2.astype(BF)
+            wide_ref[rows, :] = cot * unit
+
+        rows_out(slice(None))
+        gturned_ref[...] = gffn_ref[...].T
+        sums_ref[0:1] = jnp.sum(wide_ref[...], axis=0, keepdims=True)
+        sums_ref[1:2] = jnp.sum(cot_ref[...].astype(F32), axis=0, keepdims=True)
+        sums_ref[2:3] = jnp.sum(gfirst_ref[...], axis=0, keepdims=True)
         sums_ref[3:8] = jnp.zeros((5, sums_ref.shape[1]), F32)
 
-
-def feed(mixed, w, x, nv, hb, w_feed, cot):
+    @pl.when(step >= blocks)
+    def _():
+        block = step - blocks
+        pick = lambda i: gw_ref.at[:, :, i] if len(gw_ref.shape) == 5 else gw_ref.at[i]
+        store_matrix(pick(1), mm(gturned_ref[...], act_ref[block]))
+        wide_ref[...] = mm(gffn_ref[...], full_matrix(wback_ref))
+
+        def rows_slope(rows):
+            ghid_ref[rows, :] = (wide_ref[rows, :] * slope_ref[block, rows, :].astype(F32)).astype(BF)
+
+        rows_slope(slice(None))
+        hsum_ref[0] = jnp.sum(ghid_ref[...].astype(F32), axis=0, keepdims=True)
+        store_matrix(pick(0), mm(turned_ref[...], ghid_ref[...]))
+        gfirst_ref[...] += mm(ghid_ref[...], full_matrix(win_ref), NT)
+
+
+def mlp(mixed, w_feed, x, nv, hb, cot, lines, rows):
     length, width = x.shape
     blocks = hb.shape[0]
     one = whole((length, width))
-    column = pl.BlockSpec((None, length, width), lambda b: (b, 0, 0))
     token = lambda d: jax.ShapeDtypeStruct((length, width), d)
-    hidden = jax.ShapeDtypeStruct((blocks, length, width), BF)
+    full = grad_shape(2 * blocks, lines, rows, width // 2)
+    if len(full) == 5:
+        spec = pl.BlockSpec(
+            full[:2] + (2,) + full[3:], lambda b: (0, 0, jnp.maximum(b - blocks, 0), 0, 0)
+        )
+    else:
+        spec = pl.BlockSpec((2,) + full[1:], lambda b: (jnp.maximum(b - blocks, 0), 0, 0, 0))
+    buffer = lambda d: pltpu.VMEM((length, width), d)
     return pl.pallas_call(
-        feed_kernel,
-        grid=(blocks,),
+        mlp_kernel,
+        grid=(2 * blocks,),
         in_specs=[
-            one,
-            weight_spec(w.shape, lambda b: 4),
-            one,
+            held((length, width)),
+            weight_spec(w_feed.shape, lambda b: 0),
+            held((length, width)),
             whole(nv.shape),
-            pl.BlockSpec((1, 1, width), lambda b: (b, 0, 0)),
-            weight_spec(w_feed.shape, lambda b: b),
-            weight_spec(w_feed.shape, lambda b: b + blocks),
-            one,
+            pl.BlockSpec((1, 1, width), lambda b: (jnp.minimum(b, blocks - 1), 0, 0)),
+            weight_spec(w_feed.shape, lambda b: 1 + lax.rem(b, blocks)),
+            weight_spec(w_feed.shape, lambda b: 1 + blocks + lax.rem(b, blocks)),
+            held((length, width)),
         ],
         out_specs=[
-            one, whole((length, 128)), one, column, column, one, one, one, whole((8, width)),
+            one, one, whole((length, 128)), one, spec,
+            pl.BlockSpec((1, 1, width), lambda b: (jnp.maximum(b - blocks, 0), 0, 0)),
+            whole((8, width)),
         ],
         out_shape=[
-            token(F32), jax.ShapeDtypeStruct((length, 128), F32), token(BF), hidden, hidden,
-            token(BF), token(F32), token(BF), jax.ShapeDtypeStruct((8, width), F32),
+            token(BF), token(F32), jax.ShapeDtypeStruct((length, 128), F32), token(F32),
+            jax.ShapeDtypeStruct(full, BF),
+            jax.ShapeDtypeStruct((blocks, 1, width), F32),
+            jax.ShapeDtypeStruct((8, width), F32),
         ],
-        scratch_shapes=[pltpu.VMEM((length, width), F32), pltpu.VMEM((length, width), F32)],
-        compiler_params=params(),
-        cost_estimate=cost(17),
-        name="feed",
-    )(mixed, w, x, nv, hb, w_feed, w_feed, cot)
-
-
-def back_grad_kernel(gffn_ref, act_ref, out_ref, turned_ref):
-    @pl.when(pl.program_id(0) == 0)
-    def _():
-        turned_ref[...] = gffn_ref[...].T
-
-    store_matrix(out_ref, mm(turned_ref[...], act_ref[...]))
-
-
-def back_grad(gffn, active, lines, rows):
-    length, width = gffn.shape
-    blocks = active.shape[0]
-    shape = grad_shape(blocks, lines, rows, width // 2)
-    return pl.pallas_call(
-        back_grad_kernel,
-        grid=(blocks,),
-        in_specs=[
-            whole(gffn.shape),
-            pl.BlockSpec((None, length, width), lambda b: (b, 0, 0)),
+        scratch_shapes=[
+            buffer(F32), buffer(F32), buffer(BF), pltpu.VMEM((width, length), BF),
+            pltpu.VMEM((blocks, length, width), BF), pltpu.VMEM((blocks, length, width), BF),
+            buffer(BF), pltpu.VMEM((width, length), BF), buffer(BF),
         ],
-        out_specs=grad_spec(shape),
-        out_shape=jax.ShapeDtypeStruct(shape, BF),
-        scratch_shapes=[pltpu.VMEM((width, length), BF)],
-        compiler_params=params(),
-        cost_estimate=cost(7),
-        name="back_grad",
-    )(gffn, active)
-
-
-def feed_back_kernel(
-    gffn_ref, slope_ref, low_ref, wback_ref, win_ref, gh2_ref, unit_ref, inv_ref, nv_ref,
-    wo_ref, mixed_ref,
-    gw_ref, hsum_ref, gh1_ref, gmixed_ref, sums_ref,
-    turned_ref, acc_ref,
+        compiler_params=params(VMEM_MB),
+        cost_estimate=cost(30),
+        name="mlp",
+    )(mixed, w_feed, x, nv, hb, w_feed, w_feed, cot)
+
+
+def norm_down_kernel(
+    gfirst_ref, unit_ref, inv_ref, nv_ref, wo_ref, gh1_ref, gattn_ref, gmixed_ref, sums_ref, prod_ref
 ):
-    step = pl.program_id(0)
-    last = pl.num_programs(0) - 1
-
-    @pl.when(step == 0)
-    def _():
-        turned_ref[...] = low_ref[...].T
-        acc_ref[...] = gh2_ref[...]
-
-    @pl.when(step < last)
-    def _():
-        gact = mm(gffn_ref[...], full_matrix(wback_ref))
-        ghid = (gact * slope_ref[...].astype(F32)).astype(BF)
-        hsum_ref[0] = jnp.sum(ghid.astype(F32), axis=0, keepdims=True)
-        store_matrix(gw_ref, mm(turned_ref[...], ghid))
-        acc_ref[...] += mm(ghid, full_matrix(win_ref), NT)
-
-    @pl.when(step == last)
-    def _():
-        gfirst = acc_ref[...]
-        unit = unit_ref[...]
-        gh1 = norm_back(unit, inv_ref[:, 0:1], gfirst * nv_ref[0:1])
-        gh1_ref[...] = gh1
-        gattn = gh1.astype(BF)
-        store_matrix(gw_ref, mm(gattn.T, mixed_ref[...]))
-        gmixed_ref[...] = mm(gattn, full_matrix(wo_ref)).astype(BF)
-        sums_ref[0:1] = jnp.sum(gfirst * unit, axis=0, keepdims=True)
-        sums_ref[1:2] = jnp.sum(gfirst, axis=0, keepdims=True)
-        sums_ref[2:3] = jnp.sum(gh1, axis=0, keepdims=True)
-        sums_ref[3:8] = jnp.zeros((5, sums_ref.shape[1]), F32)
-
-
-def feed_back(gffn, slope, low, w_feed, gh2, unit, inv, nv, w, mixed, lines, rows):
-    length, width = gffn.shape
-    blocks = slope.shape[0]
-    capped = lambda b: jnp.minimum(b, blocks - 1)
+    def rows_back(rows):
+        gfirst = gfirst_ref[rows, :]
+        unit = unit_ref[rows, :]
+        gh1 = norm_back(unit, inv_ref[rows, 0:1], gfirst * nv_ref[0:1])
+        gh1_ref[rows, :] = gh1
+        gattn_ref[rows, :] = gh1.astype(BF)
+        prod_ref[rows, :] = gfirst * unit
+
+    rows_back(slice(None))
+    gmixed_ref[...] = mm(gattn_ref[...], full_matrix(wo_ref)).astype(BF)
+    sums_ref[0:1] = jnp.sum(prod_ref[...], axis=0, keepdims=True)
+    sums_ref[1:2] = jnp.sum(gfirst_ref[...], axis=0, keepdims=True)
+    sums_ref[2:3] = jnp.sum(gh1_ref[...], axis=0, keepdims=True)
+    sums_ref[3:8] = jnp.zeros((5, sums_ref.shape[1]), F32)
+
+
+def norm_down(gfirst, unit, inv, nv, w_feed):
+    length, width = gfirst.shape
     one = whole((length, width))
     token = lambda d: jax.ShapeDtypeStruct((length, width), d)
-    shape = grad_shape(blocks + 1, lines, rows, width // 2)
     return pl.pallas_call(
-        feed_back_kernel,
-        grid=(blocks + 1,),
-        in_specs=[
-            one,
-            pl.BlockSpec((None, length, width), lambda b: (capped(b), 0, 0)),
-            one,
-            weight_spec(w_feed.shape, lambda b: capped(b) + blocks),
-            weight_spec(w_feed.shape, capped),
-            one, one, whole(inv.shape), whole(nv.shape), weight_spec(w.shape, lambda b: 4), one,
-        ],
-        out_specs=[
-            grad_spec(shape),
-            pl.BlockSpec((1, 1, width), lambda b: (capped(b), 0, 0)),
-            one, one, whole((8, width)),
-        ],
-        out_shape=[
-            jax.ShapeDtypeStruct(shape, BF),
-            jax.ShapeDtypeStruct((blocks, 1, width), F32),
-            token(F32),
-            token(BF),
-            jax.ShapeDtypeStruct((8, width), F32),
-        ],
-        scratch_shapes=[pltpu.VMEM((width, length), BF), pltpu.VMEM((length, width), F32)],
-        compiler_params=params(),
-        cost_estimate=cost(17),
-        name="feed_back",
-    )(gffn, slope, low, w_feed, w_feed, gh2, unit, inv, nv, w, mixed)
+        norm_down_kernel,
+        grid=(1,),
+        in_specs=[one, one, whole(inv.shape), whole(nv.shape), weight_spec(w_feed.shape, lambda b: 0)],
+        out_specs=[one, one, one, whole((8, width))],
+        out_shape=[token(F32), token(BF), token(BF), jax.ShapeDtypeStruct((8, width), F32)],
+        scratch_shapes=[pltpu.VMEM((length, width), F32)],
+        compiler_params=params(VMEM_MB),
+        cost_estimate=cost(5),
+        name="norm_down",
+    )(gfirst, unit, inv, nv, w_feed)
 
 
 def attend_back_kernel(
@@ -500,14 +488,14 @@
             jax.ShapeDtypeStruct((8, width), F32),
         ],
         scratch_shapes=[pltpu.VMEM((rel.shape[0], pair), F32)],
-        compiler_params=params(),
+        compiler_params=params(VMEM_MB),
         cost_estimate=cost(28),
         name="attend_back",
     )(probs, gm, qc, qp, k, v, rel)
 
 
 def project_back_kernel(
-    x_ref, gq_ref, gk_ref, gv_ref, grel_ref, sine_t_ref, w_ref, gh1_ref,
+    x_ref, gq_ref, gk_ref, gv_ref, grel_ref, sine_t_ref, gattn_ref, mixed_ref, w_ref, gh1_ref,
     gw_ref, gtok_ref,
     turned_ref,
 ):
@@ -529,26 +517,33 @@
     def _():
         store_matrix(gw_ref, mm(sine_t_ref[...], grel_ref[...]))
 
-
-def project_back(x, gq, gk, gv, grel, sine_t, w, gh1, lines, rows):
+    @pl.when(step == 4)
+    def _():
+        store_matrix(gw_ref, mm(gattn_ref[...], mixed_ref[...], TN))
+
+
+def project_back(x, gq, gk, gv, grel, sine_t, gattn, mixed, w, gh1, lines, rows):
     length, width = x.shape
-    one = whole((length, width))
-    shape = grad_shape(4, lines, rows, width // 2)
+    one = held((length, width))
+    shape = grad_shape(5, lines, rows, width // 2)
     return pl.pallas_call(
         project_back_kernel,
-        grid=(4,),
+        grid=(5,),
         in_specs=[
-            one, one, one, one, whole(grel.shape), whole(sine_t.shape),
+            one, one, one, one, held(grel.shape), held(sine_t.shape), one, one,
             weight_spec(w.shape, lambda b: jnp.minimum(b, 2)),
             one,
         ],
-        out_specs=[grad_spec(shape), one],
-        out_shape=[jax.ShapeDtypeStruct(shape, BF), jax.ShapeDtypeStruct((length, width), F32)],
+        out_specs=[grad_spec(shape), whole((length, width))],
+        out_shape=[
+            jax.ShapeDtypeStruct(shape, BF),
+            jax.ShapeDtypeStruct((length, width), F32),
+        ],
         scratch_shapes=[pltpu.VMEM((width, length), BF)],
-        compiler_params=params(),
-        cost_estimate=cost(11),
+        compiler_params=params(VMEM_MB),
+        cost_estimate=cost(12),
         name="project_back",
-    )(x, gq, gk, gv, grel, sine_t, w, gh1)
+    )(x, gq, gk, gv, grel, sine_t, gattn, mixed, w, gh1)
 
 
 def swap_x(value):
@@ -565,11 +560,14 @@
 
 
 def gather_matrices(shard):
+    dp = lax.axis_size("dp")
+    if shard.shape[1] % 16 == 0:
+        order = [mp * dp + index for mp, index in ring_order(dp // 4)]
+        return lax.all_gather(
+            shard, ("mp", "dp"), axis=0, axis_index_groups=[order], tiled=False
+        )
     pieces = lax.all_gather(shard, ("mp", "dp"), axis=0, tiled=False)
-    pieces = pieces.reshape((2, lax.axis_size("dp")) + shard.shape)
-    if shard.shape[1] % 16 == 0:
-        return pieces
-    return whole_matrices(pieces)
+    return whole_matrices(pieces.reshape((2, dp) + shard.shape))
 
 
 def whole_matrices(pieces):
@@ -610,13 +608,22 @@
 ]
 
 
-def gather_stepwise(shard):
+def gather_lines(shard, others):
+    lines = lax.axis_size("dp") // 4
+    if lines != 4 or shard.shape[1] % 16 != 0:
+        return shard, others
+    near = [shard] + [shift_line(shard, step) for step in range(1, lines)]
+    near, others = lax.optimization_barrier((near, others))
+    return jnp.stack(near), others
+
+
+def gather_stepwise(near, shard):
     dp = lax.axis_size("dp")
     blocks, rows, columns = shard.shape
     lines = dp // 4
     if lines != 4 or rows % 16 != 0:
-        return gather_matrices(shard)
-    near = jnp.stack([shard] + [shift_line(shard, step) for step in range(1, lines)])
+        pieces = lax.all_gather(shard, ("mp", "dp"), axis=0, tiled=False)
+        return whole_matrices(pieces.reshape((2, dp) + shard.shape))
     cut = blocks // 2
     one, two = near[:, :cut], near[:, cut:]
     one_x = swap_x(one)
@@ -636,7 +643,7 @@
         out_specs=pl.BlockSpec(memory_space=pltpu.VMEM),
         out_shape=jax.ShapeDtypeStruct((blocks, 2, dp * rows, columns), BF),
         scratch_shapes=[pltpu.SemaphoreType.DMA((len(parts) * lines,))],
-        compiler_params=params(),
+        compiler_params=params(VMEM_MB),
         cost_estimate=cost(5),
         name="place",
     )(place.astype(jnp.int32), *parts)
@@ -682,10 +689,15 @@
     return total
 
 
-def sum_small(value):
+def sum_small(value, meanwhile):
     value = value + swap_dp(value, 1)
     value = value + swap_x(value)
     value = value + swap_dp(value, 2)
+    value, meanwhile = lax.optimization_barrier((value, meanwhile))
+    return sum_line(value), meanwhile
+
+
+def sum_line(value):
     lines = lax.axis_size("dp") // 4
     if lines != 4:
         return lax.psum(value, ("dp",), axis_index_groups=line_only(lines))
@@ -699,31 +711,30 @@
     return [[line * 4 + low for line in range(lines)] for low in range(4)]
 
 
-def adam_kernel(g_ref, p_ref, one_ref, two_ref, *refs):
+def adam_kernel(order, g_ref, p_ref, one_ref, two_ref, *refs):
     outs = refs[-3:]
-    results = adam_update(p_ref[...], g_ref[...], one_ref[...], two_ref[...], RATE_BIG)
-    for out, result in zip(outs, results):
-        out[...] = result
-
-
-def adam_blocks(grad, first, param, one, two, held):
+    for block, at in enumerate(order):
+        results = adam_update(p_ref[at], g_ref[block], one_ref[at], two_ref[at], RATE_BIG)
+        for out, result in zip(outs, results):
+            out[at] = result
+
+
+def adam_blocks(grad, order, param, one, two, done):
     blocks, rows, columns = grad.shape
-    step = 4
-    part = pl.BlockSpec((step, rows, columns), lambda b: (b + first // step, 0, 0))
-    anywhere = pl.BlockSpec(memory_space=pl.ANY)
+    part = whole((blocks, rows, columns) if done else param.shape)
     shape = jax.ShapeDtypeStruct(param.shape, F32)
     return pl.pallas_call(
-        adam_kernel,
-        grid=(pl.cdiv(blocks, step),),
-        in_specs=[pl.BlockSpec((step, rows, columns), lambda b: (b, 0, 0)), part, part, part]
-        + [anywhere] * len(held),
+        functools.partial(adam_kernel, order),
+        grid=(1,),
+        in_specs=[whole(grad.shape), part, part, part]
+        + [pl.BlockSpec(memory_space=pl.ANY)] * len(done),
         out_specs=[part] * 3,
         out_shape=[shape] * 3,
-        input_output_aliases={4 + i: i for i in range(len(held))},
-        compiler_params=params(),
+        input_output_aliases={4 + i: i for i in range(len(done))},
+        compiler_params=params(VMEM_MB),
         cost_estimate=cost(blocks // 2),
         name="adam",
-    )(grad, param, one, two, *held)
+    )(grad, param, one, two, *done)
 
 
 def per_device(
@@ -751,44 +762,38 @@
     sine = relative_embedding(seq_len, model_width).astype(BF)
     shard = weights.transpose(1, 0, 2)
     shard_low = shard.astype(BF)
-    w_feed = gather_matrices(shard_low[5:13])
-    w = gather_stepwise(shard_low[0:5])
     heads_all = lax.all_gather(head_vecs, "mp", axis=1, tiled=True)
+    near, (x, sine, sine_t, heads_all, shard_feed) = gather_lines(
+        shard_low[0:4], (x, sine, sine.T, heads_all, shard_low[4:13])
+    )
+    w_feed = gather_matrices(shard_feed)
+    w = gather_stepwise(near, shard_low[0:4])
 
     qc, qp, k, v, rel = project(x, w, heads_all[0:2], sine)
     probs, mixed = attend(used, qc, qp, k, v, rel)
     hb = heads_all[2:6].reshape(4, 1, model_width)
-    unit, inv, low, active, slope, out, gh2, gffn, sums2 = feed(
-        mixed, w, x, norm_vecs, hb, w_feed, cotangent
-    )
-    gw_back = back_grad(gffn, active, lines, weight_rows)
-    part_back = scatter_plane(gw_back)
-    gffn, _ = lax.optimization_barrier((gffn, gw_back))
-    gw_in, hsum, gh1, gmixed, sums1 = feed_back(
-        gffn, slope, low, w_feed, gh2, unit, inv, norm_vecs, w, mixed, lines, weight_rows
-    )
-    gw_in, part_back = lax.optimization_barrier((gw_in, part_back))
-    part_in = scatter_plane(gw_in)
+    out, unit, inv, gfirst, gw_feed, hsum, sums2 = mlp(
+        mixed, w_feed, x, norm_vecs, hb, cotangent, lines, weight_rows
+    )
+    part_feed = scatter_plane(gw_feed)
+    gh1, gattn, gmixed, sums1 = norm_down(gfirst, unit, inv, norm_vecs, w_feed)
     gq, gk, gv, grel, sums_q = attend_back(probs, gmixed, qc, qp, k, v, rel)
-    line_back = scatter_line(part_back)
-    gq, line_back = lax.optimization_barrier((gq, line_back))
     gproj, grad_tokens = project_back(
-        x, gq, gk, gv, grel, sine.T, w, gh1, lines, weight_rows
-    )
-    gproj, part_in = lax.optimization_barrier((gproj, part_in))
+        x, gq, gk, gv, grel, sine_t, gattn, mixed, w, gh1, lines, weight_rows
+    )
+    gproj, part_feed = lax.optimization_barrier((gproj, part_feed))
     part_proj = scatter_plane(gproj)
 
     norm_part = jnp.concatenate([sums1[0:2], sums2[0:2], sums1[2:3], sums2[2:3]], axis=0)
     head_part = jnp.concatenate([sums_q[0:2], hsum[:, 0]], axis=0)
+    line_feed = scatter_line(part_feed)
     small = jnp.concatenate([norm_part, head_part], axis=0)
-    small = sum_small(small)
+    small, line_feed = sum_small(small, line_feed)
     norm_grad = small[0:6]
     head_grad = lax.dynamic_slice_in_dim(small[6:12], mp_index * local_width, local_width, 1)
     state = (shard, weight_m1.transpose(1, 0, 2), weight_m2.transpose(1, 0, 2))
-    line_in = scatter_line(part_in)
-    early = jnp.concatenate([line_in[4:5], line_in[0:4], line_back], axis=0)
-    held = adam_blocks(early, 4, *state, ())
-    new_big = adam_blocks(scatter_line(part_proj), 0, *state, held)
+    held_big = adam_blocks(line_feed, (5, 9, 6, 10, 7, 11, 8, 12), *state, ())
+    new_big = adam_blocks(scatter_line(part_proj), tuple(range(5)), *state, held_big)
     new_weights, new_weight_m1, new_weight_m2 = [a.transpose(1, 0, 2) for a in new_big]
     new_head, new_head_m1, new_head_m2 = adam_update(
         head_vecs, head_grad, head_m1, head_m2, RATE_SMALL

time: 293 us -> 263 us (0.90)
  waiting for transfers between devices: 90.8 us -> 60.4 us
  Pallas kernels: 120 us -> 114 us
  starting transfers between devices: 37.3 us -> 42.6 us
    reduce_scatter x3 -> x2, waiting for transfers between devices: 24.4 us -> 8.45 us  [scatter_plane(): lax.psum_scatter(grads, ('mp', 'dp'), scatter_dimension=0, axis_index_gro...]
    ppermute x15 -> x12, waiting for transfers between devices: 35.3 us -> 23.4 us  [shift_line(): lax.ppermute(value, 'dp', [(d, (d + 4 * step) % dp) for d in range(dp)])]
    ppermute x4, starting transfers between devices: 5.15 us -> 15.4 us  [swap_x(): return lax.ppermute(value, 'mp', [(0, 1), (1, 0)])]
    ppermute x13, waiting for transfers between devices: 12.2 us -> 4.46 us  [swap_dp(): lax.ppermute(value, 'dp', [(d, d ^ bit) for d in range(lax.axis_size('dp'...]
    pallas_call x6 -> x5, Pallas kernels: 57.9 us -> 52.3 us  [the longest x1 28 us: mlp(): pl.pallas_call(mlp_kernel, grid=(2 * blocks,), in_specs=[held((length, wi...]
    ppermute x4, waiting for transfers between devices: 18.9 us -> 24 us  [swap_x(): return lax.ppermute(value, 'mp', [(0, 1), (1, 0)])]
    ppermute x15 -> x12, starting transfers between devices: 24.5 us -> 20.7 us  [shift_line(): lax.ppermute(value, 'dp', [(d, (d + 4 * step) % dp) for d in range(dp)])]
  transfers between devices with their start and end apart: 36 -> 32, of which waited for: 16 -> 10; matrix products, arithmetic and copies ran while one was open for 7% -> 8% of each run, Pallas kernels for 32% -> 32%
where the time goes in v3:
time: 263 us
  Pallas kernels  114 us (43%)
  waiting for transfers between devices  60.4 us (23%)
  starting transfers between devices  42.6 us (16%)
  other arithmetic  14.6 us (6%)
  between operations  14.1 us (5%)
  local copies, waits for them, and re-layouts  12.1 us (5%)
  blocking collectives  4.39 us (2%)
    pallas_call x1, Pallas kernels, attend_back(): pl.pallas_call(attend_back_kernel, grid=(heads // 2,), in_specs=[pl.Block...  28.6 us
    pallas_call x1, Pallas kernels, mlp(): pl.pallas_call(mlp_kernel, grid=(2 * blocks,), in_specs=[held((length, wi...  28 us
    ppermute x4, waiting for transfers between devices, swap_x(): return lax.ppermute(value, 'mp', [(0, 1), (1, 0)])  24 us
    ppermute x12, waiting for transfers between devices, shift_line(): lax.ppermute(value, 'dp', [(d, (d + 4 * step) % dp) for d in range(dp)])  23.4 us
    ppermute x12, starting transfers between devices, shift_line(): lax.ppermute(value, 'dp', [(d, (d + 4 * step) % dp) for d in range(dp)])  20.7 us
    pallas_call x1, Pallas kernels, attend(): pl.pallas_call(attend_kernel, grid=(heads // 2,), in_specs=[pl.BlockSpec(...  18.8 us
    ppermute x4, starting transfers between devices, swap_x(): return lax.ppermute(value, 'mp', [(0, 1), (1, 0)])  15.4 us
    pallas_call x1, Pallas kernels, project_back(): pl.pallas_call(project_back_kernel, grid=(5,), in_specs=[one, one, one, o...  12.8 us
  transfers between devices with their start and end apart: 32, of which 10 were waited for; matrix products, arithmetic and copies ran while one was open for 8% of the time, Pallas kernels for 32%

profile of v3, /device:TPU:0, one launch (start us, length us, event | category | flops | bytes accessed | tf_op | source)
XLA Modules:
  0.0 262.6 jit_solution(12426693582870306295)
XLA Ops:
  7.2 1.4 bitcast_convert_fusion
  8.6 3.1 %collective-permute-start = (bf16[4,48,384]{2,1,0:T(8,128)(2,1)S(1)}, bf16[4,48,384]{2,1,0:T(8,128)(2,1)S(1)}, u32[]{:S(2)}, u32[]{:S(2)}) collective-permute-start(bf16[4,48,384]{2,1,0:T(8,128)(2,1)S(1)} %slice.52), channel_id=1, source_target_pairs={{0,8},{2,10},{4,12},{6,14},{8,16},{10,18},{12,20},{14,22},{16,24},... | collective-permute-start | bytes 442376 | tf_op jit(solution)/shard_map/ppermute | solution.py:559
  11.7 2.6 collective-permute-start.1
  14.3 1.3 collective-permute-start.2
  15.7 6.0 %fusion = (bf16[1024,384]{0,1:T(8,128)(2,1)S(1)}, bf16[1024,384]{0,1:T(8,128)(2,1)S(1)}) fusion(f32[384]{0:T(512)S(1)} %negate_power_fusion, f32[1024]{0:T(1024)S(1)} %subtract_convert_fusion), kind=kLoop, calls=%fused_computation.2 | loop fusion | flops 1179648 | bytes 1578496 | tf_op jit(solution)/shard_map/convert.2
  21.7 1.5 fusion.8
  23.3 0.8 slice.53
  24.0 4.4 %all_gather.9 = f32[6,768]{1,0:T(8,128)S(1)} all-gather(f32[6,384]{1,0:T(8,128)S(1)} %copy-done.5), channel_id=1, replica_groups=mesh['dp'=16,'mp'=2] {'mp'}, dimensions={1}, use_global_device_ids=true | all-gather | bytes 27648 | tf_op jit(solution)/shard_map/all_gather | solution.py:765
  28.4 0.9 constant_dynamic-slice_fusion.x_ref
  29.4 1.1 pad_maximum_fusion.1
  30.6 1.6 collective-permute-start.3
  32.2 1.5 collective-permute-start.4
  34.7 10.3 %collective-permute-done.3.refs_2_ = bf16[4,2,48,384]{3,2,1,0:T(8,128)(2,1)S(1)} collective-permute-done((bf16[4,2,48,384]{3,2,1,0:T(8,128)(2,1)S(1)}, bf16[4,2,48,384]{3,2,1,0:T(8,128)(2,1)S(1)}, u32[]{:S(2)}, u32[]{:S(2)}) %collective-permute-start.3) | collective-permute-done | bytes 294944 | tf_op jit(solution)/shard_map/ppermute | solution.py:550
  45.0 1.3 collective-permute-start.7
  46.4 12.7 %collective-permute-start.8 = (bf16[4,2,48,384]{3,2,1,0:T(8,128)(2,1)S(1)}, bf16[4,2,48,384]{3,2,1,0:T(8,128)(2,1)}, u32[]{:S(2)}, u32[]{:S(2)}) collective-permute-start(bf16[4,2,48,384]{3,2,1,0:T(8,128)(2,1)S(1)} %collective-permute-done.4.refs_3_), channel_id=1, source_target_pairs={{0,1},{1,0},{2,3},{3,2},{4,5},{5,4},{6,7},{7,6},{8,9},{9,8},{10,11... | collective-permute-start | bytes 884744 | tf_op jit(solution)/shard_map/ppermute | solution.py:550
  60.1 9.6 %collective-permute-done.8.refs_7_ = bf16[4,2,48,384]{3,2,1,0:T(8,128)(2,1)} collective-permute-done((bf16[4,2,48,384]{3,2,1,0:T(8,128)(2,1)S(1)}, bf16[4,2,48,384]{3,2,1,0:T(8,128)(2,1)}, u32[]{:S(2)}, u32[]{:S(2)}) %collective-permute-start.8) | collective-permute-done | bytes 294944 | tf_op jit(solution)/shard_map/ppermute | solution.py:550
  72.7 1.6 copy.27.sine_ref
  74.9 6.0 %place.1.w_ref = bf16[4,2,768,384]{3,2,1,0:T(8,128)(2,1)} custom-call(s32[4]{0:T(128)} %pad_add_fusion.place_ref, bf16[4,2,48,384]{3,2,1,0:T(8,128)(2,1)} %copy-done.4, bf16[4,2,48,384]{3,2,1,0:T(8,128)(2,1)} %copy-done.3, bf16[4,2,48,384]{3,2,1,0:T(8,128)(2,1)} %copy-done.12, bf16[4,2,48,384]{3,2,1,0:T(8,128)(2,1)} %copy-done.13, ...), custom_call_target="tpu_custom_call" | custom-call | flops 5000000000 | tf_op jit(solution)/shard_map/place/pallas_call | solution.py:640
  80.9 8.8 %project.1 = (bf16[512,768]{1,0:T(8,128)(2,1)}, bf16[512,768]{1,0:T(8,128)(2,1)}, bf16[512,768]{1,0:T(8,128)(2,1)}, bf16[512,768]{1,0:T(8,128)(2,1)}, bf16[1024,768]{1,0:T(8,128)(2,1)}) custom-call(bf16[512,768]{1,0:T(8,128)(2,1)} %constant_dynamic-slice_fusion.x_ref, bf16[4,2,768,384]{3,2,1,0:T(8,128)(2,1)} %place.1.w_ref, f32[2,768]{1,0:T(2,128)} %slice.43.vec_ref, ...), custom_call_target="tpu_custom_call" | custom-call | flops 8999999488 | tf_op jit(solution)/shard_map/project/pallas_call | solution.py:155
  89.7 18.8 %attend.1 = (bf16[12,512,512]{2,1,0:T(8,128)(2,1)}, bf16[512,768]{1,0:T(8,128)(2,1)}) custom-call(s32[1]{0:T(128)} %dynamic_slice.35.len_ref, bf16[512,768]{1,0:T(8,128)(2,1)} %get-tuple-element.62.qc_ref, bf16[512,768]{1,0:T(8,128)(2,1)} %get-tuple-element.63.qp_ref, bf16[512,768]{1,0:T(8,128)(2,1)} %get-tuple-element.64.k_ref, ...), custom_call_target="tpu_custom_call" | custom-call | flops 19000000512 | tf_op jit(solution)/shard_map/attend/pallas_call | solution.py:212
  108.4 28.0 %mlp.1 = (bf16[512,768]{1,0:T(8,128)(2,1)}, f32[512,768]{1,0:T(8,128)}, f32[512,128]{1,0:T(8,128)}, f32[512,768]{1,0:T(8,128)}, bf16[8,4,8,48,384]{4,3,2,1,0:T(8...) custom-call(bf16[512,768]{1,0:T(8,128)(2,1)} %get-tuple-element.67.mixed_ref, bf16[32,9,48,384]{3,2,1,0:T(8,128)(2,1)} %bitcast.47, ...), custom_call_target="tpu_custom_call" | custom-call | flops 30000001024 | tf_op jit(solution)/shard_map/mlp/pallas_call | solution.py:332
  136.5 4.9 %norm_down.1 = (f32[512,768]{1,0:T(8,128)}, bf16[512,768]{1,0:T(8,128)(2,1)}, bf16[512,768]{1,0:T(8,128)(2,1)}, f32[8,768]{1,0:T(8,128)}) custom-call(f32[512,768]{1,0:T(8,128)} %get-tuple-element.71.gfirst_ref, f32[512,768]{1,0:T(8,128)} %get-tuple-element.72.unit_ref, f32[512,128]{1,0:T(8,128)} %get-tuple-element.73.inv_ref, f32[6,768]{1,0:T(8,128)} %nv_ref.3, ...), custom_call_target="tpu_custom_call" | custom-call | flops 5000000000 | tf_op jit(solution)/shard_map/norm_down/pallas_call | solution.py:390
  141.4 28.6 %attend_back.1 = (bf16[512,768]{1,0:T(8,128)(2,1)}, bf16[512,768]{1,0:T(8,128)(2,1)}, bf16[512,768]{1,0:T(8,128)(2,1)}, bf16[1024,768]{1,0:T(8,128)(2,1)}, f32[8,768]{1,0:T(8,128)}) custom-call(bf16[12,512,512]{2,1,0:T(8,128)(2,1)} %get-tuple-element.70.probs_ref, bf16[512,768]{1,0:T(8,128)(2,1)} %get-tuple-element.74.gm_ref, ...), custom_call_target="tpu_custom_call" | custom-call | flops 28000000000 | tf_op jit(solution)/shard_map/attend_back/pallas_call | solution.py:480
  170.0 12.8 %project_back.1 = (bf16[8,4,5,48,384]{4,3,2,1,0:T(8,128)(2,1)}, f32[512,768]{1,0:T(8,128)}) custom-call(bf16[512,768]{1,0:T(8,128)(2,1)} %constant_dynamic-slice_fusion.x_ref, bf16[512,768]{1,0:T(8,128)(2,1)} %get-tuple-element.75.gq_ref, bf16[512,768]{1,0:T(8,128)(2,1)} %get-tuple-element.76.gk_ref, bf16[512,768]{1,0:T(8,128)(2,1)} %get-tuple-element.77.gv_ref, ...), custom_call_target="tpu_custom_call" | custom-call | flops 12000000000 | tf_op jit(solution)/shard_map/project_back/pallas_call | solution.py:529
  182.8 8.0 %reduce-scatter.3.cloned.1.call-done = bf16[1,4,8,48,384]{4,3,2,1,0:T(8,128)(2,1)} async-done(((bf16[8,4,8,48,384]{4,3,2,1,0:T(8,128)(2,1)}), bf16[1,4,8,48,384]{4,3,2,1,0:T(8,128)(2,1)}) %reduce-scatter.3.cloned.1.call-update) | async-done | bytes 1179664 | tf_op jit(solution)/shard_map/reduce_scatter | solution.py:671
  190.9 1.2 copy-done.2
  192.2 3.4 %collective-permute-start.25 = (bf16[8,48,384]{2,1,0:T(8,128)(2,1)S(1)}, bf16[8,48,384]{2,1,0:T(8,128)(2,1)S(1)}, u32[]{:S(2)}, u32[]{:S(2)}) collective-permute-start(bf16[8,48,384]{2,1,0:T(8,128)(2,1)S(1)} %get-tuple-element.108), channel_id=1, source_target_pairs={{0,24},{2,26},{4,28},{6,30},{8,0},{10,2},{12,4},{14,6},{16,8},{18,... | collective-permute-start | bytes 884744 | tf_op jit(solution)/shard_map/ppermute | solution.py:559
  195.6 1.1 collective-permute-start.23
  197.4 0.7 slice.47
  198.2 0.7 slice.46
  198.9 0.7 slice.48
  199.7 0.7 slice.49
  200.5 1.2 collective-permute-done.20
  202.4 4.1 %collective-permute-done.21 = f32[12,768]{1,0:T(8,128)S(1)} collective-permute-done((f32[12,768]{1,0:T(8,128)S(1)}, f32[12,768]{1,0:T(8,128)S(1)}, u32[]{:S(2)}, u32[]{:S(2)}) %collective-permute-start.21) | collective-permute-done | bytes 36896 | tf_op jit(solution)/shard_map/ppermute | solution.py:550
  206.5 1.5 collective-permute-start.22
  208.1 3.2 %collective-permute-done.22 = f32[12,768]{1,0:T(8,128)S(1)} collective-permute-done((f32[12,768]{1,0:T(8,128)S(1)}, f32[12,768]{1,0:T(8,128)S(1)}, u32[]{:S(2)}, u32[]{:S(2)}) %collective-permute-start.22) | collective-permute-done | bytes 36896 | tf_op jit(solution)/shard_map/ppermute | solution.py:554
  211.3 9.5 %collective-permute-done.24 = bf16[8,48,384]{2,1,0:T(8,128)(2,1)S(1)} collective-permute-done((bf16[8,48,384]{2,1,0:T(8,128)(2,1)S(1)}, bf16[8,48,384]{2,1,0:T(8,128)(2,1)S(1)}, u32[]{:S(2)}, u32[]{:S(2)}) %collective-permute-start.24) | collective-permute-done | bytes 294944 | tf_op jit(solution)/shard_map/ppermute | solution.py:559
  220.8 1.0 fusion.3.g_ref
  221.7 2.7 %collective-permute-start.27 = (f32[12,768]{1,0:T(8,128)S(1)}, f32[12,768]{1,0:T(8,128)S(1)}, u32[]{:S(2)}, u32[]{:S(2)}) collective-permute-start(f32[12,768]{1,0:T(8,128)S(1)} %add.154), channel_id=1, source_target_pairs={{0,16},{2,18},{4,20},{6,22},{8,24},{10,26},{12,28},{14,30},{16,0},... | collective-permute-start | bytes 110600 | tf_op jit(solution)/shard_map/ppermute | solution.py:559
  224.4 2.0 collective-permute-start.26
  226.4 4.0 %adam.2 = (f32[13,48,384]{2,1,0:T(8,128)}, f32[13,48,384]{2,1,0:T(8,128)}, f32[13,48,384]{2,1,0:T(8,128)}) custom-call(f32[8,48,384]{2,1,0:T(8,128)} %fusion.3.g_ref, f32[13,48,384]{2,1,0:T(8,128)} %bitcast.42, f32[13,48,384]{2,1,0:T(8,128)} %bitcast.51, f32[13,48,384]{2,1,0:T(8,128)} %bitcast.53), custom_call_target="tpu_custom_call" | custom-call | flops 4000000000 | tf_op jit(solution)/shard_map/adam/pallas_call | solution.py:726
  231.6 1.2 dynamic-slice_bitcast_fusion.5
  232.7 3.3 %collective-permute-start.19 = (bf16[5,48,384]{2,1,0:T(8,128)(2,1)S(1)}, bf16[5,48,384]{2,1,0:T(8,128)(2,1)S(1)}, u32[]{:S(2)}, u32[]{:S(2)}) collective-permute-start(bf16[5,48,384]{2,1,0:T(8,128)(2,1)S(1)} %get-tuple-element.111), channel_id=1, source_target_pairs={{0,24},{2,26},{4,28},{6,30},{8,0},{10,2},{12,4},{14,6},{16,8},{18,... | collective-permute-start | bytes 552968 | tf_op jit(solution)/shard_map/ppermute | solution.py:559
  236.1 1.1 collective-permute-start.17
  237.8 3.4 %collective-permute-done.19 = bf16[5,48,384]{2,1,0:T(8,128)(2,1)S(1)} collective-permute-done((bf16[5,48,384]{2,1,0:T(8,128)(2,1)S(1)}, bf16[5,48,384]{2,1,0:T(8,128)(2,1)S(1)}, u32[]{:S(2)}, u32[]{:S(2)}) %collective-permute-start.19) | collective-permute-done | bytes 184352 | tf_op jit(solution)/shard_map/ppermute | solution.py:559
  241.2 10.5 %collective-permute-done.18 = bf16[5,48,384]{2,1,0:T(8,128)(2,1)S(1)} collective-permute-done((bf16[5,48,384]{2,1,0:T(8,128)(2,1)S(1)}, bf16[5,48,384]{2,1,0:T(8,128)(2,1)S(1)}, u32[]{:S(2)}, u32[]{:S(2)}) %collective-permute-start.18) | collective-permute-done | bytes 184352 | tf_op jit(solution)/shard_map/ppermute | solution.py:559
  251.7 1.8 fusion.5.g_ref
  253.5 2.7 %adam.3 = (f32[13,48,384]{2,1,0:T(8,128)}, f32[13,48,384]{2,1,0:T(8,128)}, f32[13,48,384]{2,1,0:T(8,128)}) custom-call(f32[5,48,384]{2,1,0:T(8,128)} %fusion.5.g_ref, f32[13,48,384]{2,1,0:T(8,128)} %bitcast.43, f32[13,48,384]{2,1,0:T(8,128)} %bitcast.52, f32[13,48,384]{2,1,0:T(8,128)} %bitcast.54, ...), custom_call_target="tpu_custom_call", output_to_operand_aliasing={{0}: (4, {}), {1}: (5, {}), {2}: (6, {})} | custom-call | flops 2000000000 | tf_op jit(solution)/shard_map/adam/pallas_call | solution.py:726
  (100 shorter events, 9.4 us)
Async XLA Ops:
  7.2 21.2 %copy-start = (bf16[1024,768]{1,0:T(8,128)(2,1)S(1)}, bf16[1024,768]{1,0:T(8,128)(2,1)}, u32[]{:S(2)}) copy-start(bf16[1024,768]{1,0:T(8,128)(2,1)} %param.12) | copy-start | bytes 4718596
  7.2 101.2 %all-gather.3.cloned.1.call-start = ((), (), s32[]{:S(2)}) async-start(), calls=%async_computation.4 | async-start | bytes 10948608 | tf_op jit(solution)/shard_map/all_gather | solution.py:566
  8.6 20.7 %collective-permute-start = (bf16[4,48,384]{2,1,0:T(8,128)(2,1)S(1)}, bf16[4,48,384]{2,1,0:T(8,128)(2,1)S(1)}, u32[]{:S(2)}, u32[]{:S(2)}) collective-permute-start(bf16[4,48,384]{2,1,0:T(8,128)(2,1)S(1)} %slice.52), channel_id=1, source_target_pairs={{0,8},{2,10},{4,12},{6,14},{8,16},{10,18},{12,20},{14,22},{16,24},... | collective-permute-start | bytes 442376 | tf_op jit(solution)/shard_map/ppermute | solution.py:559
  11.7 17.6 %collective-permute-start.1 = (bf16[4,48,384]{2,1,0:T(8,128)(2,1)S(1)}, bf16[4,48,384]{2,1,0:T(8,128)(2,1)}, u32[]{:S(2)}, u32[]{:S(2)}) collective-permute-start(bf16[4,48,384]{2,1,0:T(8,128)(2,1)S(1)} %slice.52), channel_id=1, source_target_pairs={{0,16},{2,18},{4,20},{6,22},{8,24},{10,26},{12,28},{14,30},{16,0},... | collective-permute-start | bytes 442376 | tf_op jit(solution)/shard_map/ppermute | solution.py:559
  14.3 15.1 %collective-permute-start.2 = (bf16[4,48,384]{2,1,0:T(8,128)(2,1)S(1)}, bf16[4,48,384]{2,1,0:T(8,128)(2,1)}, u32[]{:S(2)}, u32[]{:S(2)}) collective-permute-start(bf16[4,48,384]{2,1,0:T(8,128)(2,1)S(1)} %slice.52), channel_id=1, source_target_pairs={{0,24},{2,26},{4,28},{6,30},{8,0},{10,2},{12,4},{14,6},{16,8},{18,... | collective-permute-start | bytes 442376 | tf_op jit(solution)/shard_map/ppermute | solution.py:559
  29.3 41.5 %copy-start.18 = (s32[2]{0:T(128)S(1)}, s32[2]{0:T(128)}, u32[]{:S(2)}) copy-start(s32[2]{0:T(128)} %param.13) | copy-start | bytes 28
  29.4 161.4 %reduce-scatter.3.cloned.1.call-start = ((), (), s32[]{:S(2)}) async-start(), calls=%async_computation.2 | async-start | bytes 10616832 | tf_op jit(solution)/shard_map/reduce_scatter | solution.py:671
  30.6 43.6 %copy-start.3 = (bf16[4,2,48,384]{3,2,1,0:T(8,128)(2,1)}, bf16[4,2,48,384]{3,2,1,0:T(8,128)(2,1)S(1)}, u32[]{:S(2)}) copy-start(bf16[4,2,48,384]{3,2,1,0:T(8,128)(2,1)S(1)} %get-tuple-element.113.refs_1_) | copy-start | bytes 884740
  30.6 43.6 %copy-start.4 = (bf16[4,2,48,384]{3,2,1,0:T(8,128)(2,1)}, bf16[4,2,48,384]{3,2,1,0:T(8,128)(2,1)S(1)}, u32[]{:S(2)}) copy-start(bf16[4,2,48,384]{3,2,1,0:T(8,128)(2,1)S(1)} %get-tuple-element.114.refs_0_) | copy-start | bytes 884740
  30.6 14.4 %collective-permute-start.3 = (bf16[4,2,48,384]{3,2,1,0:T(8,128)(2,1)S(1)}, bf16[4,2,48,384]{3,2,1,0:T(8,128)(2,1)S(1)}, u32[]{:S(2)}, u32[]{:S(2)}) collective-permute-start(bf16[4,2,48,384]{3,2,1,0:T(8,128)(2,1)S(1)} %get-tuple-element.114.refs_0_), channel_id=1, source_target_pairs={{0,1},{1,0},{2,3},{3,2},{4,5},{5,4},{6,7},{7,6},{8,9},{9,8},{10,11... | collective-permute-start | bytes 884744 | tf_op jit(solution)/shard_map/ppermute | solution.py:550
  32.2 12.9 %collective-permute-start.4 = (bf16[4,2,48,384]{3,2,1,0:T(8,128)(2,1)S(1)}, bf16[4,2,48,384]{3,2,1,0:T(8,128)(2,1)S(1)}, u32[]{:S(2)}, u32[]{:S(2)}) collective-permute-start(bf16[4,2,48,384]{3,2,1,0:T(8,128)(2,1)S(1)} %get-tuple-element.113.refs_1_), channel_id=1, source_target_pairs={{0,4},{2,6},{4,0},{6,2},{8,12},{10,14},{12,8},{14,10},{16,20},{18,... | collective-permute-start | bytes 884744 | tf_op jit(solution)/shard_map/ppermute | solution.py:554
  33.7 12.7 %collective-permute-start.5 = (bf16[4,2,48,384]{3,2,1,0:T(8,128)(2,1)S(1)}, bf16[4,2,48,384]{3,2,1,0:T(8,128)(2,1)S(1)}, u32[]{:S(2)}, u32[]{:S(2)}) collective-permute-start(bf16[4,2,48,384]{3,2,1,0:T(8,128)(2,1)S(1)} %get-tuple-element.114.refs_0_), channel_id=1, source_target_pairs={{0,4},{2,6},{4,0},{6,2},{8,12},{10,14},{12,8},{14,10},{16,20},{18,... | collective-permute-start | bytes 884744 | tf_op jit(solution)/shard_map/ppermute | solution.py:554
  34.2 24.8 %collective-permute-start.6 = (bf16[4,2,48,384]{3,2,1,0:T(8,128)(2,1)S(1)}, bf16[4,2,48,384]{3,2,1,0:T(8,128)(2,1)}, u32[]{:S(2)}, u32[]{:S(2)}) collective-permute-start(bf16[4,2,48,384]{3,2,1,0:T(8,128)(2,1)S(1)} %get-tuple-element.113.refs_1_), channel_id=1, source_target_pairs={{0,1},{1,0},{2,3},{3,2},{4,5},{5,4},{6,7},{7,6},{8,9},{9,8},{10,11... | collective-permute-start | bytes 884744 | tf_op jit(solution)/shard_map/ppermute | solution.py:550
  34.7 24.3 %collective-permute-start.9 = (bf16[4,2,48,384]{3,2,1,0:T(8,128)(2,1)S(1)}, bf16[4,2,48,384]{3,2,1,0:T(8,128)(2,1)S(1)}, u32[]{:S(2)}, u32[]{:S(2)}) collective-permute-start(bf16[4,2,48,384]{3,2,1,0:T(8,128)(2,1)S(1)} %get-tuple-element.114.refs_0_), channel_id=1, source_target_pairs={{0,2},{2,0},{4,6},{6,4},{8,10},{10,8},{12,14},{14,12},{16,18},{18,... | collective-permute-start | bytes 884744 | tf_op jit(solution)/shard_map/ppermute | solution.py:554
  45.0 29.2 %copy-start.12 = (bf16[4,2,48,384]{3,2,1,0:T(8,128)(2,1)}, bf16[4,2,48,384]{3,2,1,0:T(8,128)(2,1)S(1)}, u32[]{:S(2)}) copy-start(bf16[4,2,48,384]{3,2,1,0:T(8,128)(2,1)S(1)} %collective-permute-done.3.refs_2_) | copy-start | bytes 884740
  45.0 14.5 %collective-permute-start.10 = (bf16[4,2,48,384]{3,2,1,0:T(8,128)(2,1)S(1)}, bf16[4,2,48,384]{3,2,1,0:T(8,128)(2,1)S(1)}, u32[]{:S(2)}, u32[]{:S(2)}) collective-permute-start(bf16[4,2,48,384]{3,2,1,0:T(8,128)(2,1)S(1)} %get-tuple-element.113.refs_1_), channel_id=1, source_target_pairs={{0,2},{2,0},{4,6},{6,4},{8,10},{10,8},{12,14},{14,12},{16,18},{18,... | collective-permute-start | bytes 884744 | tf_op jit(solution)/shard_map/ppermute | solution.py:554
  45.0 29.2 %copy-start.13 = (bf16[4,2,48,384]{3,2,1,0:T(8,128)(2,1)}, bf16[4,2,48,384]{3,2,1,0:T(8,128)(2,1)S(1)}, u32[]{:S(2)}) copy-start(bf16[4,2,48,384]{3,2,1,0:T(8,128)(2,1)S(1)} %collective-permute-done.4.refs_3_) | copy-start | bytes 884740
  45.0 14.6 %collective-permute-start.7 = (bf16[4,2,48,384]{3,2,1,0:T(8,128)(2,1)S(1)}, bf16[4,2,48,384]{3,2,1,0:T(8,128)(2,1)}, u32[]{:S(2)}, u32[]{:S(2)}) collective-permute-start(bf16[4,2,48,384]{3,2,1,0:T(8,128)(2,1)S(1)} %collective-permute-done.3.refs_2_), channel_id=1, source_target_pairs={{0,4},{2,6},{4,0},{6,2},{8,12},{10,14},{12,8},{14,10},{16,20},{18,... | collective-permute-start | bytes 884744 | tf_op jit(solution)/shard_map/ppermute | solution.py:554
  46.4 27.9 %copy-start.14 = (bf16[4,2,48,384]{3,2,1,0:T(8,128)(2,1)}, bf16[4,2,48,384]{3,2,1,0:T(8,128)(2,1)S(1)}, u32[]{:S(2)}) copy-start(bf16[4,2,48,384]{3,2,1,0:T(8,128)(2,1)S(1)} %collective-permute-done.5.refs_4_) | copy-start | bytes 884740
  46.4 23.3 %collective-permute-start.8 = (bf16[4,2,48,384]{3,2,1,0:T(8,128)(2,1)S(1)}, bf16[4,2,48,384]{3,2,1,0:T(8,128)(2,1)}, u32[]{:S(2)}, u32[]{:S(2)}) collective-permute-start(bf16[4,2,48,384]{3,2,1,0:T(8,128)(2,1)S(1)} %collective-permute-done.4.refs_3_), channel_id=1, source_target_pairs={{0,1},{1,0},{2,3},{3,2},{4,5},{5,4},{6,7},{7,6},{8,9},{9,8},{10,11... | collective-permute-start | bytes 884744 | tf_op jit(solution)/shard_map/ppermute | solution.py:550
  59.0 10.6 %collective-permute-start.11 = (bf16[4,2,48,384]{3,2,1,0:T(8,128)(2,1)S(1)}, bf16[4,2,48,384]{3,2,1,0:T(8,128)(2,1)S(1)}, u32[]{:S(2)}, u32[]{:S(2)}) collective-permute-start(bf16[4,2,48,384]{3,2,1,0:T(8,128)(2,1)S(1)} %collective-permute-done.3.refs_2_), channel_id=1, source_target_pairs={{0,2},{2,0},{4,6},{6,4},{8,10},{10,8},{12,14},{14,12},{16,18},{18,... | collective-permute-start | bytes 884744 | tf_op jit(solution)/shard_map/ppermute | solution.py:554
  59.0 13.0 %copy-start.15 = (bf16[4,2,48,384]{3,2,1,0:T(8,128)(2,1)}, bf16[4,2,48,384]{3,2,1,0:T(8,128)(2,1)S(1)}, u32[]{:S(2)}) copy-start(bf16[4,2,48,384]{3,2,1,0:T(8,128)(2,1)S(1)} %collective-permute-done.9.refs_8_) | copy-start | bytes 884740
  59.0 15.8 %collective-permute-start.12 = (bf16[4,2,48,384]{3,2,1,0:T(8,128)(2,1)S(1)}, bf16[4,2,48,384]{3,2,1,0:T(8,128)(2,1)}, u32[]{:S(2)}, u32[]{:S(2)}) collective-permute-start(bf16[4,2,48,384]{3,2,1,0:T(8,128)(2,1)S(1)} %collective-permute-done.4.refs_3_), channel_id=1, source_target_pairs={{0,2},{2,0},{4,6},{6,4},{8,10},{10,8},{12,14},{14,12},{16,18},{18,... | collective-permute-start | bytes 884744 | tf_op jit(solution)/shard_map/ppermute | solution.py:554
  59.5 10.1 %copy-start.16 = (bf16[4,2,48,384]{3,2,1,0:T(8,128)(2,1)}, bf16[4,2,48,384]{3,2,1,0:T(8,128)(2,1)S(1)}, u32[]{:S(2)}) copy-start(bf16[4,2,48,384]{3,2,1,0:T(8,128)(2,1)S(1)} %collective-permute-done.10.refs_9_) | copy-start | bytes 884740
  59.5 15.3 %collective-permute-start.13 = (bf16[4,2,48,384]{3,2,1,0:T(8,128)(2,1)S(1)}, bf16[4,2,48,384]{3,2,1,0:T(8,128)(2,1)}, u32[]{:S(2)}, u32[]{:S(2)}) collective-permute-start(bf16[4,2,48,384]{3,2,1,0:T(8,128)(2,1)S(1)} %collective-permute-done.5.refs_4_), channel_id=1, source_target_pairs={{0,2},{2,0},{4,6},{6,4},{8,10},{10,8},{12,14},{14,12},{16,18},{18,... | collective-permute-start | bytes 884744 | tf_op jit(solution)/shard_map/ppermute | solution.py:554
  59.6 15.2 %collective-permute-start.14 = (bf16[4,2,48,384]{3,2,1,0:T(8,128)(2,1)}, bf16[4,2,48,384]{3,2,1,0:T(8,128)(2,1)}, u32[]{:S(2)}, u32[]{:S(2)}) collective-permute-start(bf16[4,2,48,384]{3,2,1,0:T(8,128)(2,1)} %collective-permute-done.6.refs_5_), channel_id=1, source_target_pairs={{0,2},{2,0},{4,6},{6,4},{8,10},{10,8},{12,14},{14,12},{16,18},{18,... | collective-permute-start | bytes 884744 | tf_op jit(solution)/shard_map/ppermute | solution.py:554
  69.6 5.2 %collective-permute-start.15 = (bf16[4,2,48,384]{3,2,1,0:T(8,128)(2,1)}, bf16[4,2,48,384]{3,2,1,0:T(8,128)(2,1)}, u32[]{:S(2)}, u32[]{:S(2)}) collective-permute-start(bf16[4,2,48,384]{3,2,1,0:T(8,128)(2,1)} %collective-permute-done.7.refs_6_), channel_id=1, source_target_pairs={{0,2},{2,0},{4,6},{6,4},{8,10},{10,8},{12,14},{14,12},{16,18},{18,... | collective-permute-start | bytes 884744 | tf_op jit(solution)/shard_map/ppermute | solution.py:554
  70.4 4.5 %collective-permute-start.16 = (bf16[4,2,48,384]{3,2,1,0:T(8,128)(2,1)}, bf16[4,2,48,384]{3,2,1,0:T(8,128)(2,1)}, u32[]{:S(2)}, u32[]{:S(2)}) collective-permute-start(bf16[4,2,48,384]{3,2,1,0:T(8,128)(2,1)} %collective-permute-done.8.refs_7_), channel_id=1, source_target_pairs={{0,2},{2,0},{4,6},{6,4},{8,10},{10,8},{12,14},{14,12},{16,18},{18,... | collective-permute-start | bytes 884744 | tf_op jit(solution)/shard_map/ppermute | solution.py:554
  136.4 95.2 %reduce-scatter.5.cloned.1.call-start = ((), (), s32[]{:S(2)}) async-start(), calls=%async_computation.3 | async-start | bytes 6635520 | tf_op jit(solution)/shard_map/reduce_scatter | solution.py:671
  190.8 9.6 %copy-start.9 = (f32[4,1,768]{2,1,0:T(1,128)S(1)}, f32[4,1,768]{2,1,0:T(1,128)}, u32[]{:S(2)}) copy-start(f32[4,1,768]{2,1,0:T(1,128)} %get-tuple-element.89) | copy-start | bytes 36868
  192.2 19.1 %collective-permute-start.25 = (bf16[8,48,384]{2,1,0:T(8,128)(2,1)S(1)}, bf16[8,48,384]{2,1,0:T(8,128)(2,1)S(1)}, u32[]{:S(2)}, u32[]{:S(2)}) collective-permute-start(bf16[8,48,384]{2,1,0:T(8,128)(2,1)S(1)} %get-tuple-element.108), channel_id=1, source_target_pairs={{0,24},{2,26},{4,28},{6,30},{8,0},{10,2},{12,4},{14,6},{16,8},{18,... | collective-permute-start | bytes 884744 | tf_op jit(solution)/shard_map/ppermute | solution.py:559
  195.6 25.2 %collective-permute-start.24 = (bf16[8,48,384]{2,1,0:T(8,128)(2,1)S(1)}, bf16[8,48,384]{2,1,0:T(8,128)(2,1)S(1)}, u32[]{:S(2)}, u32[]{:S(2)}) collective-permute-start(bf16[8,48,384]{2,1,0:T(8,128)(2,1)S(1)} %get-tuple-element.109), channel_id=1, source_target_pairs={{0,16},{2,18},{4,20},{6,22},{8,24},{10,26},{12,28},{14,30},{16,0},... | collective-permute-start | bytes 884744 | tf_op jit(solution)/shard_map/ppermute | solution.py:559
  195.6 25.2 %collective-permute-start.23 = (bf16[8,48,384]{2,1,0:T(8,128)(2,1)S(1)}, bf16[8,48,384]{2,1,0:T(8,128)(2,1)S(1)}, u32[]{:S(2)}, u32[]{:S(2)}) collective-permute-start(bf16[8,48,384]{2,1,0:T(8,128)(2,1)S(1)} %get-tuple-element.107), channel_id=1, source_target_pairs={{0,8},{2,10},{4,12},{6,14},{8,16},{10,18},{12,20},{14,22},{16,24},... | collective-permute-start | bytes 884744 | tf_op jit(solution)/shard_map/ppermute | solution.py:559
  200.5 1.3 collective-permute-start.20
  201.8 4.7 %collective-permute-start.21 = (f32[12,768]{1,0:T(8,128)S(1)}, f32[12,768]{1,0:T(8,128)S(1)}, u32[]{:S(2)}, u32[]{:S(2)}) collective-permute-start(f32[12,768]{1,0:T(8,128)S(1)} %add.152), channel_id=1, source_target_pairs={{0,1},{1,0},{2,3},{3,2},{4,5},{5,4},{6,7},{7,6},{8,9},{9,8},{10,11... | collective-permute-start | bytes 110600 | tf_op jit(solution)/shard_map/ppermute | solution.py:550
  206.5 4.8 %collective-permute-start.22 = (f32[12,768]{1,0:T(8,128)S(1)}, f32[12,768]{1,0:T(8,128)S(1)}, u32[]{:S(2)}, u32[]{:S(2)}) collective-permute-start(f32[12,768]{1,0:T(8,128)S(1)} %add.153), channel_id=1, source_target_pairs={{0,4},{2,6},{4,0},{6,2},{8,12},{10,14},{12,8},{14,10},{16,20},{18,... | collective-permute-start | bytes 110600 | tf_op jit(solution)/shard_map/ppermute | solution.py:554
  221.7 8.7 %collective-permute-start.28 = (f32[12,768]{1,0:T(8,128)S(1)}, f32[12,768]{1,0:T(8,128)S(1)}, u32[]{:S(2)}, u32[]{:S(2)}) collective-permute-start(f32[12,768]{1,0:T(8,128)S(1)} %add.154), channel_id=1, source_target_pairs={{0,24},{2,26},{4,28},{6,30},{8,0},{10,2},{12,4},{14,6},{16,8},{18,... | collective-permute-start | bytes 110600 | tf_op jit(solution)/shard_map/ppermute | solution.py:559
  221.7 8.7 %collective-permute-start.27 = (f32[12,768]{1,0:T(8,128)S(1)}, f32[12,768]{1,0:T(8,128)S(1)}, u32[]{:S(2)}, u32[]{:S(2)}) collective-permute-start(f32[12,768]{1,0:T(8,128)S(1)} %add.154), channel_id=1, source_target_pairs={{0,16},{2,18},{4,20},{6,22},{8,24},{10,26},{12,28},{14,30},{16,0},... | collective-permute-start | bytes 110600 | tf_op jit(solution)/shard_map/ppermute | solution.py:559
  224.4 6.0 %collective-permute-start.26 = (f32[12,768]{1,0:T(8,128)S(1)}, f32[12,768]{1,0:T(8,128)S(1)}, u32[]{:S(2)}, u32[]{:S(2)}) collective-permute-start(f32[12,768]{1,0:T(8,128)S(1)} %add.154), channel_id=1, source_target_pairs={{0,8},{2,10},{4,12},{6,14},{8,16},{10,18},{12,20},{14,22},{16,24},... | collective-permute-start | bytes 110600 | tf_op jit(solution)/shard_map/ppermute | solution.py:559
  226.4 4.0 %copy-start.6 = (f32[6,768]{1,0:T(8,128)S(1)}, f32[6,768]{1,0:T(8,128)}, u32[]{:S(2)}) copy-start(f32[6,768]{1,0:T(8,128)} %nv_ref.3) | copy-start | bytes 55300
  226.4 4.0 %copy-start.7 = (f32[6,768]{1,0:T(8,128)S(1)}, f32[6,768]{1,0:T(8,128)}, u32[]{:S(2)}) copy-start(f32[6,768]{1,0:T(8,128)} %param.21) | copy-start | bytes 55300
  226.4 4.0 %copy-start.8 = (f32[6,768]{1,0:T(8,128)S(1)}, f32[6,768]{1,0:T(8,128)}, u32[]{:S(2)}) copy-start(f32[6,768]{1,0:T(8,128)} %param.22) | copy-start | bytes 55300
  230.4 6.8 %copy-start.10 = (f32[6,384]{1,0:T(8,128)S(1)}, f32[6,384]{1,0:T(8,128)}, u32[]{:S(2)}) copy-start(f32[6,384]{1,0:T(8,128)} %param.18) | copy-start | bytes 27652
  230.4 6.8 %copy-start.11 = (f32[6,384]{1,0:T(8,128)S(1)}, f32[6,384]{1,0:T(8,128)}, u32[]{:S(2)}) copy-start(f32[6,384]{1,0:T(8,128)} %param.19) | copy-start | bytes 27652
  232.7 8.4 %collective-permute-start.19 = (bf16[5,48,384]{2,1,0:T(8,128)(2,1)S(1)}, bf16[5,48,384]{2,1,0:T(8,128)(2,1)S(1)}, u32[]{:S(2)}, u32[]{:S(2)}) collective-permute-start(bf16[5,48,384]{2,1,0:T(8,128)(2,1)S(1)} %get-tuple-element.111), channel_id=1, source_target_pairs={{0,24},{2,26},{4,28},{6,30},{8,0},{10,2},{12,4},{14,6},{16,8},{18,... | collective-permute-start | bytes 552968 | tf_op jit(solution)/shard_map/ppermute | solution.py:559
  236.1 15.6 %collective-permute-start.18 = (bf16[5,48,384]{2,1,0:T(8,128)(2,1)S(1)}, bf16[5,48,384]{2,1,0:T(8,128)(2,1)S(1)}, u32[]{:S(2)}, u32[]{:S(2)}) collective-permute-start(bf16[5,48,384]{2,1,0:T(8,128)(2,1)S(1)} %get-tuple-element.112), channel_id=1, source_target_pairs={{0,16},{2,18},{4,20},{6,22},{8,24},{10,26},{12,28},{14,30},{16,0},... | collective-permute-start | bytes 552968 | tf_op jit(solution)/shard_map/ppermute | solution.py:559
  236.1 15.6 %collective-permute-start.17 = (bf16[5,48,384]{2,1,0:T(8,128)(2,1)S(1)}, bf16[5,48,384]{2,1,0:T(8,128)(2,1)S(1)}, u32[]{:S(2)}, u32[]{:S(2)}) collective-permute-start(bf16[5,48,384]{2,1,0:T(8,128)(2,1)S(1)} %get-tuple-element.110), channel_id=1, source_target_pairs={{0,8},{2,10},{4,12},{6,14},{8,16},{10,18},{12,20},{14,22},{16,24},... | collective-permute-start | bytes 552968 | tf_op jit(solution)/shard_map/ppermute | solution.py:559
  253.5 2.7 %copy-start.1 = (bf16[1024,768]{1,0:T(8,128)(2,1)S(1)}, bf16[1024,768]{1,0:T(8,128)(2,1)}, u32[]{:S(2)}) copy-start(bf16[1024,768]{1,0:T(8,128)(2,1)} %param.12) | copy-start | bytes 4718596
  (3 other events, 4.3 us)
Sparse Core Ops, SparseCore 0:
  29.5 77.6 all-gather.2
  136.5 54.2 reduce-scatter.2
  193.1 38.4 reduce-scatter.4
